TPU v7x, 512 devices: a whole 4x8x8 slice. The times are simulated.
512 devices in a mesh: dp: 32 (over x, y), tensor: 8 (over z), section: 2 (over core).
Axes of the slice: x: 4, y: 8, z: 8, core: 2. Of those that a mesh axis runs over, the one named last changes fastest.
Arguments:
- hidden_in: bfloat16 [192, 8192], P(None, 'dp'), may hold values from -12 to 12
- norm_gain: float32 [2, 8192], P('section', 'dp'), may hold values from 0.25 to 1.75
- w_query: bfloat16 [2, 8192, 8192], P('section', 'dp', 'tensor'), may hold values from -0.0625 to 0.0625
- w_key: bfloat16 [2, 8192, 1024], P('section', 'dp', 'tensor'), may hold values from -0.0625 to 0.0625
- w_value: bfloat16 [2, 8192, 1024], P('section', 'dp', 'tensor'), may hold values from -0.0625 to 0.0625
- w_out: bfloat16 [2, 8192, 8192], P('section', 'tensor', 'dp'), may hold values from -0.0625 to 0.0625
- key_cache: bfloat16 [2, 192, 64, 1024], P('section', 'dp', None, 'tensor'), may hold values from -320 to 320
- value_cache: bfloat16 [2, 192, 64, 1024], P('section', 'dp', None, 'tensor'), may hold values from -6 to 6
- context_len: int32 [192], replicated, may hold values from 1 to 63, as said below
- dest_replica: int32 [192], replicated, may hold values from 0 to 31, as said below
- dest_slot: int32 [192], replicated, may hold values from 0 to 5
Outputs:
- layer_out: bfloat16 [2, 192, 8192], P('section', None, 'dp')
- key_out: bfloat16 [2, 192, 64, 1024], P('section', 'dp', None, 'tensor')
- value_out: bfloat16 [2, 192, 64, 1024], P('section', 'dp', None, 'tensor')
Inputs may be any that keep to these rules, and one draw needn't show every extreme that they name: `context_len`: the longest row has exactly 63 live positions. dest_replica[g] * 6 + dest_slot[g] is a permutation of 0..191; every replica hands exactly 4 of its rows to other replicas, never two to the same one, and receives 4.
All inputs are finite; a program needn't handle non-finite values.
Results may differ from a plain program's by a relative error of at most 0.015.
Values may be sent and summed in bfloat16 or wider, within the bound.
No kernel may reach another device: no remote copies, remote signals or barrier semaphores. Data moves between devices by JAX's collectives and lax.ppermute only.
A program may use at most 64 MiB of HBM per device.

v0:
```python
import jax
import jax.numpy as jnp
from jax import lax
from jax.sharding import PartitionSpec as P

HEAD = 128


epsilon = 1e-06
rope_base = 1000000.0


def passed_along(value, axis, by):
    devices = lax.axis_size(axis)
    pairs = [(i, i + by) for i in range(devices) if 0 <= i + by < devices]
    return lax.ppermute(value, axis, pairs)


def rotate(vectors, positions):
    half_width = vectors.shape[-1] // 2
    exponent = jnp.arange(half_width, dtype=jnp.float32) * (2.0 / vectors.shape[-1])
    inverse_freq = rope_base ** (-exponent)
    angles = positions.astype(jnp.float32)[:, None] * inverse_freq[None, :]
    cosine = jnp.cos(angles)[:, None, :]
    sine = jnp.sin(angles)[:, None, :]
    first_half = vectors[..., :half_width]
    second_half = vectors[..., half_width:]
    return jnp.concatenate(
        [first_half * cosine - second_half * sine, second_half * cosine + first_half * sine], -1
    )


def attend(queries, cached_keys, cached_values, own_key, own_value, lengths):
    score_scale = queries.shape[-1] ** (-0.5)
    scores = (
        jnp.einsum("nkgd,nckd->nkgc", queries, cached_keys, preferred_element_type=jnp.float32)
        * score_scale
    )
    own_score = (
        jnp.einsum("nkgd,nkd->nkg", queries, own_key, preferred_element_type=jnp.float32)
        * score_scale
    )
    live_mask = (jnp.arange(cached_keys.shape[1], dtype=jnp.int32)[None, :] < lengths[:, None])[
        :, None, None, :
    ]
    scores = jnp.where(live_mask, scores, -1e30)
    highest = jnp.maximum(jnp.max(scores, -1), own_score)
    cache_terms = jnp.exp(scores - highest[..., None])
    own_term = jnp.exp(own_score - highest)
    denominator = jnp.sum(cache_terms, -1) + own_term
    cache_weights = (cache_terms / denominator[..., None]).astype(jnp.bfloat16)
    own_weight = (own_term / denominator).astype(jnp.bfloat16)
    attended = jnp.einsum(
        "nkgc,nckd->nkgd", cache_weights, cached_values, preferred_element_type=jnp.float32
    )
    attended = (
        attended
        + own_weight.astype(jnp.float32)[..., None] * own_value.astype(jnp.float32)[:, :, None, :]
    )
    return attended.astype(jnp.bfloat16)


def on_device(
    hidden_in,
    norm_gain,
    w_query,
    w_key,
    w_value,
    w_out,
    key_cache,
    value_cache,
    context_len,
    dest_replica,
    dest_slot,
):
    replicas = lax.axis_size("dp")
    replica_id = lax.axis_index("dp")
    section_id = lax.axis_index("section")
    rows_local = key_cache.shape[1]
    context = key_cache.shape[2]
    kv_width = key_cache.shape[3]
    head_width = HEAD
    kv_local = kv_width // head_width
    heads_local = w_query.shape[2] // head_width
    group_size = heads_local // kv_local
    query_width = heads_local * head_width
    model_width = hidden_in.shape[1] * replicas
    gain_row = norm_gain[0]
    query_weight = w_query[0]
    key_weight = w_key[0]
    value_weight = w_value[0]
    out_weight = w_out[0]
    keys_held = key_cache[0]
    values_held = value_cache[0]
    all_rows = dest_replica.shape[0]
    new_index = dest_replica * rows_local + dest_slot
    source_of = (
        jnp.zeros((all_rows,), jnp.int32).at[new_index].set(jnp.arange(all_rows, dtype=jnp.int32))
    )
    arrivals = lax.dynamic_slice_in_dim(source_of, replica_id * rows_local, rows_local)
    lengths = jnp.take(context_len, arrivals)
    anchor = arrivals // rows_local
    staying = anchor == replica_id
    held_index = jnp.where(staying, arrivals - replica_id * rows_local, 0)
    leaving_to = lax.dynamic_slice_in_dim(dest_replica, replica_id * rows_local, rows_local)
    peer_ids = jnp.arange(replicas, dtype=jnp.int32)
    outgoing = (leaving_to[:, None] == peer_ids[None, :]) & (peer_ids[None, :] != replica_id)
    out_onehot = outgoing.astype(jnp.bfloat16)
    send_keys = jnp.einsum(
        "rp,rcw->pcw", out_onehot, keys_held, preferred_element_type=jnp.float32
    ).astype(jnp.bfloat16)
    send_values = jnp.einsum(
        "rp,rcw->pcw", out_onehot, values_held, preferred_element_type=jnp.float32
    ).astype(jnp.bfloat16)
    moved_keys, moved_values = (
        lax.all_to_all(send_keys, "dp", split_axis=0, concat_axis=0, tiled=True),
        lax.all_to_all(send_values, "dp", split_axis=0, concat_axis=0, tiled=True),
    )
    keys_placed = jnp.where(
        staying[:, None, None], jnp.take(keys_held, held_index, 0), jnp.take(moved_keys, anchor, 0)
    )
    values_placed = jnp.where(
        staying[:, None, None],
        jnp.take(values_held, held_index, 0),
        jnp.take(moved_values, anchor, 0),
    )

    def attend_rows(queries, own_key, own_value):
        return attend(
            queries,
            keys_placed.reshape(rows_local, context, kv_local, head_width),
            values_placed.reshape(rows_local, context, kv_local, head_width),
            own_key,
            own_value,
            lengths,
        )

    def one_pass(hidden):
        widened = hidden.astype(jnp.float32)
        square_sum = lax.psum(jnp.sum(widened * widened, 1), "dp")
        normed = (
            widened * lax.rsqrt(square_sum / model_width + epsilon)[:, None] * gain_row[None, :]
        ).astype(jnp.bfloat16)
        combined = lax.psum_scatter(
            jnp.concatenate(
                [
                    jnp.dot(normed, query_weight, preferred_element_type=jnp.float32),
                    jnp.dot(normed, key_weight, preferred_element_type=jnp.float32),
                    jnp.dot(normed, value_weight, preferred_element_type=jnp.float32),
                ],
                1,
            ),
            "dp",
            scatter_dimension=0,
            tiled=True,
        )
        queries = rotate(
            combined[:, :query_width].reshape(rows_local, heads_local, head_width), lengths
        ).astype(jnp.bfloat16)
        queries = queries.reshape(rows_local, kv_local, group_size, head_width)
        own_key = rotate(
            combined[:, query_width : query_width + kv_width].reshape(
                rows_local, kv_local, head_width
            ),
            lengths,
        ).astype(jnp.bfloat16)
        own_value = (
            combined[:, query_width + kv_width :]
            .reshape(rows_local, kv_local, head_width)
            .astype(jnp.bfloat16)
        )
        attended = attend_rows(queries, own_key, own_value)
        flattened = attended.reshape(rows_local, query_width)
        partial_out = jnp.dot(
            lax.all_gather(flattened, "dp", axis=0, tiled=True),
            out_weight,
            preferred_element_type=jnp.float32,
        )
        result = (
            widened + lax.psum(partial_out.astype(jnp.bfloat16), "tensor").astype(jnp.float32)
        ).astype(jnp.bfloat16)
        written = (jnp.arange(context, dtype=jnp.int32)[None, :] == lengths[:, None])[:, :, None]
        keys_out = jnp.where(written, own_key, keys_placed)
        values_out = jnp.where(written, own_value, values_placed)
        return (result, keys_out, values_out)

    first_out, first_keys, first_values = one_pass(hidden_in)
    received = passed_along(first_out, "section", 1)
    second_out, second_keys, second_values = one_pass(received)
    at_first = section_id == 0
    layer_out = jnp.where(at_first, first_out, second_out)[None]
    key_out = jnp.where(at_first, first_keys, second_keys)[None]
    value_out = jnp.where(at_first, first_values, second_values)[None]
    return (layer_out, key_out, value_out)


def solution(mesh):
    return jax.shard_map(
        on_device,
        mesh=mesh,
        in_specs=(
            P(None, "dp"),
            P("section", "dp"),
            P("section", "dp", "tensor"),
            P("section", "dp", "tensor"),
            P("section", "dp", "tensor"),
            P("section", "tensor", "dp"),
            P("section", "dp", None, "tensor"),
            P("section", "dp", None, "tensor"),
            P(),
            P(),
            P(),
        ),
        out_specs=(
            P("section", None, "dp"),
            P("section", "dp", None, "tensor"),
            P("section", "dp", None, "tensor"),
        ),
        check_vma=False,
    )
```

profile of v0, /device:TPU:1, one launch (start us, length us, event | category | flops | bytes accessed | tf_op | source)
XLA Modules:
  0.0 755.4 jit_solution(9487655578420716211)
XLA Ops:
  7.2 0.7 copy-done.9
  8.0 1.3 convolution_convert_fusion
  9.3 1.0 copy.30
  10.4 10.6 %all-to-all-start.1 = ((bf16[32,64,128]{2,1,0:T(8,128)(2,1)}), bf16[32,64,128]{2,1,0:T(8,128)(2,1)S(1)}, u32[]{:S(2)}, u32[]{:S(2)}) async-start(bf16[32,64,128]{2,1,0:T(8,128)(2,1)} %copy.30), calls=%async_computation.1 | async-start | bytes 1048576 | tf_op jit(solution)/shard_map/all_to_all | solution.py:117
  21.2 65.0 %psum.28 = f32[192]{0:T(256)S(1)} all-reduce(f32[192]{0:T(256)S(1)} %fusion.10), channel_id=1, replica_groups=mesh['dp'=32,'tensor'=8,'section'=2] {'dp'}, use_global_device_ids=true, to_apply=%region_2.3 | all-reduce | flops 192 | bytes 1536 | tf_op jit(solution)/shard_map/psum | solution.py:140
  88.3 1.1 pad_maximum_fusion
  90.0 1.2 scatter_custom_fusion
  93.5 1.0 copy.28
  94.5 1.3 dynamic-slice
  97.4 3.9 all-to-all-start
  101.4 156.3 %all-reduce.11.cloned.1.call-done = f32[192,1280]{1,0:T(8,128)} async-done(((f32[192,1280]{1,0:T(8,128)}), f32[192,1280]{1,0:T(8,128)}) %all-reduce.11.cloned.1.call-update) | async-done | bytes 983056
  257.7 0.8 dynamic-slice_bitcast_fusion.1
  258.5 0.8 dynamic-slice_bitcast_fusion.3
  259.5 0.8 fusion.91
  262.6 35.9 %all-gather = bf16[32,6,1024]{2,1,0:T(8,128)(2,1)S(1)} all-gather(bf16[1,6,1024]{2,1,0:T(8,128)(2,1)S(1)} %reshape.439), channel_id=1, replica_groups=mesh['dp'=32,'tensor'=8,'section'=2] {'dp'}, dimensions={0}, use_global_device_ids=true | all-gather | bytes 405504 | tf_op jit(solution)/shard_map/all_gather | solution.py:175
  298.6 0.9 copy-done.3
  299.5 0.9 convolution_convert_fusion.3
  300.5 87.7 %all-reduce.7.cloned.1.call-done = bf16[192,256]{1,0:T(8,128)(2,1)} async-done(((bf16[192,256]{1,0:T(8,128)(2,1)}), bf16[192,256]{1,0:T(8,128)(2,1)}) %all-reduce.7.cloned.1.call-update) | async-done | bytes 98320 | tf_op jit(solution)/shard_map/psum | solution.py:180
  388.2 0.9 fusion.13
  389.1 1.3 collective-permute-start
  390.4 6.2 collective-permute-done
  396.7 60.6 %psum.30 = f32[192]{0:T(256)S(1)} all-reduce(f32[192]{0:T(256)S(1)} %fusion.14), channel_id=1, replica_groups=mesh['dp'=32,'tensor'=8,'section'=2] {'dp'}, use_global_device_ids=true, to_apply=%region_8.11 | all-reduce | flops 192 | bytes 1536 | tf_op jit(solution)/shard_map/psum | solution.py:140
  458.2 1.1 pad_maximum_fusion.1
  459.4 159.6 %all-reduce.13.cloned.1.call-done = f32[192,1280]{1,0:T(8,128)} async-done(((f32[192,1280]{1,0:T(8,128)}), f32[192,1280]{1,0:T(8,128)}) %all-reduce.13.cloned.1.call-update) | async-done | bytes 983056
  619.0 0.8 dynamic-slice_bitcast_fusion.2
  619.9 0.9 dynamic-slice_bitcast_fusion
  621.1 0.8 fusion.90
  622.6 35.9 %all-gather.1 = bf16[32,6,1024]{2,1,0:T(8,128)(2,1)S(1)} all-gather(bf16[1,6,1024]{2,1,0:T(8,128)(2,1)S(1)} %reshape.441), channel_id=1, replica_groups=mesh['dp'=32,'tensor'=8,'section'=2] {'dp'}, dimensions={0}, use_global_device_ids=true | all-gather | bytes 405504 | tf_op jit(solution)/shard_map/all_gather | solution.py:175
  658.6 0.9 convolution_convert_fusion.2
  659.6 0.8 select_bitcast_fusion
  660.4 86.9 %all-reduce.9.cloned.1.call-done = bf16[192,256]{1,0:T(8,128)(2,1)} async-done(((bf16[192,256]{1,0:T(8,128)(2,1)}), bf16[192,256]{1,0:T(8,128)(2,1)}) %all-reduce.9.cloned.1.call-update) | async-done | bytes 98320 | tf_op jit(solution)/shard_map/psum | solution.py:180
  747.3 1.6 fusion.21
  (86 shorter events, 11.1 us)
Async XLA Ops:
  7.2 80.8 %copy-start = (bf16[1,256,1024]{2,1,0:T(8,128)(2,1)S(1)}, bf16[1,256,1024]{2,1,0:T(8,128)(2,1)}, u32[]{:S(2)}) copy-start(bf16[1,256,1024]{2,1,0:T(8,128)(2,1)} %param.17) | copy-start | bytes 1572868
  7.2 0.7 copy-start.9
  10.4 10.7 %copy-start.2 = (bf16[192,256]{1,0:T(8,128)(2,1)S(1)}, bf16[192,256]{1,0:T(8,128)(2,1)}, u32[]{:S(2)}) copy-start(bf16[192,256]{1,0:T(8,128)(2,1)} %param.15) | copy-start | bytes 294916
  10.4 87.0 %all-to-all-start.1 = ((bf16[32,64,128]{2,1,0:T(8,128)(2,1)}), bf16[32,64,128]{2,1,0:T(8,128)(2,1)S(1)}, u32[]{:S(2)}, u32[]{:S(2)}) async-start(bf16[32,64,128]{2,1,0:T(8,128)(2,1)} %copy.30), calls=%async_computation.1 | async-start | bytes 1048576 | tf_op jit(solution)/shard_map/all_to_all | solution.py:117
  21.0 65.2 %copy-start.6 = (bf16[1,256,128]{2,1,0:T(8,128)(2,1)S(1)}, bf16[1,256,128]{2,1,0:T(8,128)(2,1)}, u32[]{:S(2)}) copy-start(bf16[1,256,128]{2,1,0:T(8,128)(2,1)} %param.18) | copy-start | bytes 196612
  21.0 236.7 %all-reduce.11.cloned.1.call-start = ((), (), s32[]{:S(2)}) async-start(), calls=%async_computation.4 | async-start | bytes 1966080
  86.2 0.7 copy-start.8
  86.9 0.8 copy-start.7
  89.4 0.7 copy-start.10
  89.4 2.1 copy-start.5
  91.5 0.9 copy-start.4
  93.5 2.9 copy-start.1
  97.4 163.8 %all-to-all-start = ((bf16[32,64,128]{2,1,0:T(8,128)(2,1)}), bf16[32,64,128]{2,1,0:T(8,128)(2,1)S(1)}, u32[]{:S(2)}, u32[]{:S(2)}) async-start(bf16[32,64,128]{2,1,0:T(8,128)(2,1)} %copy.28), calls=%async_computation | async-start | bytes 1048576 | tf_op jit(solution)/shard_map/all_to_all | solution.py:116
  101.3 286.9 %all-reduce.7.cloned.1.call-start = ((), (), s32[]{:S(2)}) async-start(), calls=%async_computation.2 | async-start | bytes 196608 | tf_op jit(solution)/shard_map/psum | solution.py:180
  298.5 1.0 copy-start.3
  300.5 318.5 %all-reduce.13.cloned.1.call-start = ((), (), s32[]{:S(2)}) async-start(), calls=%async_computation.5 | async-start | bytes 1966080
  389.1 7.5 collective-permute-start
  459.3 288.0 %all-reduce.9.cloned.1.call-start = ((), (), s32[]{:S(2)}) async-start(), calls=%async_computation.3 | async-start | bytes 196608 | tf_op jit(solution)/shard_map/psum | solution.py:180
Sparse Core Ops, SparseCore 0:
  89.5 168.1 all-reduce.10
  300.6 87.5 all-reduce.6
  459.4 159.5 all-reduce.12
  659.7 87.5 all-reduce.8
where the time goes:
time: 760 us; the launch traced here: 755 us
  waiting for transfers between devices  497 us (65%)
  blocking collectives  197 us (26%)
  starting transfers between devices  16 us (2%)
  local copies, waits for them, and re-layouts  15.2 us (2%)
  between operations  14.8 us (2%)
  other arithmetic  8.82 us (1%)
    unnamed x6, waiting for transfers between devices  316 us
    psum x2, waiting for transfers between devices, one_pass(): lax.psum(partial_out.astype(jnp.bfloat16), 'tensor').astype(jnp.float32)  175 us
    psum x2, blocking collectives, one_pass(): square_sum = lax.psum(jnp.sum(widened * widened, 1), 'dp')  126 us
    all_gather x2, blocking collectives, one_pass(): lax.all_gather(flattened, 'dp', axis=0, tiled=True)  71.8 us
  transfers between devices with their start and end apart: 7, of which 5 were waited for; matrix products, arithmetic and copies ran while one was open for 2% of the time, Pallas kernels for 0%

commit v1 on v0

v1 whole, which is shorter than its diff:
```python
import jax
import jax.numpy as jnp
from jax import lax
from jax.experimental import pallas as pl
from jax.experimental.pallas import tpu as pltpu
from jax.sharding import PartitionSpec as P

N_DP = 32
ROWS_DEV = 6
ROWS = 192
SLOTS = 8
PADDED = N_DP * SLOTS
CONTEXT = 64
HEAD = 128
GROUP = 8
PARTS = GROUP + 2
BLOCK = 64
WIDTH = 256
MODEL = 8192
N_TS = 16
TS_ROWS = PADDED // N_TS
EPSILON = 1e-06
ROPE_BASE = 1000000.0
F32 = jnp.float32
BF16 = jnp.bfloat16

SECTION, REPLICA, TS_BLOCK, DEST, HELD_LEN, SOURCE, NEW_LEN = 0, 1, 2, 4, 10, 16, 22

SMEM_SPEC = pl.BlockSpec(memory_space=pltpu.SMEM)
VMEM_SPEC = pl.BlockSpec(memory_space=pltpu.VMEM)


def iota(shape, dim):
    return lax.broadcasted_iota(jnp.int32, shape, dim)


def pick(condition):
    return jnp.where(condition, 1.0, 0.0).astype(BF16)


def over_six(index):
    return (index * 171) >> 10


def dot(left, right, contract=((1,), (0,))):
    return lax.dot_general(left, right, (contract, ((), ())), preferred_element_type=F32)


def old_order(new_index, hidden):
    to_new = pick(iota((ROWS, ROWS), 0) == new_index)
    return dot(to_new, hidden, ((0,), (0,))).astype(BF16)


def project_kernel(layer, scalars, *refs):
    if layer == 0:
        replica, slot, hidden, gain, w_query, w_key, w_value, keys, payload, spread = refs
    else:
        hidden, gain, w_query, w_key, w_value, keys, payload, spread = refs

    @pl.when(scalars[SECTION] == layer)
    def _():
        if layer == 0:
            new_index = replica[...] * ROWS_DEV + slot[...]
            rows = old_order(new_index, hidden[...])
            row, column = iota((ROWS, ROWS), 0), iota((ROWS, ROWS), 1)
            order = pick(column == (row & (N_DP - 1)) * ROWS_DEV + (row >> 5))
        else:
            rows = hidden[...].reshape(PADDED, WIDTH)
            row, column = iota((ROWS, PADDED), 0), iota((ROWS, PADDED), 1)
            order = pick(column == (row & (N_DP - 1)) * SLOTS + (row >> 5))
        by_slot = dot(order, rows)
        square = jnp.sum(by_slot * by_slot, axis=1, keepdims=True)
        scaled = (by_slot * gain[...]).astype(BF16)

        def place(part, product):
            for s in range(ROWS_DEV):
                spread[pl.ds((s * PARTS + part) * N_DP, N_DP), :] = product[s * N_DP : (s + 1) * N_DP]

        for part in range(0, GROUP, 2):
            product = dot(scaled, w_query[:, part * HEAD : (part + 2) * HEAD])
            place(part, product[:, :HEAD])
            place(part + 1, product[:, HEAD:])
        place(GROUP, dot(scaled, w_key[...]))
        place(GROUP + 1, dot(scaled, w_value[...]))
        lane = iota((N_DP, HEAD), 1)
        squares = jnp.zeros((N_DP, HEAD), F32)
        for s in range(ROWS_DEV):
            squares = jnp.where(lane == s, square[s * N_DP : (s + 1) * N_DP], squares)
        high = squares.astype(BF16).astype(F32)
        tail = ROWS_DEV * PARTS
        spread[pl.ds(tail * N_DP, N_DP), :] = high
        spread[pl.ds((tail + 1) * N_DP, N_DP), :] = squares - high
        spread[pl.ds((tail + 2) * N_DP, 2 * N_DP), :] = jnp.zeros((2 * N_DP, HEAD), F32)
        for p in range(N_DP):
            payload[p] = spread[pl.ds(p, BLOCK, stride=N_DP), :].astype(BF16)

    @pl.when(scalars[SECTION] != layer)
    def _():
        for s in range(ROWS_DEV):
            payload[scalars[DEST + s]] = keys[s]


def attend_kernel(layer, scalars, cosine, sine, received, keys, values, payload, own):
    @pl.when(scalars[SECTION] == layer)
    def _():
        total = received[0].astype(F32)
        for p in range(1, N_DP):
            total = total + received[p].astype(F32)
        row = iota((BLOCK, HEAD), 0)
        lane = iota((BLOCK, HEAD), 1)
        slot = (row * 205) >> 11
        part = row - slot * PARTS
        tail = ROWS_DEV * PARTS
        squares = total[tail : tail + 1] + total[tail + 1 : tail + 2]
        square = jnp.sum(jnp.where(lane == slot, squares, 0.0), axis=1, keepdims=True)
        projected = total * lax.rsqrt(square / MODEL + EPSILON)
        cos_rows = jnp.ones((BLOCK, HEAD), F32)
        sin_rows = jnp.zeros((BLOCK, HEAD), F32)
        for s in range(ROWS_DEV):
            turned = (slot == s) & (part <= GROUP)
            cos_rows = jnp.where(turned, cosine[s : s + 1, :], cos_rows)
            sin_rows = jnp.where(turned, sine[s : s + 1, :], sin_rows)
        vectors = (
            projected * cos_rows + pltpu.roll(projected, HEAD // 2, 1) * sin_rows
        ).astype(BF16)

        all_keys = keys[...].reshape(ROWS_DEV * CONTEXT, HEAD)
        all_values = values[...].reshape(ROWS_DEV * CONTEXT, HEAD)
        scale = HEAD ** (-0.5)
        scores = dot(vectors, all_keys, ((1,), (1,))) * scale
        among = dot(vectors, vectors, ((1,), (1,))) * scale
        wide = (BLOCK, ROWS_DEV * CONTEXT)
        wide_slot = (iota(wide, 0) * 205) >> 11
        column = iota(wide, 1)
        live = column < 0
        for s in range(ROWS_DEV):
            live = live | (
                (wide_slot == s)
                & (column >= s * CONTEXT)
                & (column < s * CONTEXT + scalars[HELD_LEN + s])
            )
        scores = jnp.where(live, scores, -1e30)
        narrow_slot = slot[:, :BLOCK]
        narrow_column = lane[:, :BLOCK]
        own_score = jnp.sum(
            jnp.where(narrow_column == narrow_slot * PARTS + GROUP, among, 0.0), axis=1, keepdims=True
        )
        highest = jnp.maximum(jnp.max(scores, axis=1, keepdims=True), own_score)
        terms = jnp.exp(scores - highest)
        own_term = jnp.exp(own_score - highest)
        denominator = jnp.sum(terms, axis=1, keepdims=True) + own_term
        weights = (terms / denominator).astype(BF16)
        own_weight = own_term / denominator
        own_weights = jnp.where(
            narrow_column == narrow_slot * PARTS + GROUP + 1, own_weight, 0.0
        ).astype(BF16)
        attended = (dot(weights, all_values) + dot(own_weights, vectors)).astype(BF16)

        out_row, in_row = iota((BLOCK, BLOCK), 0), iota((BLOCK, BLOCK), 1)
        out_slot = out_row & (SLOTS - 1)
        order = pick((in_row == out_slot * PARTS + (out_row >> 3)) & (out_slot < ROWS_DEV))
        block = dot(order, attended)
        own_row, own_in = iota((16, BLOCK), 0), iota((16, BLOCK), 1)
        own_slot = own_row & (SLOTS - 1)
        own_pick = pick(
            (own_in == own_slot * PARTS + GROUP + (own_row >> 3)) & (own_slot < ROWS_DEV)
        )
        own_pair = dot(own_pick, vectors)
        own[...] = own_pair.astype(BF16)
        block_out = block.astype(BF16)
        for p in range(N_DP):
            payload[p] = block_out
        for s in range(ROWS_DEV):
            with_own = jnp.where(row == ROWS_DEV, own_pair[s : s + 1], block)
            with_own = jnp.where(row == ROWS_DEV + 1, own_pair[SLOTS + s : SLOTS + s + 1], with_own)
            payload[scalars[DEST + s]] = with_own.astype(BF16)

    @pl.when(scalars[SECTION] != layer)
    def _():
        for s in range(ROWS_DEV):
            payload[scalars[DEST + s]] = values[s]


def output_kernel(layer, scalars, received, w_out, payload):
    @pl.when(scalars[SECTION] == layer)
    def _():
        total = jnp.zeros((PADDED, WIDTH), F32)
        for h in range(0, GROUP, 2):
            pair = received[:, h * SLOTS : (h + 2) * SLOTS, :].astype(F32)
            left = pair[:, :SLOTS].reshape(PADDED, HEAD).astype(BF16)
            right = pair[:, SLOTS:].reshape(PADDED, HEAD).astype(BF16)
            total = total + dot(
                jnp.concatenate([left, right], 1), w_out[h * HEAD : (h + 2) * HEAD, :]
            )
        real = (iota((PADDED, WIDTH), 0) & (SLOTS - 1)) < ROWS_DEV
        payload[...] = jnp.where(real, total, 0.0).astype(BF16).reshape(N_TS, TS_ROWS, WIDTH)


def sum_kernel(layer, scalars, *refs):
    if layer == 0:
        replica, slot, hidden, received, payload, result = refs
        new_index = replica[...] * ROWS_DEV + slot[...]
        rows = old_order(new_index, hidden[...])
        row, column = iota((TS_ROWS, ROWS), 0), iota((TS_ROWS, ROWS), 1)
        in_slot = row & (SLOTS - 1)
        place = (scalars[TS_BLOCK] * 2 + (row >> 3)) * ROWS_DEV + in_slot
        residual = dot(pick((column == place) & (in_slot < ROWS_DEV)), rows)
    else:
        before, received, payload, result = refs
        residual = before[...].astype(F32)
    total = received[layer].astype(F32)
    for t in range(1, N_TS // 2):
        total = total + received[2 * t + layer].astype(F32)
    total = (residual + total).astype(BF16)
    result[...] = total
    for i in range(N_TS):
        payload[i] = total


def order_kernel(scalars, replica, slot, first, second, out):
    new_index = replica[...] * ROWS_DEV + slot[...]
    to_new = pick(iota((ROWS, ROWS), 0) == new_index)
    row, column = iota((ROWS, PADDED), 0), iota((ROWS, PADDED), 1)
    group = over_six(row)
    compact = pick(column == group * SLOTS + row - group * ROWS_DEV)

    def write(source):
        rows = dot(compact, source[...].reshape(PADDED, WIDTH)).astype(BF16)
        out[...] = dot(to_new, rows).astype(BF16)

    pl.when(scalars[SECTION] == 0)(lambda: write(first))
    pl.when(scalars[SECTION] == 1)(lambda: write(second))


def cache_kernel(
    scalars, keys, values, own_0, own_1, scatter_0, gather_0, scatter_1, gather_1, key_out, value_out
):
    me = scalars[REPLICA]
    position = iota((CONTEXT, HEAD), 0)

    def write(moved_keys, moved_values, gathered, own):
        own_rows = own[...].astype(F32)
        for r in range(ROWS_DEV):
            source = scalars[SOURCE + r]
            anchor = over_six(source)
            held = source - anchor * ROWS_DEV
            written = position == scalars[NEW_LEN + r]

            @pl.when(anchor == me)
            def _():
                own_row = iota((16, HEAD), 0)
                new_key = jnp.sum(jnp.where(own_row == held, own_rows, 0.0), axis=0, keepdims=True)
                new_value = jnp.sum(
                    jnp.where(own_row == held + SLOTS, own_rows, 0.0), axis=0, keepdims=True
                )
                key_out[r] = jnp.where(written, new_key, keys[held].astype(F32)).astype(BF16)
                value_out[r] = jnp.where(written, new_value, values[held].astype(F32)).astype(BF16)

            @pl.when(anchor != me)
            def _():
                pair = gathered[anchor, 0:16, :].astype(F32)
                new_key = pair[ROWS_DEV : ROWS_DEV + 1]
                new_value = pair[ROWS_DEV + 1 : ROWS_DEV + 2]
                key_out[r] = jnp.where(written, new_key, moved_keys[anchor].astype(F32)).astype(BF16)
                value_out[r] = jnp.where(
                    written, new_value, moved_values[anchor].astype(F32)
                ).astype(BF16)

    pl.when(scalars[SECTION] == 0)(lambda: write(scatter_1, gather_1, gather_0, own_0))
    pl.when(scalars[SECTION] == 1)(lambda: write(scatter_0, gather_0, gather_1, own_1))


def call(kernel, out_shapes, operands, scratch=(), name=None):
    return pl.pallas_call(
        kernel,
        out_shape=out_shapes,
        in_specs=[SMEM_SPEC] + [VMEM_SPEC] * (len(operands) - 1),
        out_specs=jax.tree.map(lambda _: VMEM_SPEC, out_shapes),
        scratch_shapes=list(scratch),
        compiler_params=pltpu.CompilerParams(vmem_limit_bytes=24 * 1024 * 1024),
        name=name,
    )(*operands)


def exchange(value, axes):
    return lax.all_to_all(value, axes, split_axis=0, concat_axis=0, tiled=True)


def on_device(
    hidden_in,
    norm_gain,
    w_query,
    w_key,
    w_value,
    w_out,
    key_cache,
    value_cache,
    context_len,
    dest_replica,
    dest_slot,
):
    me = lax.axis_index("dp")
    section = lax.axis_index("section")
    ts_block = lax.axis_index("tensor") * 2 + section
    keys, values = key_cache[0], value_cache[0]
    first_row = me * ROWS_DEV
    new_index = dest_replica * ROWS_DEV + dest_slot
    dest = lax.dynamic_slice_in_dim(dest_replica, first_row, ROWS_DEV)
    held_len = lax.dynamic_slice_in_dim(context_len, first_row, ROWS_DEV)
    mine = new_index[None, :] == (first_row + jnp.arange(ROWS_DEV, dtype=jnp.int32))[:, None]
    source = jnp.sum(jnp.where(mine, jnp.arange(ROWS, dtype=jnp.int32)[None, :], 0), 1)
    new_len = jnp.sum(jnp.where(mine, context_len[None, :], 0), 1)
    scalars = jnp.concatenate(
        [jnp.stack([section, me, ts_block, section]).astype(jnp.int32), dest, held_len, source, new_len]
    )
    half = HEAD // 2
    inverse_freq = ROPE_BASE ** (-(jnp.arange(half, dtype=F32) * (2.0 / HEAD)))
    padded_len = jnp.concatenate([held_len, jnp.zeros((SLOTS - ROWS_DEV,), jnp.int32)])
    angles = padded_len.astype(F32)[:, None] * jnp.concatenate([inverse_freq, inverse_freq])[None, :]
    cosine = jnp.cos(angles)
    sine = jnp.sin(angles) * jnp.where(jnp.arange(HEAD) < half, -1.0, 1.0)[None, :]
    replica_row, slot_row = dest_replica[None, :], dest_slot[None, :]

    block_shape = jax.ShapeDtypeStruct((N_DP, BLOCK, HEAD), BF16)
    ts_shape = jax.ShapeDtypeStruct((N_TS, TS_ROWS, WIDTH), BF16)
    result_shape = jax.ShapeDtypeStruct((TS_ROWS, WIDTH), BF16)
    own_shape = jax.ShapeDtypeStruct((16, HEAD), BF16)
    tables = (replica_row, slot_row)
    weights = (norm_gain, w_query[0], w_key[0], w_value[0])

    hidden, before = hidden_in, None
    scattered, gathered, owns, outputs = [], [], [], []
    for layer in range(2):
        project = lambda *refs, layer=layer: project_kernel(layer, *refs)
        attend = lambda *refs, layer=layer: attend_kernel(layer, *refs)
        output = lambda *refs, layer=layer: output_kernel(layer, *refs)
        summed = lambda *refs, layer=layer: sum_kernel(layer, *refs)
        payload = call(
            project,
            block_shape,
            (scalars,) + (tables if layer == 0 else ()) + (hidden,) + weights + (keys,),
            [pltpu.VMEM((BLOCK * N_DP, HEAD), F32)],
            name="project",
        )
        partials = exchange(payload, "dp")
        payload, own = call(
            attend,
            (block_shape, own_shape),
            (scalars, cosine, sine, partials, keys, values),
            name="attend",
        )
        rows = exchange(payload, "dp")
        payload = call(output, ts_shape, (scalars, rows, w_out[0]), name="output")
        received = exchange(payload, ("tensor", "section"))
        payload, before = call(
            summed,
            (ts_shape, result_shape),
            (scalars,) + (tables + (hidden_in,) if layer == 0 else (before,)) + (received,),
            name="sum",
        )
        hidden = exchange(payload, ("tensor", "section"))
        scattered.append(partials)
        gathered.append(rows)
        owns.append(own)
        outputs.append(hidden)

    cache_shape = jax.ShapeDtypeStruct((ROWS_DEV, CONTEXT, HEAD), BF16)
    key_out, value_out = call(
        cache_kernel,
        (cache_shape, cache_shape),
        (scalars, keys, values, *owns, scattered[0], gathered[0], scattered[1], gathered[1]),
        name="caches",
    )
    layer_out = call(
        order_kernel,
        jax.ShapeDtypeStruct((ROWS, WIDTH), BF16),
        (scalars,) + tables + tuple(outputs),
        name="order",
    )
    return layer_out[None], key_out[None], value_out[None]


def solution(mesh):
    return jax.shard_map(
        on_device,
        mesh=mesh,
        in_specs=(
            P(None, "dp"),
            P("section", "dp"),
            P("section", "dp", "tensor"),
            P("section", "dp", "tensor"),
            P("section", "dp", "tensor"),
            P("section", "tensor", "dp"),
            P("section", "dp", None, "tensor"),
            P("section", "dp", None, "tensor"),
            P(),
            P(),
            P(),
        ),
        out_specs=(
            P("section", None, "dp"),
            P("section", "dp", None, "tensor"),
            P("section", "dp", None, "tensor"),
        ),
        check_vma=False,
    )
```

time: 760 us -> 169 us (0.22)
  waiting for transfers between devices: 497 us -> 19.8 us
  blocking collectives: 197 us -> 113 us
  between operations: 14.8 us -> 0.8 us
  Pallas kernels: 0 us -> 11.4 us
  local copies, waits for them, and re-layouts: 15.2 us -> 7.34 us
    unnamed x6 -> x0, waiting for transfers between devices: 316 us -> none
    psum x2 -> x0, waiting for transfers between devices: 175 us -> none  [one_pass(): lax.psum(partial_out.astype(jnp.bfloat16), 'tensor').astype(jnp.float32)]
    psum x2 -> x0, blocking collectives: 126 us -> none  [one_pass(): square_sum = lax.psum(jnp.sum(widened * widened, 1), 'dp')]
    all_to_all x0 -> x6, blocking collectives: none -> 113 us  [exchange(): return lax.all_to_all(value, axes, split_axis=0, concat_axis=0, tiled=True)]
    all_gather x2 -> x0, blocking collectives: 71.8 us -> none  [one_pass(): lax.all_gather(flattened, 'dp', axis=0, tiled=True)]
    all_to_all x2, waiting for transfers between devices: 0.01 us -> 19.8 us  [exchange(): return lax.all_to_all(value, axes, split_axis=0, concat_axis=0, tiled=True)]
    pallas_call x0 -> x10, Pallas kernels: none -> 11.4 us  [call(): pl.pallas_call(kernel, out_shape=out_shapes, in_specs=[SMEM_SPEC] + [VMEM...]
  transfers between devices with their start and end apart: 7 -> 2, of which waited for: 5 -> 2; matrix products, arithmetic and copies ran while one was open for 2% -> 0% of each run, Pallas kernels for 0% -> 1%
where the time goes in v1:
time: 169 us; the launch traced here: 168 us
  blocking collectives  113 us (67%)
  waiting for transfers between devices  19.8 us (12%)
  starting transfers between devices  14 us (8%)
  Pallas kernels  11.4 us (7%)
  local copies, waits for them, and re-layouts  7.34 us (4%)
  other arithmetic  1.79 us (1%)
    all_to_all x6, blocking collectives, exchange(): return lax.all_to_all(value, axes, split_axis=0, concat_axis=0, tiled=True)  113 us
    all_to_all x2, waiting for transfers between devices, exchange(): return lax.all_to_all(value, axes, split_axis=0, concat_axis=0, tiled=True)  19.8 us
    all_to_all x2, starting transfers between devices, exchange(): return lax.all_to_all(value, axes, split_axis=0, concat_axis=0, tiled=True)  14 us
    pallas_call x10, Pallas kernels, call(): pl.pallas_call(kernel, out_shape=out_shapes, in_specs=[SMEM_SPEC] + [VMEM...  11.4 us
    unnamed x32, local copies, waits for them, and re-layouts  5.75 us
  transfers between devices with their start and end apart: 2, of which 2 were waited for; matrix products, arithmetic and copies ran while one was open for 0% of the time, Pallas kernels for 1%

profile of v1, /device:TPU:1, one launch (start us, length us, event | category | flops | bytes accessed | tf_op | source)
XLA Modules:
  0.0 168.2 jit_solution(11085786640495989444)
XLA Ops:
  0.7 0.8 dynamic_slice.7
  1.4 0.8 dynamic_slice.6
  2.2 0.7 multiply_add_fusion
  2.9 0.9 fusion.1
  3.9 0.7 copy-done.11
  4.5 0.9 copy-done
  5.4 1.0 copy-done.2
  6.5 0.9 copy-done.6
  7.4 0.8 copy-done.9
  8.2 0.7 copy-done.12
  8.9 0.7 copy-done.14
  9.6 1.4 project.2
  10.9 10.6 %all-to-all-start = ((bf16[32,64,128]{2,1,0:T(8,128)(2,1)}), bf16[32,64,128]{2,1,0:T(8,128)(2,1)S(1)}, u32[]{:S(2)}, u32[]{:S(2)}) async-start(bf16[32,64,128]{2,1,0:T(8,128)(2,1)} %project.2), calls=%async_computation | async-start | bytes 1048576 | tf_op jit(solution)/shard_map/all_to_all | solution.py:286
  21.7 0.1 fusion.2
  21.8 12.6 %all-to-all-done.refs_3_.scatter_0 = bf16[32,64,128]{2,1,0:T(8,128)(2,1)S(1)} async-done(((bf16[32,64,128]{2,1,0:T(8,128)(2,1)}), bf16[32,64,128]{2,1,0:T(8,128)(2,1)S(1)}, u32[]{:S(2)}, u32[]{:S(2)}) %all-to-all-start) | async-done | bytes 524320 | tf_op jit(solution)/shard_map/all_to_all | solution.py:286
  34.4 0.6 attend.2
  35.0 19.3 %all_to_all.40.refs_1_.gather_0 = bf16[32,64,128]{2,1,0:T(8,128)(2,1)S(1)} all-to-all(bf16[32,64,128]{2,1,0:T(8,128)(2,1)S(1)} %get-tuple-element.12), channel_id=1, replica_groups=mesh['dp'=32,'tensor'=8,'section'=2] {'dp'}, dimensions={0} | all-to-all | bytes 1048576 | tf_op jit(solution)/shard_map/all_to_all | solution.py:286
  54.3 0.5 output.2
  54.9 25.8 %all_to_all.41.refs_4_ = bf16[16,16,256]{2,1,0:T(8,128)(2,1)S(1)} all-to-all(bf16[16,16,256]{2,1,0:T(8,128)(2,1)S(1)} %output.2), channel_id=1, replica_groups=mesh['dp'=32,'tensor'=8,'section'=2] {'tensor','section'}, dimensions={0} | all-to-all | bytes 262144 | tf_op jit(solution)/shard_map/all_to_all | solution.py:286
  80.6 0.9 sum.2
  81.6 11.7 %all_to_all.42.refs_1_.first = bf16[16,16,256]{2,1,0:T(8,128)(2,1)S(1)} all-to-all(bf16[16,16,256]{2,1,0:T(8,128)(2,1)S(1)} %get-tuple-element.13), channel_id=1, replica_groups=mesh['dp'=32,'tensor'=8,'section'=2] {'tensor','section'}, dimensions={0} | all-to-all | bytes 262144 | tf_op jit(solution)/shard_map/all_to_all | solution.py:286
  93.3 1.6 project.3
  94.9 21.7 %all_to_all.43.refs_3_.scatter_1 = bf16[32,64,128]{2,1,0:T(8,128)(2,1)S(1)} all-to-all(bf16[32,64,128]{2,1,0:T(8,128)(2,1)S(1)} %project.3), channel_id=1, replica_groups=mesh['dp'=32,'tensor'=8,'section'=2] {'dp'}, dimensions={0} | all-to-all | bytes 1048576 | tf_op jit(solution)/shard_map/all_to_all | solution.py:286
  116.6 1.4 attend.3
  118.0 22.1 %all_to_all.44.refs_1_.gather_1 = bf16[32,64,128]{2,1,0:T(8,128)(2,1)S(1)} all-to-all(bf16[32,64,128]{2,1,0:T(8,128)(2,1)S(1)} %get-tuple-element.15), channel_id=1, replica_groups=mesh['dp'=32,'tensor'=8,'section'=2] {'dp'}, dimensions={0} | all-to-all | bytes 1048576 | tf_op jit(solution)/shard_map/all_to_all | solution.py:286
  140.1 0.8 output.3
  140.9 12.5 %all_to_all.45.refs_2_ = bf16[16,16,256]{2,1,0:T(8,128)(2,1)S(1)} all-to-all(bf16[16,16,256]{2,1,0:T(8,128)(2,1)S(1)} %output.3), channel_id=1, replica_groups=mesh['dp'=32,'tensor'=8,'section'=2] {'tensor','section'}, dimensions={0} | all-to-all | bytes 262144 | tf_op jit(solution)/shard_map/all_to_all | solution.py:286
  153.4 1.2 sum.3
  154.7 3.4 %all-to-all-start.7 = ((bf16[16,16,256]{2,1,0:T(8,128)(2,1)}), bf16[16,16,256]{2,1,0:T(8,128)(2,1)S(1)}, u32[]{:S(2)}, u32[]{:S(2)}) async-start(bf16[16,16,256]{2,1,0:T(8,128)(2,1)} %get-tuple-element.16), calls=%async_computation.7 | async-start | bytes 262144 | tf_op jit(solution)/shard_map/all_to_all | solution.py:286
  158.1 1.4 caches.1
  159.4 7.1 %all-to-all-done.7.second = bf16[16,16,256]{2,1,0:T(8,128)(2,1)S(1)} async-done(((bf16[16,16,256]{2,1,0:T(8,128)(2,1)}), bf16[16,16,256]{2,1,0:T(8,128)(2,1)S(1)}, u32[]{:S(2)}, u32[]{:S(2)}) %all-to-all-start.7) | async-done | bytes 131104 | tf_op jit(solution)/shard_map/all_to_all | solution.py:286
  166.5 1.6 order.1
  (30 shorter events, 0.2 us)
Async XLA Ops:
  0.6 3.2 %copy-start.8 = (bf16[1,256,128]{2,1,0:T(8,128)(2,1)S(1)}, bf16[1,256,128]{2,1,0:T(8,128)(2,1)}, u32[]{:S(2)}) copy-start(bf16[1,256,128]{2,1,0:T(8,128)(2,1)} %param.14) | copy-start | bytes 196612
  3.8 0.7 copy-start.11
  4.5 0.9 copy-start
  5.4 1.0 copy-start.2
  6.5 0.9 copy-start.6
  7.4 0.8 copy-start.9
  8.2 0.7 copy-start.12
  8.9 0.7 copy-start.14
  10.9 23.5 %copy-start.1 = (bf16[1,6,64,128]{3,2,1,0:T(8,128)(2,1)S(1)}, bf16[1,6,64,128]{3,2,1,0:T(8,128)(2,1)}, u32[]{:S(2)}) copy-start(bf16[1,6,64,128]{3,2,1,0:T(8,128)(2,1)} %param.17) | copy-start | bytes 294916
  10.9 23.5 %copy-start.5 = (bf16[1,6,64,128]{3,2,1,0:T(8,128)(2,1)S(1)}, bf16[1,6,64,128]{3,2,1,0:T(8,128)(2,1)}, u32[]{:S(2)}) copy-start(bf16[1,6,64,128]{3,2,1,0:T(8,128)(2,1)} %param.18) | copy-start | bytes 294916
  10.9 23.5 %all-to-all-start = ((bf16[32,64,128]{2,1,0:T(8,128)(2,1)}), bf16[32,64,128]{2,1,0:T(8,128)(2,1)S(1)}, u32[]{:S(2)}, u32[]{:S(2)}) async-start(bf16[32,64,128]{2,1,0:T(8,128)(2,1)} %project.2), calls=%async_computation | async-start | bytes 1048576 | tf_op jit(solution)/shard_map/all_to_all | solution.py:286
  35.0 19.3 %copy-start.4 = (bf16[1,1024,256]{2,1,0:T(8,128)(2,1)S(1)}, bf16[1,1024,256]{2,1,0:T(8,128)(2,1)}, u32[]{:S(2)}) copy-start(bf16[1,1024,256]{2,1,0:T(8,128)(2,1)} %param.16) | copy-start | bytes 1572868
  54.3 26.3 %copy-start.7 = (bf16[192,256]{1,0:T(8,128)(2,1)S(1)}, bf16[192,256]{1,0:T(8,128)(2,1)}, u32[]{:S(2)}) copy-start(bf16[192,256]{1,0:T(8,128)(2,1)} %refs_3_.3) | copy-start | bytes 294916
  54.3 26.3 %copy-start.13 = (s32[192]{0:T(256)S(1)}, s32[192]{0:T(256)}, u32[]{:S(2)}) copy-start(s32[192]{0:T(256)} %param.21) | copy-start | bytes 2308
  54.9 38.4 %copy-start.3 = (bf16[1,256,1024]{2,1,0:T(8,128)(2,1)S(1)}, bf16[1,256,1024]{2,1,0:T(8,128)(2,1)}, u32[]{:S(2)}) copy-start(bf16[1,256,1024]{2,1,0:T(8,128)(2,1)} %param.13) | copy-start | bytes 1572868
  81.5 11.8 %copy-start.10 = (bf16[1,256,128]{2,1,0:T(8,128)(2,1)S(1)}, bf16[1,256,128]{2,1,0:T(8,128)(2,1)}, u32[]{:S(2)}) copy-start(bf16[1,256,128]{2,1,0:T(8,128)(2,1)} %param.15) | copy-start | bytes 196612
  81.6 11.7 %copy-start.15 = (f32[1,256]{1,0:T(1,128)S(1)}, f32[1,256]{1,0:T(1,128)}, u32[]{:S(2)}) copy-start(f32[1,256]{1,0:T(1,128)} %refs_2_.1) | copy-start | bytes 3076
  154.7 11.9 %all-to-all-start.7 = ((bf16[16,16,256]{2,1,0:T(8,128)(2,1)}), bf16[16,16,256]{2,1,0:T(8,128)(2,1)S(1)}, u32[]{:S(2)}, u32[]{:S(2)}) async-start(bf16[16,16,256]{2,1,0:T(8,128)(2,1)} %get-tuple-element.16), calls=%async_computation.7 | async-start | bytes 262144 | tf_op jit(solution)/shard_map/all_to_all | solution.py:286

commit v2 on v1

v2 whole, which is shorter than its diff:
```python
import jax
import jax.numpy as jnp
from jax import lax
from jax.experimental import pallas as pl
from jax.experimental.pallas import tpu as pltpu
from jax.sharding import PartitionSpec as P

N_DP = 32
N_TENSOR = 8
ROWS_DEV = 6
ROWS = 192
TRIO = 3
HALF_ROWS = N_DP * TRIO
CONTEXT = 64
MOVES = 4
PIECES = 4
HEAD = 128
GROUP = 8
PARTS = GROUP + 2
USED = 32
BLOCK = USED + MOVES * PIECES
WIDTH = 256
MODEL = 8192
CACHE_ROWS = TRIO * CONTEXT
GAIN_ROW = CACHE_ROWS + WIDTH
EPSILON = 1e-06
ROPE_BASE = 1000000.0
F32 = jnp.float32
BF16 = jnp.bfloat16

SECTION, REPLICA = 0, 1
DEST, HELD_LEN, NEW_LEN, SOURCE = 0, 6, 12, 18

SMEM_SPEC = pl.BlockSpec(memory_space=pltpu.SMEM)
VMEM_SPEC = pl.BlockSpec(memory_space=pltpu.VMEM)
HBM_SPEC = pl.BlockSpec(memory_space=pltpu.HBM)


def iota(shape, dim):
    return lax.broadcasted_iota(jnp.int32, shape, dim)


def pick(condition):
    return jnp.where(condition, 1.0, 0.0).astype(BF16)


def over_six(index):
    return (index * 171) >> 10


def over_ten(index):
    return (index * 205) >> 11


def dot(left, right, contract=((1,), (0,))):
    return lax.dot_general(left, right, (contract, ((), ())), preferred_element_type=F32)


def to_new_order(new_index):
    return pick(iota((ROWS, ROWS), 0) == new_index)


def spread_part(spread, slots, part, product, first=0):
    for s in range(slots):
        row = (s // TRIO) * USED + (s % TRIO) * PARTS + part
        spread[pl.ds(row * N_DP, N_DP), :] = product[s * N_DP : (s + 1) * N_DP]


def spread_squares(spread, slots, square):
    lane = iota((N_DP, HEAD), 1)
    for half in range(slots // TRIO):
        squares = jnp.zeros((N_DP, HEAD), F32)
        for s in range(TRIO):
            first = (half * TRIO + s) * N_DP
            squares = jnp.where(lane == s, square[first : first + N_DP], squares)
        high = squares.astype(BF16).astype(F32)
        row = half * USED + TRIO * PARTS
        spread[pl.ds(row * N_DP, N_DP), :] = high
        spread[pl.ds((row + 1) * N_DP, N_DP), :] = squares - high


def spread_products(spread, slots, scaled, w_query, w_key, w_value):
    for part in range(0, GROUP, 2):
        product = dot(scaled, w_query[:, part * HEAD : (part + 2) * HEAD])
        spread_part(spread, slots, part, product[:, :HEAD])
        spread_part(spread, slots, part + 1, product[:, HEAD:])
    spread_part(spread, slots, GROUP, dot(scaled, w_key))
    spread_part(spread, slots, GROUP + 1, dot(scaled, w_value))


def gathered_block(spread, half, replica):
    return spread[pl.ds(half * USED * N_DP + replica, USED, stride=N_DP), :].astype(BF16)


def first_kernel(
    ids, new_index, hidden_in, gain_in, query_in, key_in, value_in,
    kept, shipped, residual, to_slots_out,
    spread, hidden, gain, w_query, w_key, w_value, arrived,
):
    pairs = (
        (hidden_in, hidden),
        (gain_in, gain),
        (query_in.at[0], w_query),
        (key_in.at[0], w_key),
        (value_in.at[0], w_value),
    )
    copies = [pltpu.make_async_copy(src, dst, arrived.at[i]) for i, (src, dst) in enumerate(pairs)]
    for copy in copies:
        copy.start()
    row, column = iota((ROWS, ROWS), 0), iota((ROWS, ROWS), 1)
    by_slot_order = pick(column == (row & (N_DP - 1)) * ROWS_DEV + (row >> 5))
    to_slots = dot(by_slot_order, to_new_order(new_index[...]), ((1,), (1,))).astype(BF16)
    to_slots_out[...] = to_slots
    copies[0].wait()
    by_slot = dot(to_slots, hidden[...])

    @pl.when(ids[SECTION] == 0)
    def _():
        residual[...] = by_slot[:HALF_ROWS].astype(BF16)

    @pl.when(ids[SECTION] == 1)
    def _():
        residual[...] = by_slot[HALF_ROWS:].astype(BF16)

    for copy in copies[1:]:
        copy.wait()

    @pl.when(ids[SECTION] == 0)
    def _():
        square = jnp.sum(by_slot * by_slot, axis=1, keepdims=True)
        scaled = (by_slot * gain[...]).astype(BF16)
        spread_products(spread, ROWS_DEV, scaled, w_query, w_key[...], w_value[...])
        spread_squares(spread, ROWS_DEV, square)
        for p in range(N_DP):
            kept[p] = gathered_block(spread, 0, p)
            shipped[p] = gathered_block(spread, 1, p)


def join_kernel(ids, table, kept, received, keys, values, payload, spread):
    count = jnp.int32(0)
    for s in range(ROWS_DEV):
        leaves = table[DEST + s] != ids[REPLICA]

        @pl.when(leaves)
        def _():
            base = pl.multiple_of(count * (PIECES * N_DP), N_DP)
            spread[pl.ds(base, CONTEXT), :] = keys[s].astype(F32)
            spread[pl.ds(base + CONTEXT, CONTEXT), :] = values[s].astype(F32)

        count = count + jnp.where(leaves, 1, 0)
    for p in range(N_DP):
        payload[p, USED:, :] = spread[pl.ds(p, MOVES * PIECES, stride=N_DP), :].astype(BF16)

    @pl.when(ids[SECTION] == 0)
    def _():
        payload[:, :USED, :] = kept[...]

    @pl.when(ids[SECTION] == 1)
    def _():
        payload[:, :USED, :] = received[...]


def pack_kernel(ids, keys, values, w_key, w_value, gain, packed):
    other = (1 - ids[SECTION]) * TRIO
    for s in range(TRIO):
        packed[s * CONTEXT : (s + 1) * CONTEXT, :HEAD] = keys[other + s]
        packed[s * CONTEXT : (s + 1) * CONTEXT, HEAD:] = values[other + s]
    packed[CACHE_ROWS:GAIN_ROW, :HEAD] = w_key[...]
    packed[CACHE_ROWS:GAIN_ROW, HEAD:] = w_value[...]
    high = gain[...].astype(BF16).astype(F32)
    middle = (gain[...] - high).astype(BF16).astype(F32)
    low = gain[...] - high - middle
    row = iota((16, WIDTH), 0)
    terms = jnp.where(row == 0, high, jnp.where(row == 1, middle, jnp.where(row == 2, low, 0.0)))
    packed[GAIN_ROW:, :] = terms.astype(BF16)


def choose_kernel(layer, ids, local, other, chosen):
    @pl.when(ids[SECTION] == layer)
    def _():
        chosen[...] = local[...]

    @pl.when(ids[SECTION] != layer)
    def _():
        chosen[...] = other[...]


def forward(route, received, payload, pieces, sorted_pieces):
    count = N_DP * MOVES
    for p in range(N_DP):
        pieces[pl.ds(p * MOVES * PIECES, MOVES * PIECES), :] = received[p, USED:, :].astype(F32)
    to_replica = pick(iota((count, count), 0) == route[...])
    for i in range(PIECES):
        part = pieces[pl.ds(i, count, stride=PIECES), :].astype(BF16)
        sorted_pieces[pl.ds(i, count, stride=PIECES), :] = dot(to_replica, part, ((0,), (0,)))
    for p in range(N_DP):
        payload[p, USED:, :] = sorted_pieces[
            pl.ds(p * MOVES * PIECES, MOVES * PIECES), :
        ].astype(BF16)


def attend_kernel(
    layer, ids, table, cosine, sine, received, keys, values, packed, *refs
):
    if layer == 0:
        route, payload, own, pieces, sorted_pieces = refs
        forward(route, received, payload, pieces, sorted_pieces)
    else:
        payload, own = refs
    section = ids[SECTION]

    def attend(all_keys, all_values):
        total = received[0, :USED, :].astype(F32)
        for p in range(1, N_DP):
            total = total + received[p, :USED, :].astype(F32)
        row = iota((USED, HEAD), 0)
        lane = iota((USED, HEAD), 1)
        slot = over_ten(row)
        part = row - slot * PARTS
        tail = TRIO * PARTS
        squares = total[tail : tail + 1] + total[tail + 1 : tail + 2]
        square = jnp.sum(jnp.where(lane == slot, squares, 0.0), axis=1, keepdims=True)
        projected = total * lax.rsqrt(square / MODEL + EPSILON)
        cos_rows = jnp.ones((USED, HEAD), F32)
        sin_rows = jnp.zeros((USED, HEAD), F32)
        for s in range(TRIO):
            turned = (slot == s) & (part <= GROUP)
            cos_rows = jnp.where(turned, cosine[pl.ds(section * TRIO + s, 1), :], cos_rows)
            sin_rows = jnp.where(turned, sine[pl.ds(section * TRIO + s, 1), :], sin_rows)
        vectors = (
            projected * cos_rows + pltpu.roll(projected, HEAD // 2, 1) * sin_rows
        ).astype(BF16)

        scale = HEAD ** (-0.5)
        scores = dot(vectors, all_keys, ((1,), (1,))) * scale
        among = dot(vectors, vectors, ((1,), (1,))) * scale
        wide = (USED, CACHE_ROWS)
        wide_slot = over_ten(iota(wide, 0))
        column = iota(wide, 1)
        live = column < 0
        for s in range(TRIO):
            live = live | (
                (wide_slot == s)
                & (column >= s * CONTEXT)
                & (column < s * CONTEXT + table[HELD_LEN + section * TRIO + s])
            )
        scores = jnp.where(live, scores, -1e30)
        small_slot = over_ten(iota((USED, USED), 0))
        small_column = iota((USED, USED), 1)
        own_score = jnp.sum(
            jnp.where(small_column == small_slot * PARTS + GROUP, among, 0.0), axis=1, keepdims=True
        )
        highest = jnp.maximum(jnp.max(scores, axis=1, keepdims=True), own_score)
        terms = jnp.exp(scores - highest)
        own_term = jnp.exp(own_score - highest)
        denominator = jnp.sum(terms, axis=1, keepdims=True) + own_term
        weights = (terms / denominator).astype(BF16)
        own_weights = jnp.where(
            small_column == small_slot * PARTS + GROUP + 1, own_term / denominator, 0.0
        ).astype(BF16)
        attended = (dot(weights, all_values) + dot(own_weights, vectors)).astype(BF16)

        out_row, in_row = iota((USED, USED), 0), iota((USED, USED), 1)
        out_slot = out_row >> 3
        order = pick((in_row == out_slot * PARTS + (out_row & 7)) & (out_slot < TRIO))
        block = dot(order, attended)
        own_row, own_in = iota((16, USED), 0), iota((16, USED), 1)
        own_slot = own_row & 7
        own_pick = pick(
            (own_in == own_slot * PARTS + GROUP + (own_row >> 3)) & (own_slot < TRIO)
        )
        own_pair = dot(own_pick, vectors)
        own[...] = own_pair.astype(BF16)
        block_out = block.astype(BF16)
        for p in range(N_DP):
            payload[p, :USED, :] = block_out
        for s in range(TRIO):
            with_own = jnp.where(row == TRIO * 8, own_pair[s : s + 1], block)
            with_own = jnp.where(row == TRIO * 8 + 1, own_pair[8 + s : 9 + s], with_own)
            payload[table[DEST + section * TRIO + s], :USED, :] = with_own.astype(BF16)

    @pl.when(section == layer)
    def _():
        first = layer * TRIO
        attend(
            keys[first : first + TRIO].reshape(CACHE_ROWS, HEAD),
            values[first : first + TRIO].reshape(CACHE_ROWS, HEAD),
        )

    @pl.when(section != layer)
    def _():
        attend(packed[:CACHE_ROWS, :HEAD], packed[:CACHE_ROWS, HEAD:])


def output_kernel(received, weight, payload, wide, rows):
    for p in range(N_DP):
        wide[pl.ds(p * USED, USED), :] = received[p, :USED, :].astype(F32)
    for s in range(TRIO):
        for h in range(GROUP):
            rows[s * N_DP : (s + 1) * N_DP, h * HEAD : (h + 1) * HEAD] = wide[
                pl.ds(s * 8 + h, N_DP, stride=USED), :
            ].astype(BF16)

    product = dot(rows[...], weight[...]).astype(BF16)
    for t in range(N_TENSOR):
        payload[t] = product


def summed(received, residual):
    total = received[0].astype(F32)
    for t in range(1, N_TENSOR):
        total = total + received[t].astype(F32)
    return (residual[...].astype(F32) + total).astype(BF16)


def second_kernel(
    ids, received, residual, gain, query, w_key, w_value, packed, payload, result, spread
):
    rows = summed(received, residual)
    result[...] = rows
    by_slot = rows.astype(F32)
    spread_squares(spread, TRIO, jnp.sum(by_slot * by_slot, axis=1, keepdims=True))

    @pl.when(ids[SECTION] == 1)
    def _():
        scaled = (by_slot * gain[...]).astype(BF16)
        spread_products(spread, TRIO, scaled, query, w_key[...], w_value[...])

    @pl.when(ids[SECTION] == 0)
    def _():
        terms = packed[GAIN_ROW:, :].astype(F32)
        other_gain = terms[0:1] + terms[1:2] + terms[2:3]
        scaled = (by_slot * other_gain).astype(BF16)
        spread_products(
            spread,
            TRIO,
            scaled,
            query,
            packed[CACHE_ROWS:GAIN_ROW, :HEAD],
            packed[CACHE_ROWS:GAIN_ROW, HEAD:],
        )

    for p in range(N_DP):
        payload[p] = gathered_block(spread, 0, p)


def last_kernel(ids, received, before, done, result, swapped):
    rows = summed(received, before)
    result[...] = rows

    @pl.when(ids[SECTION] == 0)
    def _():
        swapped[...] = rows

    @pl.when(ids[SECTION] == 1)
    def _():
        swapped[...] = before[...]


def order_kernel(ids, to_slots, first, second, received, out):
    def write(low, high):
        out[...] = (
            dot(to_slots[:HALF_ROWS, :], low[...], ((0,), (0,)))
            + dot(to_slots[HALF_ROWS:, :], high[...], ((0,), (0,)))
        ).astype(BF16)

    pl.when(ids[SECTION] == 0)(lambda: write(first, received))
    pl.when(ids[SECTION] == 1)(lambda: write(received, second))


def own_kernel(ids, table, gathered_0, gathered_1, own_0, own_1, mine, swapped):
    me, section = ids[REPLICA], ids[SECTION]
    row = iota((16, HEAD), 0)
    for layer, (gathered, own) in enumerate(((gathered_0, own_0), (gathered_1, own_1))):
        own_rows = own[...].astype(F32)
        total = jnp.zeros((16, HEAD), F32)
        for r in range(ROWS_DEV):
            source = table[SOURCE + r]
            anchor = over_six(source)
            held = source - anchor * ROWS_DEV
            slot = held - section * TRIO
            here = (slot >= 0) & (slot < TRIO)
            stays = jnp.where(here & (anchor == me), 1.0, 0.0)
            moves = jnp.where(here & (anchor != me), 1.0, 0.0)
            pair = gathered[anchor, USED - 16 : USED, :].astype(F32)
            kept_key = jnp.sum(jnp.where(row == slot, own_rows, 0.0), axis=0, keepdims=True)
            kept_value = jnp.sum(jnp.where(row == slot + 8, own_rows, 0.0), axis=0, keepdims=True)
            new_key = kept_key * stays + pair[8:9] * moves
            new_value = kept_value * stays + pair[9:10] * moves
            total = jnp.where(row == r, new_key, jnp.where(row == r + 8, new_value, total))
        total = total.astype(BF16)

        @pl.when(section == layer)
        def _():
            mine[...] = total

        @pl.when(section != layer)
        def _():
            swapped[...] = total


def cache_kernel(
    ids, table, keys, values, mine, received, gathered, key_out, value_out, done, pieces
):
    me = ids[REPLICA]
    position = iota((CONTEXT, HEAD), 0)
    own = mine[...].astype(F32) + received[...].astype(F32)
    done[...] = own[:8]
    for p in range(N_DP):
        pieces[pl.ds(p * MOVES * PIECES, MOVES * PIECES), :] = gathered[p, USED:, :].astype(F32)
    count = jnp.int32(0)
    for r in range(ROWS_DEV):
        source = table[SOURCE + r]
        anchor = over_six(source)
        written = position == table[NEW_LEN + r]
        moves = anchor != me

        def write(key_rows, value_rows):
            key_out[r] = jnp.where(written, own[r : r + 1], key_rows).astype(BF16)
            value_out[r] = jnp.where(written, own[r + 8 : r + 9], value_rows).astype(BF16)

        @pl.when(anchor == me)
        def _():
            held = source - anchor * ROWS_DEV
            write(keys[held].astype(F32), values[held].astype(F32))

        @pl.when(moves)
        def _():
            parts = [
                pieces[pl.ds(count * PIECES + i, N_DP, stride=MOVES * PIECES), :]
                for i in range(PIECES)
            ]
            write(jnp.concatenate(parts[:2], 0), jnp.concatenate(parts[2:], 0))

        count = count + jnp.where(moves, 1, 0)


def call(kernel, name, specs, out_shapes, operands, scratch=()):
    spec_of = {"s": SMEM_SPEC, "v": VMEM_SPEC, "h": HBM_SPEC, "a": pl.BlockSpec(memory_space=pl.ANY)}
    return pl.pallas_call(
        kernel,
        out_shape=out_shapes,
        in_specs=[spec_of[letter] for letter in specs],
        out_specs=jax.tree.map(lambda _: VMEM_SPEC, out_shapes),
        scratch_shapes=list(scratch),
        compiler_params=pltpu.CompilerParams(vmem_limit_bytes=8 * 1024 * 1024),
        name=name,
    )(*operands)


def exchange(value, axis):
    return lax.all_to_all(value, axis, split_axis=0, concat_axis=0, tiled=True)


def swap(value):
    return lax.ppermute(value, "section", [(0, 1), (1, 0)])


def shape(*dims):
    return jax.ShapeDtypeStruct(dims, BF16)


def on_device(
    hidden_in,
    norm_gain,
    w_query,
    w_key,
    w_value,
    w_out,
    key_cache,
    value_cache,
    context_len,
    dest_replica,
    dest_slot,
):
    me = lax.axis_index("dp")
    section = lax.axis_index("section")
    ids = jnp.stack([section, me]).astype(jnp.int32)
    keys, values = key_cache[0], value_cache[0]
    new_index = (dest_replica * ROWS_DEV + dest_slot)[None, :]
    row = jnp.arange(ROWS, dtype=jnp.int32)
    leaves = dest_replica != row // ROWS_DEV
    before = (row[None, :] // ROWS_DEV == row[:, None] // ROWS_DEV) & (row[None, :] < row[:, None])
    rank = jnp.sum(jnp.where(before & leaves[None, :], 1, 0), 1)
    before = (dest_replica[None, :] == dest_replica[:, None]) & (
        dest_slot[None, :] < dest_slot[:, None]
    )
    place = jnp.sum(jnp.where(before & leaves[None, :], 1, 0), 1)
    arrival = jnp.where(leaves, dest_replica * MOVES + place, -1)
    chosen = arrival[None, :] == jnp.arange(N_DP * MOVES, dtype=jnp.int32)[:, None]
    route = jnp.sum(jnp.where(chosen, (row // ROWS_DEV * MOVES + rank)[None, :], 0), 1)[None, :]
    entry = jnp.arange(4 * ROWS_DEV, dtype=jnp.int32)[:, None]
    kind = entry // ROWS_DEV
    wanted = me * ROWS_DEV + entry % ROWS_DEV
    found = jnp.where(kind < 2, row[None, :], new_index) == wanted
    chosen = jnp.where(
        kind == 0, dest_replica[None, :], jnp.where(kind == 3, row[None, :], context_len[None, :])
    )
    table = jnp.sum(jnp.where(found, chosen, 0), 1)

    half = HEAD // 2
    inverse_freq = ROPE_BASE ** (-(jnp.arange(half, dtype=F32) * (2.0 / HEAD)))
    held_len = jnp.concatenate([table[HELD_LEN : HELD_LEN + ROWS_DEV], jnp.zeros((2,), jnp.int32)])
    angles = held_len.astype(F32)[:, None] * jnp.concatenate([inverse_freq, inverse_freq])[None, :]
    cosine = jnp.cos(angles)
    sine = jnp.sin(angles) * jnp.where(jnp.arange(HEAD) < half, -1.0, 1.0)[None, :]

    kept, shipped, residual, to_slots = call(
        first_kernel,
        "first",
        "svhhhhh",
        (shape(N_DP, USED, HEAD), shape(N_DP, USED, HEAD), shape(HALF_ROWS, WIDTH), shape(ROWS, ROWS)),
        (ids, new_index, hidden_in, norm_gain, w_query, w_key, w_value),
        [
            pltpu.VMEM((2 * USED * N_DP, HEAD), F32),
            pltpu.VMEM((ROWS, WIDTH), BF16),
            pltpu.VMEM((1, WIDTH), F32),
            pltpu.VMEM((WIDTH, GROUP * HEAD), BF16),
            pltpu.VMEM((WIDTH, HEAD), BF16),
            pltpu.VMEM((WIDTH, HEAD), BF16),
            pltpu.SemaphoreType.DMA((5,)),
        ],
    )
    payload = call(
        join_kernel,
        "join",
        "ssvvvv",
        shape(N_DP, BLOCK, HEAD),
        (ids, table, kept, swap(shipped), keys, values),
        [pltpu.VMEM((MOVES * PIECES * N_DP, HEAD), F32)],
    )
    first = exchange(payload, "dp")

    late_keys, late_values, late_key, late_value, late_gain, late_query, late_out, _ = (
        lax.optimization_barrier(
            (keys, values, w_key[0], w_value[0], norm_gain, w_query[0], w_out[0], payload)
        )
    )
    packed = swap(
        call(
            pack_kernel,
            "pack",
            "svvvvv",
            shape(GAIN_ROW + 16, WIDTH),
            (ids, late_keys, late_values, late_key, late_value, late_gain),
        )
    )

    def choose(layer, local, other):
        return call(
            lambda *refs: choose_kernel(layer, *refs),
            "choose",
            "svv",
            shape(*local.shape),
            (ids, local, other),
        )

    def attend(layer, received, *more):
        return call(
            lambda *refs: attend_kernel(layer, *refs),
            "attend",
            "ssvvvvvv" + "v" * len(more),
            (shape(N_DP, USED if layer else BLOCK, HEAD), shape(16, HEAD)),
            (ids, table, cosine, sine, received, keys, values, packed, *more),
            [] if layer else [pltpu.VMEM((N_DP * MOVES * PIECES, HEAD), F32)] * 2,
        )

    def output(received, weight):
        return call(
            output_kernel,
            "output",
            "vv",
            shape(N_TENSOR, HALF_ROWS, WIDTH),
            (received, weight),
            [pltpu.VMEM((N_DP * USED, HEAD), F32), pltpu.VMEM((HALF_ROWS, GROUP * HEAD), BF16)],
        )

    payload, own_0 = attend(0, first, route)
    second = exchange(payload, "dp")
    out_other = swap(late_out)
    sums = exchange(output(second, choose(0, late_out, out_other)), "tensor")
    query = choose(1, late_query, swap(late_query))
    payload, result_0 = call(
        second_kernel,
        "second",
        "svvvvvvv",
        (shape(N_DP, USED, HEAD), shape(HALF_ROWS, WIDTH)),
        (ids, sums, residual, late_gain, query, late_key, late_value, packed),
        [pltpu.VMEM((USED * N_DP, HEAD), F32)],
    )
    third = exchange(payload, "dp")
    payload, own_1 = attend(1, third)
    fourth = exchange(payload, "dp")
    sums = exchange(output(fourth, choose(1, late_out, out_other)), "tensor")
    mine, swapped_own = call(
        own_kernel,
        "own",
        "ssvvvv",
        (shape(16, HEAD), shape(16, HEAD)),
        (ids, table, second, fourth, own_0, own_1),
    )
    key_out, value_out, done = call(
        cache_kernel,
        "caches",
        "ssvvvvv",
        (
            shape(ROWS_DEV, CONTEXT, HEAD),
            shape(ROWS_DEV, CONTEXT, HEAD),
            jax.ShapeDtypeStruct((8, HEAD), F32),
        ),
        (ids, table, keys, values, mine, swap(swapped_own), second),
        [pltpu.VMEM((N_DP * MOVES * PIECES, HEAD), F32)],
    )
    result_1, swapped = call(
        last_kernel,
        "last",
        "svva",
        (shape(HALF_ROWS, WIDTH), shape(HALF_ROWS, WIDTH)),
        (ids, sums, result_0, done),
    )
    layer_out = call(
        order_kernel,
        "order",
        "svvvv",
        shape(ROWS, WIDTH),
        (ids, to_slots, result_0, result_1, swap(swapped)),
    )
    return layer_out[None], key_out[None], value_out[None]


def solution(mesh):
    return jax.shard_map(
        on_device,
        mesh=mesh,
        in_specs=(
            P(None, "dp"),
            P("section", "dp"),
            P("section", "dp", "tensor"),
            P("section", "dp", "tensor"),
            P("section", "dp", "tensor"),
            P("section", "tensor", "dp"),
            P("section", "dp", None, "tensor"),
            P("section", "dp", None, "tensor"),
            P(),
            P(),
            P(),
        ),
        out_specs=(
            P("section", None, "dp"),
            P("section", "dp", None, "tensor"),
            P("section", "dp", None, "tensor"),
        ),
        check_vma=False,
    )
```

time: 169 us -> 146 us (0.86)
  blocking collectives: 113 us -> 19.9 us
  starting transfers between devices: 14 us -> 66.9 us
  waiting for transfers between devices: 19.8 us -> 31.1 us
  Pallas kernels: 11.4 us -> 17.3 us
    all_to_all x6 -> x1, blocking collectives: 113 us -> 19.9 us  [exchange(): return lax.all_to_all(value, axis, split_axis=0, concat_axis=0, tiled=True)]
    ppermute x0 -> x6, starting transfers between devices: none -> 36.2 us  [swap(): return lax.ppermute(value, 'section', [(0, 1), (1, 0)])]
    all_to_all x2 -> x5, starting transfers between devices: 14 us -> 30.7 us  [exchange(): return lax.all_to_all(value, axis, split_axis=0, concat_axis=0, tiled=True)]
    ppermute x0 -> x6, waiting for transfers between devices: none -> 5.87 us  [swap(): return lax.ppermute(value, 'section', [(0, 1), (1, 0)])]
    pallas_call x10 -> x15, Pallas kernels: 11.4 us -> 17.3 us  [call(): pl.pallas_call(kernel, out_shape=out_shapes, in_specs=[spec_of[letter] fo...]
    all_to_all x2 -> x5, waiting for transfers between devices: 19.8 us -> 25.2 us  [exchange(): return lax.all_to_all(value, axis, split_axis=0, concat_axis=0, tiled=True)]
    unnamed x32 -> x46, local copies, waits for them, and re-layouts: 5.75 us -> 7.68 us
  transfers between devices with their start and end apart: 2 -> 11, of which waited for: 2 -> 11; matrix products, arithmetic and copies ran while one was open for 0% -> 0% of each run, Pallas kernels for 1% -> 3%
where the time goes in v2:
time: 146 us; the launch traced here: 145 us
  starting transfers between devices  66.9 us (46%)
  waiting for transfers between devices  31.1 us (21%)
  blocking collectives  19.9 us (14%)
  Pallas kernels  17.3 us (12%)
  local copies, waits for them, and re-layouts  7.75 us (5%)
    ppermute x6, starting transfers between devices, swap(): return lax.ppermute(value, 'section', [(0, 1), (1, 0)])  36.2 us
    all_to_all x5, starting transfers between devices, exchange(): return lax.all_to_all(value, axis, split_axis=0, concat_axis=0, tiled=True)  30.7 us
    all_to_all x5, waiting for transfers between devices, exchange(): return lax.all_to_all(value, axis, split_axis=0, concat_axis=0, tiled=True)  25.2 us
    all_to_all x1, blocking collectives, exchange(): return lax.all_to_all(value, axis, split_axis=0, concat_axis=0, tiled=True)  19.9 us
    pallas_call x15, Pallas kernels, call(): pl.pallas_call(kernel, out_shape=out_shapes, in_specs=[spec_of[letter] fo...  17.3 us
    unnamed x46, local copies, waits for them, and re-layouts  7.68 us
    ppermute x6, waiting for transfers between devices, swap(): return lax.ppermute(value, 'section', [(0, 1), (1, 0)])  5.87 us
  transfers between devices with their start and end apart: 11, of which 11 were waited for; matrix products, arithmetic and copies ran while one was open for 0% of the time, Pallas kernels for 3%

profile of v2, /device:TPU:1, one launch (start us, length us, event | category | flops | bytes accessed | tf_op | source)
XLA Modules:
  0.0 144.8 jit_solution(9227240690613103503)
XLA Ops:
  3.0 1.0 copy-done.2
  5.7 0.9 copy-done.9
  6.6 1.3 first.1
  8.0 9.7 %collective-permute-start = (bf16[32,32,128]{2,1,0:T(8,128)(2,1)S(1)}, bf16[32,32,128]{2,1,0:T(8,128)(2,1)S(1)}, u32[]{:S(2)}, u32[]{:S(2)}) collective-permute-start(bf16[32,32,128]{2,1,0:T(8,128)(2,1)S(1)} %get-tuple-element.29), channel_id=1, source_target_pairs={{0,1},{1,0},{2,3},{3,2},{4,5},{5,4},{6,7},{7,6},{8,9},{9,8},{10,11... | collective-permute-start | bytes 786440 | tf_op jit(solution)/shard_map/ppermute | solution.py:456
  18.8 1.5 %join.1 = bf16[32,48,128]{2,1,0:T(8,128)(2,1)} custom-call(s32[2]{0:T(128)S(1)} %pad_add_fusion.ids.refs_0_, s32[24]{0:T(128)S(1)} %select_reduce_fusion.3.table.refs_1_, bf16[32,32,128]{2,1,0:T(8,128)(2,1)S(1)} %get-tuple-element.28.kept, bf16[32,32,128]{2,1,0:T(8,128)(2,1)S(1)} %collective-permute-done.received, bf16[6,64,128]{2,1,0:T(8,128)(2,1)S(1)} %bitcast.13, ...), custom_call_target="tpu_custom_call" | custom-call | tf_op jit(solution)/shard_map/join/pallas_call | solution.py:440
  20.4 4.4 %all-to-all-start = ((bf16[32,48,128]{2,1,0:T(8,128)(2,1)}), bf16[32,48,128]{2,1,0:T(8,128)(2,1)S(1)}, u32[]{:S(2)}, u32[]{:S(2)}) async-start(bf16[32,48,128]{2,1,0:T(8,128)(2,1)} %join.1), calls=%async_computation | async-start | bytes 786432 | tf_op jit(solution)/shard_map/all_to_all | solution.py:452
  25.7 2.6 %collective-permute-start.1 = (bf16[464,256]{1,0:T(8,128)(2,1)S(1)}, bf16[464,256]{1,0:T(8,128)(2,1)S(1)}, u32[]{:S(2)}, u32[]{:S(2)}) collective-permute-start(bf16[464,256]{1,0:T(8,128)(2,1)S(1)} %pack.1), channel_id=1, source_target_pairs={{0,1},{1,0},{2,3},{3,2},{4,5},{5,4},{6,7},{7,6},{8,9},{9,8},{10,11... | collective-permute-start | bytes 712712 | tf_op jit(solution)/shard_map/ppermute | solution.py:456
  28.4 1.0 collective-permute-done.1.refs_7_.packed
  29.4 7.2 %all-to-all-done.refs_4_ = bf16[32,48,128]{2,1,0:T(8,128)(2,1)S(1)} async-done(((bf16[32,48,128]{2,1,0:T(8,128)(2,1)}), bf16[32,48,128]{2,1,0:T(8,128)(2,1)S(1)}, u32[]{:S(2)}, u32[]{:S(2)}) %all-to-all-start) | async-done | bytes 393248 | tf_op jit(solution)/shard_map/all_to_all | solution.py:452
  36.6 2.3 %attend.2 = (bf16[32,48,128]{2,1,0:T(8,128)(2,1)}, bf16[16,128]{1,0:T(8,128)(2,1)S(1)}) custom-call(s32[2]{0:T(128)S(1)} %pad_add_fusion.ids.refs_0_, s32[24]{0:T(128)S(1)} %select_reduce_fusion.3.table.refs_1_, f32[8,128]{1,0:T(8,128)S(1)} %get-tuple-element.56.refs_2_, f32[8,128]{1,0:T(8,128)S(1)} %get-tuple-element.55.refs_3_, ...), custom_call_target="tpu_custom_call" | custom-call | tf_op jit(solution)/shard_map/attend/pallas_call | solution.py:440
  39.5 7.6 %all-to-all-start.1 = ((bf16[32,48,128]{2,1,0:T(8,128)(2,1)}), bf16[32,48,128]{2,1,0:T(8,128)(2,1)S(1)}, u32[]{:S(2)}, u32[]{:S(2)}) async-start(bf16[32,48,128]{2,1,0:T(8,128)(2,1)} %get-tuple-element.35), calls=%async_computation.1 | async-start | bytes 786432 | tf_op jit(solution)/shard_map/all_to_all | solution.py:452
  47.1 3.2 %collective-permute-start.2 = (bf16[1024,256]{1,0:T(8,128)(2,1)S(1)}, bf16[1024,256]{1,0:T(8,128)(2,1)S(1)}, u32[]{:S(2)}, u32[]{:S(2)}) collective-permute-start(bf16[1024,256]{1,0:T(8,128)(2,1)S(1)} %bitcast.25), channel_id=1, source_target_pairs={{0,1},{1,0},{2,3},{3,2},{4,5},{5,4},{6,7},{7,6},{8,9},{9,8},{10,11... | collective-permute-start | bytes 1572872 | tf_op jit(solution)/shard_map/ppermute | solution.py:456
  50.3 1.5 %collective-permute-done.2.refs_2_ = bf16[1024,256]{1,0:T(8,128)(2,1)S(1)} collective-permute-done((bf16[1024,256]{1,0:T(8,128)(2,1)S(1)}, bf16[1024,256]{1,0:T(8,128)(2,1)S(1)}, u32[]{:S(2)}, u32[]{:S(2)}) %collective-permute-start.2) | collective-permute-done | bytes 524320 | tf_op jit(solution)/shard_map/ppermute | solution.py:456
  52.4 5.5 %all-to-all-done.1.received.gathered_0.gathered = bf16[32,48,128]{2,1,0:T(8,128)(2,1)S(1)} async-done(((bf16[32,48,128]{2,1,0:T(8,128)(2,1)}), bf16[32,48,128]{2,1,0:T(8,128)(2,1)S(1)}, u32[]{:S(2)}, u32[]{:S(2)}) %all-to-all-start.1) | async-done | bytes 393248 | tf_op jit(solution)/shard_map/all_to_all | solution.py:452
  57.9 1.2 output.2
  59.1 10.2 %all-to-all-start.2 = ((bf16[8,96,256]{2,1,0:T(8,128)(2,1)}), bf16[8,96,256]{2,1,0:T(8,128)(2,1)S(1)}, u32[]{:S(2)}, u32[]{:S(2)}) async-start(bf16[8,96,256]{2,1,0:T(8,128)(2,1)} %output.2), calls=%async_computation.2 | async-start | bytes 786432 | tf_op jit(solution)/shard_map/all_to_all | solution.py:452
  69.3 6.8 %collective-permute-start.3 = (bf16[256,1024]{1,0:T(8,128)(2,1)S(1)}, bf16[256,1024]{1,0:T(8,128)(2,1)S(1)}, u32[]{:S(2)}, u32[]{:S(2)}) collective-permute-start(bf16[256,1024]{1,0:T(8,128)(2,1)S(1)} %bitcast.23), channel_id=1, source_target_pairs={{0,1},{1,0},{2,3},{3,2},{4,5},{5,4},{6,7},{7,6},{8,9},{9,8},{10,11... | collective-permute-start | bytes 1572872 | tf_op jit(solution)/shard_map/ppermute | solution.py:456
  76.1 1.5 %collective-permute-done.3.refs_2_ = bf16[256,1024]{1,0:T(8,128)(2,1)S(1)} collective-permute-done((bf16[256,1024]{1,0:T(8,128)(2,1)S(1)}, bf16[256,1024]{1,0:T(8,128)(2,1)S(1)}, u32[]{:S(2)}, u32[]{:S(2)}) %collective-permute-start.3) | collective-permute-done | bytes 524320 | tf_op jit(solution)/shard_map/ppermute | solution.py:456
  78.2 1.9 %all-to-all-done.2.received = bf16[8,96,256]{2,1,0:T(8,128)(2,1)S(1)} async-done(((bf16[8,96,256]{2,1,0:T(8,128)(2,1)}), bf16[8,96,256]{2,1,0:T(8,128)(2,1)S(1)}, u32[]{:S(2)}, u32[]{:S(2)}) %all-to-all-start.2) | async-done | bytes 393248 | tf_op jit(solution)/shard_map/all_to_all | solution.py:452
  80.9 1.2 second.1
  82.2 19.9 %all_to_all.30.refs_4_ = bf16[32,32,128]{2,1,0:T(8,128)(2,1)S(1)} all-to-all(bf16[32,32,128]{2,1,0:T(8,128)(2,1)S(1)} %get-tuple-element.40), channel_id=1, replica_groups=mesh['dp'=32,'tensor'=8,'section'=2] {'dp'}, dimensions={0} | all-to-all | bytes 524288 | tf_op jit(solution)/shard_map/all_to_all | solution.py:452
  102.1 2.0 %attend.3 = (bf16[32,32,128]{2,1,0:T(8,128)(2,1)}, bf16[16,128]{1,0:T(8,128)(2,1)S(1)}) custom-call(s32[2]{0:T(128)S(1)} %pad_add_fusion.ids.refs_0_, s32[24]{0:T(128)S(1)} %copy-done.15, f32[8,128]{1,0:T(8,128)S(1)} %copy-done.13, f32[8,128]{1,0:T(8,128)S(1)} %get-tuple-element.55.refs_3_, bf16[32,32,128]{2,1,0:T(8,128)(2,1)S(1)} %all_to_all.30.refs_4_, ...), custom_call_target="tpu_custom_call" | custom-call | tf_op jit(solution)/shard_map/attend/pallas_call | solution.py:440
  104.1 4.7 %all-to-all-start.4 = ((bf16[32,32,128]{2,1,0:T(8,128)(2,1)}), bf16[32,32,128]{2,1,0:T(8,128)(2,1)S(1)}, u32[]{:S(2)}, u32[]{:S(2)}) async-start(bf16[32,32,128]{2,1,0:T(8,128)(2,1)} %get-tuple-element.41), calls=%async_computation.4 | async-start | bytes 524288 | tf_op jit(solution)/shard_map/all_to_all | solution.py:452
  109.4 9.2 %all-to-all-done.4.received.gathered_1 = bf16[32,32,128]{2,1,0:T(8,128)(2,1)S(1)} async-done(((bf16[32,32,128]{2,1,0:T(8,128)(2,1)}), bf16[32,32,128]{2,1,0:T(8,128)(2,1)S(1)}, u32[]{:S(2)}, u32[]{:S(2)}) %all-to-all-start.4) | async-done | bytes 262176 | tf_op jit(solution)/shard_map/all_to_all | solution.py:452
  118.6 1.2 output.3
  119.8 3.9 %all-to-all-start.5 = ((bf16[8,96,256]{2,1,0:T(8,128)(2,1)}), bf16[8,96,256]{2,1,0:T(8,128)(2,1)S(1)}, u32[]{:S(2)}, u32[]{:S(2)}) async-start(bf16[8,96,256]{2,1,0:T(8,128)(2,1)} %output.3), calls=%async_computation.5 | async-start | bytes 786432 | tf_op jit(solution)/shard_map/all_to_all | solution.py:452
  124.3 6.5 %collective-permute-start.4 = (bf16[16,128]{1,0:T(8,128)(2,1)S(1)}, bf16[16,128]{1,0:T(8,128)(2,1)S(1)}, u32[]{:S(2)}, u32[]{:S(2)}) collective-permute-start(bf16[16,128]{1,0:T(8,128)(2,1)S(1)} %get-tuple-element.45), channel_id=1, source_target_pairs={{0,1},{1,0},{2,3},{3,2},{4,5},{5,4},{6,7},{7,6},{8,9},{9,8},{10,11... | collective-permute-start | bytes 12296 | tf_op jit(solution)/shard_map/ppermute | solution.py:456
  131.6 1.4 caches.1
  133.0 1.4 all-to-all-done.5.received
  135.0 7.5 %collective-permute-start.5 = (bf16[96,256]{1,0:T(8,128)(2,1)S(1)}, bf16[96,256]{1,0:T(8,128)(2,1)S(1)}, u32[]{:S(2)}, u32[]{:S(2)}) collective-permute-start(bf16[96,256]{1,0:T(8,128)(2,1)S(1)} %get-tuple-element.48), channel_id=1, source_target_pairs={{0,1},{1,0},{2,3},{3,2},{4,5},{5,4},{6,7},{7,6},{8,9},{9,8},{10,11... | collective-permute-start | bytes 147464 | tf_op jit(solution)/shard_map/ppermute | solution.py:456
  142.5 0.9 collective-permute-done.5.received
  143.4 1.4 order.1
  (67 shorter events, 11.4 us)
Async XLA Ops:
  0.7 0.7 copy-start.20
  2.3 0.7 copy-start.16
  3.0 1.0 copy-start.2
  4.1 0.8 copy-start.5
  4.9 0.8 copy-start.7
  5.7 0.9 copy-start.9
  6.6 12.2 %copy-start = (bf16[1,6,64,128]{3,2,1,0:T(8,128)(2,1)S(1)}, bf16[1,6,64,128]{3,2,1,0:T(8,128)(2,1)}, u32[]{:S(2)}) copy-start(bf16[1,6,64,128]{3,2,1,0:T(8,128)(2,1)} %param.17) | copy-start | bytes 294916
  6.6 12.2 %copy-start.1 = (bf16[1,6,64,128]{3,2,1,0:T(8,128)(2,1)S(1)}, bf16[1,6,64,128]{3,2,1,0:T(8,128)(2,1)}, u32[]{:S(2)}) copy-start(bf16[1,6,64,128]{3,2,1,0:T(8,128)(2,1)} %param.18) | copy-start | bytes 294916
  8.0 12.4 %copy-start.10 = (bf16[96,256]{1,0:T(8,128)(2,1)}, bf16[96,256]{1,0:T(8,128)(2,1)S(1)}, u32[]{:S(2)}) copy-start(bf16[96,256]{1,0:T(8,128)(2,1)S(1)} %get-tuple-element.37.residual) | copy-start | bytes 147460
  8.0 10.8 %collective-permute-start = (bf16[32,32,128]{2,1,0:T(8,128)(2,1)S(1)}, bf16[32,32,128]{2,1,0:T(8,128)(2,1)S(1)}, u32[]{:S(2)}, u32[]{:S(2)}) collective-permute-start(bf16[32,32,128]{2,1,0:T(8,128)(2,1)S(1)} %get-tuple-element.29), channel_id=1, source_target_pairs={{0,1},{1,0},{2,3},{3,2},{4,5},{5,4},{6,7},{7,6},{8,9},{9,8},{10,11... | collective-permute-start | bytes 786440 | tf_op jit(solution)/shard_map/ppermute | solution.py:456
  17.7 0.7 copy-start.22
  18.6 18.0 %copy-start.14 = (s32[24]{0:T(128)}, s32[24]{0:T(128)S(1)}, u32[]{:S(2)}) copy-start(s32[24]{0:T(128)S(1)} %select_reduce_fusion.3.table.refs_1_) | copy-start | bytes 292
  20.3 4.7 %copy-start.6 = (bf16[1,256,128]{2,1,0:T(8,128)(2,1)S(1)}, bf16[1,256,128]{2,1,0:T(8,128)(2,1)}, u32[]{:S(2)}) copy-start(bf16[1,256,128]{2,1,0:T(8,128)(2,1)} %key_in.1) | copy-start | bytes 196612
  20.4 4.8 %copy-start.8 = (bf16[1,256,128]{2,1,0:T(8,128)(2,1)S(1)}, bf16[1,256,128]{2,1,0:T(8,128)(2,1)}, u32[]{:S(2)}) copy-start(bf16[1,256,128]{2,1,0:T(8,128)(2,1)} %value_in.1) | copy-start | bytes 196612
  20.4 16.2 %all-to-all-start = ((bf16[32,48,128]{2,1,0:T(8,128)(2,1)}), bf16[32,48,128]{2,1,0:T(8,128)(2,1)S(1)}, u32[]{:S(2)}, u32[]{:S(2)}) async-start(bf16[32,48,128]{2,1,0:T(8,128)(2,1)} %join.1), calls=%async_computation | async-start | bytes 786432 | tf_op jit(solution)/shard_map/all_to_all | solution.py:452
  25.7 3.7 %collective-permute-start.1 = (bf16[464,256]{1,0:T(8,128)(2,1)S(1)}, bf16[464,256]{1,0:T(8,128)(2,1)S(1)}, u32[]{:S(2)}, u32[]{:S(2)}) collective-permute-start(bf16[464,256]{1,0:T(8,128)(2,1)S(1)} %pack.1), channel_id=1, source_target_pairs={{0,1},{1,0},{2,3},{3,2},{4,5},{5,4},{6,7},{7,6},{8,9},{9,8},{10,11... | collective-permute-start | bytes 712712 | tf_op jit(solution)/shard_map/ppermute | solution.py:456
  28.4 10.5 %copy-start.12 = (f32[8,128]{1,0:T(8,128)}, f32[8,128]{1,0:T(8,128)S(1)}, u32[]{:S(2)}) copy-start(f32[8,128]{1,0:T(8,128)S(1)} %get-tuple-element.56.refs_2_) | copy-start | bytes 12292
  38.9 8.2 %copy-start.4 = (bf16[1,1024,256]{2,1,0:T(8,128)(2,1)S(1)}, bf16[1,1024,256]{2,1,0:T(8,128)(2,1)}, u32[]{:S(2)}) copy-start(bf16[1,1024,256]{2,1,0:T(8,128)(2,1)} %param.16) | copy-start | bytes 1572868
  39.5 18.4 %all-to-all-start.1 = ((bf16[32,48,128]{2,1,0:T(8,128)(2,1)}), bf16[32,48,128]{2,1,0:T(8,128)(2,1)S(1)}, u32[]{:S(2)}, u32[]{:S(2)}) async-start(bf16[32,48,128]{2,1,0:T(8,128)(2,1)} %get-tuple-element.35), calls=%async_computation.1 | async-start | bytes 786432 | tf_op jit(solution)/shard_map/all_to_all | solution.py:452
  47.1 4.7 %collective-permute-start.2 = (bf16[1024,256]{1,0:T(8,128)(2,1)S(1)}, bf16[1024,256]{1,0:T(8,128)(2,1)S(1)}, u32[]{:S(2)}, u32[]{:S(2)}) collective-permute-start(bf16[1024,256]{1,0:T(8,128)(2,1)S(1)} %bitcast.25), channel_id=1, source_target_pairs={{0,1},{1,0},{2,3},{3,2},{4,5},{5,4},{6,7},{7,6},{8,9},{9,8},{10,11... | collective-permute-start | bytes 1572872 | tf_op jit(solution)/shard_map/ppermute | solution.py:456
  59.1 10.2 %copy-start.3 = (bf16[1,256,1024]{2,1,0:T(8,128)(2,1)S(1)}, bf16[1,256,1024]{2,1,0:T(8,128)(2,1)}, u32[]{:S(2)}) copy-start(bf16[1,256,1024]{2,1,0:T(8,128)(2,1)} %query_in.1) | copy-start | bytes 1572868
  59.1 21.0 %all-to-all-start.2 = ((bf16[8,96,256]{2,1,0:T(8,128)(2,1)}), bf16[8,96,256]{2,1,0:T(8,128)(2,1)S(1)}, u32[]{:S(2)}, u32[]{:S(2)}) async-start(bf16[8,96,256]{2,1,0:T(8,128)(2,1)} %output.2), calls=%async_computation.2 | async-start | bytes 786432 | tf_op jit(solution)/shard_map/all_to_all | solution.py:452
  69.3 8.3 %collective-permute-start.3 = (bf16[256,1024]{1,0:T(8,128)(2,1)S(1)}, bf16[256,1024]{1,0:T(8,128)(2,1)S(1)}, u32[]{:S(2)}, u32[]{:S(2)}) collective-permute-start(bf16[256,1024]{1,0:T(8,128)(2,1)S(1)} %bitcast.23), channel_id=1, source_target_pairs={{0,1},{1,0},{2,3},{3,2},{4,5},{5,4},{6,7},{7,6},{8,9},{9,8},{10,11... | collective-permute-start | bytes 1572872 | tf_op jit(solution)/shard_map/ppermute | solution.py:456
  78.2 1.9 %copy-start.17 = (f32[1,256]{1,0:T(1,128)S(1)}, f32[1,256]{1,0:T(1,128)}, u32[]{:S(2)}) copy-start(f32[1,256]{1,0:T(1,128)} %gain.1) | copy-start | bytes 3076
  80.1 0.8 copy-start.11
  82.1 20.0 %copy-start.13 = (f32[8,128]{1,0:T(8,128)S(1)}, f32[8,128]{1,0:T(8,128)}, u32[]{:S(2)}) copy-start(f32[8,128]{1,0:T(8,128)} %copy-done.12) | copy-start | bytes 12292
  82.1 20.0 %copy-start.15 = (s32[24]{0:T(128)S(1)}, s32[24]{0:T(128)}, u32[]{:S(2)}) copy-start(s32[24]{0:T(128)} %copy-done.14) | copy-start | bytes 292
  104.1 14.5 %all-to-all-start.4 = ((bf16[32,32,128]{2,1,0:T(8,128)(2,1)}), bf16[32,32,128]{2,1,0:T(8,128)(2,1)S(1)}, u32[]{:S(2)}, u32[]{:S(2)}) async-start(bf16[32,32,128]{2,1,0:T(8,128)(2,1)} %get-tuple-element.41), calls=%async_computation.4 | async-start | bytes 524288 | tf_op jit(solution)/shard_map/all_to_all | solution.py:452
  119.8 3.9 %copy-start.19 = (bf16[16,128]{1,0:T(8,128)(2,1)S(1)}, bf16[16,128]{1,0:T(8,128)(2,1)}, u32[]{:S(2)}) copy-start(bf16[16,128]{1,0:T(8,128)(2,1)} %copy-done.18) | copy-start | bytes 12292
  119.8 14.6 %all-to-all-start.5 = ((bf16[8,96,256]{2,1,0:T(8,128)(2,1)}), bf16[8,96,256]{2,1,0:T(8,128)(2,1)S(1)}, u32[]{:S(2)}, u32[]{:S(2)}) async-start(bf16[8,96,256]{2,1,0:T(8,128)(2,1)} %output.3), calls=%async_computation.5 | async-start | bytes 786432 | tf_op jit(solution)/shard_map/all_to_all | solution.py:452
  124.3 7.3 %collective-permute-start.4 = (bf16[16,128]{1,0:T(8,128)(2,1)S(1)}, bf16[16,128]{1,0:T(8,128)(2,1)S(1)}, u32[]{:S(2)}, u32[]{:S(2)}) collective-permute-start(bf16[16,128]{1,0:T(8,128)(2,1)S(1)} %get-tuple-element.45), channel_id=1, source_target_pairs={{0,1},{1,0},{2,3},{3,2},{4,5},{5,4},{6,7},{7,6},{8,9},{9,8},{10,11... | collective-permute-start | bytes 12296 | tf_op jit(solution)/shard_map/ppermute | solution.py:456
  135.0 8.4 %collective-permute-start.5 = (bf16[96,256]{1,0:T(8,128)(2,1)S(1)}, bf16[96,256]{1,0:T(8,128)(2,1)S(1)}, u32[]{:S(2)}, u32[]{:S(2)}) collective-permute-start(bf16[96,256]{1,0:T(8,128)(2,1)S(1)} %get-tuple-element.48), channel_id=1, source_target_pairs={{0,1},{1,0},{2,3},{3,2},{4,5},{5,4},{6,7},{7,6},{8,9},{9,8},{10,11... | collective-permute-start | bytes 147464 | tf_op jit(solution)/shard_map/ppermute | solution.py:456
  (2 other events, 1.3 us)

commit v3 on v2

--- a/solution.py
+++ b/solution.py
@@ -22,7 +22,8 @@
 WIDTH = 256
 MODEL = 8192
 CACHE_ROWS = TRIO * CONTEXT
-GAIN_ROW = CACHE_ROWS + WIDTH
+QUERY = GROUP * HEAD
+ALL_PARTS = PARTS * HEAD
 EPSILON = 1e-06
 ROPE_BASE = 1000000.0
 F32 = jnp.float32
@@ -60,129 +61,100 @@
     return pick(iota((ROWS, ROWS), 0) == new_index)
 
 
-def spread_part(spread, slots, part, product, first=0):
-    for s in range(slots):
-        row = (s // TRIO) * USED + (s % TRIO) * PARTS + part
-        spread[pl.ds(row * N_DP, N_DP), :] = product[s * N_DP : (s + 1) * N_DP]
-
-
-def spread_squares(spread, slots, square):
+def project(rows, weights, spread):
+    by_slot = rows.astype(F32)
+    terms = weights[WIDTH:, :WIDTH].astype(F32)
+    gain = terms[0:1] + terms[1:2] + terms[2:3]
+    scaled = (by_slot * gain).astype(BF16)
+    for pair in range(PARTS // 2):
+        product = dot(scaled, weights[:WIDTH, pair * 2 * HEAD : (pair + 1) * 2 * HEAD])
+        for s in range(TRIO):
+            for side in range(2):
+                row = s * PARTS + 2 * pair + side
+                spread[pl.ds(row * N_DP, N_DP), :] = product[
+                    s * N_DP : (s + 1) * N_DP, side * HEAD : (side + 1) * HEAD
+                ]
+
+
+def spread_squares(rows, spread):
+    by_slot = rows.astype(F32)
+    square = jnp.sum(by_slot * by_slot, axis=1, keepdims=True)
     lane = iota((N_DP, HEAD), 1)
-    for half in range(slots // TRIO):
-        squares = jnp.zeros((N_DP, HEAD), F32)
-        for s in range(TRIO):
-            first = (half * TRIO + s) * N_DP
-            squares = jnp.where(lane == s, square[first : first + N_DP], squares)
-        high = squares.astype(BF16).astype(F32)
-        row = half * USED + TRIO * PARTS
-        spread[pl.ds(row * N_DP, N_DP), :] = high
-        spread[pl.ds((row + 1) * N_DP, N_DP), :] = squares - high
-
-
-def spread_products(spread, slots, scaled, w_query, w_key, w_value):
-    for part in range(0, GROUP, 2):
-        product = dot(scaled, w_query[:, part * HEAD : (part + 2) * HEAD])
-        spread_part(spread, slots, part, product[:, :HEAD])
-        spread_part(spread, slots, part + 1, product[:, HEAD:])
-    spread_part(spread, slots, GROUP, dot(scaled, w_key))
-    spread_part(spread, slots, GROUP + 1, dot(scaled, w_value))
-
-
-def gathered_block(spread, half, replica):
-    return spread[pl.ds(half * USED * N_DP + replica, USED, stride=N_DP), :].astype(BF16)
-
-
-def first_kernel(
-    ids, new_index, hidden_in, gain_in, query_in, key_in, value_in,
-    kept, shipped, residual, to_slots_out,
-    spread, hidden, gain, w_query, w_key, w_value, arrived,
-):
-    pairs = (
-        (hidden_in, hidden),
-        (gain_in, gain),
-        (query_in.at[0], w_query),
-        (key_in.at[0], w_key),
-        (value_in.at[0], w_value),
-    )
-    copies = [pltpu.make_async_copy(src, dst, arrived.at[i]) for i, (src, dst) in enumerate(pairs)]
+    squares = jnp.zeros((N_DP, HEAD), F32)
+    for s in range(TRIO):
+        squares = jnp.where(lane == s, square[s * N_DP : (s + 1) * N_DP], squares)
+    high = squares.astype(BF16).astype(F32)
+    row = TRIO * PARTS
+    spread[pl.ds(row * N_DP, N_DP), :] = high
+    spread[pl.ds((row + 1) * N_DP, N_DP), :] = squares - high
+
+
+def load_kernel(query_in, key_in, value_in, gain_in, weights, gain, arrived):
+    copies = [
+        pltpu.make_async_copy(source, target, arrived.at[i])
+        for i, (source, target) in enumerate(
+            (
+                (gain_in, gain),
+                (query_in.at[0], weights.at[:WIDTH, :QUERY]),
+                (key_in.at[0], weights.at[:WIDTH, QUERY : QUERY + HEAD]),
+                (value_in.at[0], weights.at[:WIDTH, QUERY + HEAD :]),
+            )
+        )
+    ]
     for copy in copies:
         copy.start()
-    row, column = iota((ROWS, ROWS), 0), iota((ROWS, ROWS), 1)
-    by_slot_order = pick(column == (row & (N_DP - 1)) * ROWS_DEV + (row >> 5))
-    to_slots = dot(by_slot_order, to_new_order(new_index[...]), ((1,), (1,))).astype(BF16)
-    to_slots_out[...] = to_slots
     copies[0].wait()
-    by_slot = dot(to_slots, hidden[...])
-
-    @pl.when(ids[SECTION] == 0)
-    def _():
-        residual[...] = by_slot[:HALF_ROWS].astype(BF16)
-
-    @pl.when(ids[SECTION] == 1)
-    def _():
-        residual[...] = by_slot[HALF_ROWS:].astype(BF16)
-
-    for copy in copies[1:]:
-        copy.wait()
-
-    @pl.when(ids[SECTION] == 0)
-    def _():
-        square = jnp.sum(by_slot * by_slot, axis=1, keepdims=True)
-        scaled = (by_slot * gain[...]).astype(BF16)
-        spread_products(spread, ROWS_DEV, scaled, w_query, w_key[...], w_value[...])
-        spread_squares(spread, ROWS_DEV, square)
-        for p in range(N_DP):
-            kept[p] = gathered_block(spread, 0, p)
-            shipped[p] = gathered_block(spread, 1, p)
-
-
-def join_kernel(ids, table, kept, received, keys, values, payload, spread):
-    count = jnp.int32(0)
-    for s in range(ROWS_DEV):
-        leaves = table[DEST + s] != ids[REPLICA]
-
-        @pl.when(leaves)
-        def _():
-            base = pl.multiple_of(count * (PIECES * N_DP), N_DP)
-            spread[pl.ds(base, CONTEXT), :] = keys[s].astype(F32)
-            spread[pl.ds(base + CONTEXT, CONTEXT), :] = values[s].astype(F32)
-
-        count = count + jnp.where(leaves, 1, 0)
-    for p in range(N_DP):
-        payload[p, USED:, :] = spread[pl.ds(p, MOVES * PIECES, stride=N_DP), :].astype(BF16)
-
-    @pl.when(ids[SECTION] == 0)
-    def _():
-        payload[:, :USED, :] = kept[...]
-
-    @pl.when(ids[SECTION] == 1)
-    def _():
-        payload[:, :USED, :] = received[...]
-
-
-def pack_kernel(ids, keys, values, w_key, w_value, gain, packed):
-    other = (1 - ids[SECTION]) * TRIO
-    for s in range(TRIO):
-        packed[s * CONTEXT : (s + 1) * CONTEXT, :HEAD] = keys[other + s]
-        packed[s * CONTEXT : (s + 1) * CONTEXT, HEAD:] = values[other + s]
-    packed[CACHE_ROWS:GAIN_ROW, :HEAD] = w_key[...]
-    packed[CACHE_ROWS:GAIN_ROW, HEAD:] = w_value[...]
     high = gain[...].astype(BF16).astype(F32)
     middle = (gain[...] - high).astype(BF16).astype(F32)
     low = gain[...] - high - middle
     row = iota((16, WIDTH), 0)
     terms = jnp.where(row == 0, high, jnp.where(row == 1, middle, jnp.where(row == 2, low, 0.0)))
-    packed[GAIN_ROW:, :] = terms.astype(BF16)
-
-
-def choose_kernel(layer, ids, local, other, chosen):
-    @pl.when(ids[SECTION] == layer)
+    weights[WIDTH:, :WIDTH] = terms.astype(BF16)
+    weights[WIDTH:, WIDTH:] = jnp.zeros((16, ALL_PARTS - WIDTH), BF16)
+    for copy in copies[1:]:
+        copy.wait()
+
+
+def prepare_kernel(ids, new_index, hidden, residual, to_slots_out):
+    row, column = iota((ROWS, ROWS), 0), iota((ROWS, ROWS), 1)
+    by_slot_order = pick(column == (row & (N_DP - 1)) * ROWS_DEV + (row >> 5))
+    to_slots = dot(by_slot_order, to_new_order(new_index[...]), ((1,), (1,))).astype(BF16)
+    to_slots_out[...] = to_slots
+    by_slot = dot(to_slots, hidden[...]).astype(BF16)
+
+    @pl.when(ids[SECTION] == 0)
     def _():
-        chosen[...] = local[...]
-
-    @pl.when(ids[SECTION] != layer)
+        residual[...] = by_slot[:HALF_ROWS]
+
+    @pl.when(ids[SECTION] == 1)
     def _():
-        chosen[...] = other[...]
+        residual[...] = by_slot[HALF_ROWS:]
+
+
+def first_kernel(ids, table, rows, weights, other, keys, values, payload, spread):
+    count = jnp.int32(0)
+    for s in range(ROWS_DEV):
+        leaves = table[DEST + s] != ids[REPLICA]
+
+        @pl.when(leaves)
+        def _():
+            base = pl.multiple_of(USED * N_DP + count * (PIECES * N_DP), N_DP)
+            spread[pl.ds(base, CONTEXT), :] = keys[s].astype(F32)
+            spread[pl.ds(base + CONTEXT, CONTEXT), :] = values[s].astype(F32)
+
+        count = count + jnp.where(leaves, 1, 0)
+    spread_squares(rows[...], spread)
+    pl.when(ids[SECTION] == 0)(lambda: project(rows[...], weights, spread))
+    pl.when(ids[SECTION] == 1)(lambda: project(rows[...], other, spread))
+    for p in range(N_DP):
+        payload[p] = spread[pl.ds(p, BLOCK, stride=N_DP), :].astype(BF16)
+
+
+def pack_kernel(ids, keys, values, packed):
+    other = (1 - ids[SECTION]) * TRIO
+    for s in range(TRIO):
+        packed[s * CONTEXT : (s + 1) * CONTEXT, :HEAD] = keys[other + s]
+        packed[s * CONTEXT : (s + 1) * CONTEXT, HEAD:] = values[other + s]
 
 
 def forward(route, received, payload, pieces, sorted_pieces):
@@ -203,7 +175,7 @@
     layer, ids, table, cosine, sine, received, keys, values, packed, *refs
 ):
     if layer == 0:
-        route, payload, own, pieces, sorted_pieces = refs
+        route, _, payload, own, pieces, sorted_pieces = refs
         forward(route, received, payload, pieces, sorted_pieces)
     else:
         payload, own = refs
@@ -289,10 +261,10 @@
 
     @pl.when(section != layer)
     def _():
-        attend(packed[:CACHE_ROWS, :HEAD], packed[:CACHE_ROWS, HEAD:])
-
-
-def output_kernel(received, weight, payload, wide, rows):
+        attend(packed[:, :HEAD], packed[:, HEAD:])
+
+
+def output_kernel(layer, ids, received, w_out, w_other, payload, wide, rows):
     for p in range(N_DP):
         wide[pl.ds(p * USED, USED), :] = received[p, :USED, :].astype(F32)
     for s in range(TRIO):
@@ -301,9 +273,13 @@
                 pl.ds(s * 8 + h, N_DP, stride=USED), :
             ].astype(BF16)
 
-    product = dot(rows[...], weight[...]).astype(BF16)
-    for t in range(N_TENSOR):
-        payload[t] = product
+    def write(weight):
+        product = dot(rows[...], weight[...]).astype(BF16)
+        for t in range(N_TENSOR):
+            payload[t] = product
+
+    pl.when(ids[SECTION] == layer)(lambda: write(w_out))
+    pl.when(ids[SECTION] != layer)(lambda: write(w_other))
 
 
 def summed(received, residual):
@@ -313,35 +289,14 @@
     return (residual[...].astype(F32) + total).astype(BF16)
 
 
-def second_kernel(
-    ids, received, residual, gain, query, w_key, w_value, packed, payload, result, spread
-):
+def second_kernel(ids, received, residual, weights, other, payload, result, spread):
     rows = summed(received, residual)
     result[...] = rows
-    by_slot = rows.astype(F32)
-    spread_squares(spread, TRIO, jnp.sum(by_slot * by_slot, axis=1, keepdims=True))
-
-    @pl.when(ids[SECTION] == 1)
-    def _():
-        scaled = (by_slot * gain[...]).astype(BF16)
-        spread_products(spread, TRIO, scaled, query, w_key[...], w_value[...])
-
-    @pl.when(ids[SECTION] == 0)
-    def _():
-        terms = packed[GAIN_ROW:, :].astype(F32)
-        other_gain = terms[0:1] + terms[1:2] + terms[2:3]
-        scaled = (by_slot * other_gain).astype(BF16)
-        spread_products(
-            spread,
-            TRIO,
-            scaled,
-            query,
-            packed[CACHE_ROWS:GAIN_ROW, :HEAD],
-            packed[CACHE_ROWS:GAIN_ROW, HEAD:],
-        )
-
+    spread_squares(rows, spread)
+    pl.when(ids[SECTION] == 1)(lambda: project(rows, weights, spread))
+    pl.when(ids[SECTION] == 0)(lambda: project(rows, other, spread))
     for p in range(N_DP):
-        payload[p] = gathered_block(spread, 0, p)
+        payload[p] = spread[pl.ds(p, USED, stride=N_DP), :].astype(BF16)
 
 
 def last_kernel(ids, received, before, done, result, swapped):
@@ -435,7 +390,7 @@
         count = count + jnp.where(moves, 1, 0)
 
 
-def call(kernel, name, specs, out_shapes, operands, scratch=()):
+def call(kernel, name, specs, out_shapes, operands, scratch=(), limit=8):
     spec_of = {"s": SMEM_SPEC, "v": VMEM_SPEC, "h": HBM_SPEC, "a": pl.BlockSpec(memory_space=pl.ANY)}
     return pl.pallas_call(
         kernel,
@@ -443,7 +398,7 @@
         in_specs=[spec_of[letter] for letter in specs],
         out_specs=jax.tree.map(lambda _: VMEM_SPEC, out_shapes),
         scratch_shapes=list(scratch),
-        compiler_params=pltpu.CompilerParams(vmem_limit_bytes=8 * 1024 * 1024),
+        compiler_params=pltpu.CompilerParams(vmem_limit_bytes=limit * 1024 * 1024),
         name=name,
     )(*operands)
 
@@ -479,16 +434,6 @@
     keys, values = key_cache[0], value_cache[0]
     new_index = (dest_replica * ROWS_DEV + dest_slot)[None, :]
     row = jnp.arange(ROWS, dtype=jnp.int32)
-    leaves = dest_replica != row // ROWS_DEV
-    before = (row[None, :] // ROWS_DEV == row[:, None] // ROWS_DEV) & (row[None, :] < row[:, None])
-    rank = jnp.sum(jnp.where(before & leaves[None, :], 1, 0), 1)
-    before = (dest_replica[None, :] == dest_replica[:, None]) & (
-        dest_slot[None, :] < dest_slot[:, None]
-    )
-    place = jnp.sum(jnp.where(before & leaves[None, :], 1, 0), 1)
-    arrival = jnp.where(leaves, dest_replica * MOVES + place, -1)
-    chosen = arrival[None, :] == jnp.arange(N_DP * MOVES, dtype=jnp.int32)[:, None]
-    route = jnp.sum(jnp.where(chosen, (row // ROWS_DEV * MOVES + rank)[None, :], 0), 1)[None, :]
     entry = jnp.arange(4 * ROWS_DEV, dtype=jnp.int32)[:, None]
     kind = entry // ROWS_DEV
     wanted = me * ROWS_DEV + entry % ROWS_DEV
@@ -505,93 +450,86 @@
     cosine = jnp.cos(angles)
     sine = jnp.sin(angles) * jnp.where(jnp.arange(HEAD) < half, -1.0, 1.0)[None, :]
 
-    kept, shipped, residual, to_slots = call(
+    weights = call(
+        load_kernel,
+        "load",
+        "hhhh",
+        shape(WIDTH + 16, ALL_PARTS),
+        (w_query, w_key, w_value, norm_gain),
+        [pltpu.VMEM((1, WIDTH), F32), pltpu.SemaphoreType.DMA((4,))],
+        8,
+    )
+    other = swap(weights)
+    residual, to_slots = call(
+        prepare_kernel,
+        "prepare",
+        "svv",
+        (shape(HALF_ROWS, WIDTH), shape(ROWS, ROWS)),
+        (ids, new_index, hidden_in),
+    )
+    payload = call(
         first_kernel,
         "first",
-        "svhhhhh",
-        (shape(N_DP, USED, HEAD), shape(N_DP, USED, HEAD), shape(HALF_ROWS, WIDTH), shape(ROWS, ROWS)),
-        (ids, new_index, hidden_in, norm_gain, w_query, w_key, w_value),
-        [
-            pltpu.VMEM((2 * USED * N_DP, HEAD), F32),
-            pltpu.VMEM((ROWS, WIDTH), BF16),
-            pltpu.VMEM((1, WIDTH), F32),
-            pltpu.VMEM((WIDTH, GROUP * HEAD), BF16),
-            pltpu.VMEM((WIDTH, HEAD), BF16),
-            pltpu.VMEM((WIDTH, HEAD), BF16),
-            pltpu.SemaphoreType.DMA((5,)),
-        ],
-    )
-    payload = call(
-        join_kernel,
-        "join",
-        "ssvvvv",
+        "ssvvvvv",
         shape(N_DP, BLOCK, HEAD),
-        (ids, table, kept, swap(shipped), keys, values),
-        [pltpu.VMEM((MOVES * PIECES * N_DP, HEAD), F32)],
+        (ids, table, residual, weights, other, keys, values),
+        [pltpu.VMEM((BLOCK * N_DP, HEAD), F32)],
     )
     first = exchange(payload, "dp")
 
-    late_keys, late_values, late_key, late_value, late_gain, late_query, late_out, _ = (
-        lax.optimization_barrier(
-            (keys, values, w_key[0], w_value[0], norm_gain, w_query[0], w_out[0], payload)
-        )
+    late_keys, late_values, late_out, late_replica, late_slot, _ = lax.optimization_barrier(
+        (keys, values, w_out[0], dest_replica, dest_slot, payload)
     )
     packed = swap(
-        call(
-            pack_kernel,
-            "pack",
-            "svvvvv",
-            shape(GAIN_ROW + 16, WIDTH),
-            (ids, late_keys, late_values, late_key, late_value, late_gain),
-        )
-    )
-
-    def choose(layer, local, other):
-        return call(
-            lambda *refs: choose_kernel(layer, *refs),
-            "choose",
-            "svv",
-            shape(*local.shape),
-            (ids, local, other),
-        )
-
-    def attend(layer, received, *more):
+        call(pack_kernel, "pack", "svv", shape(CACHE_ROWS, WIDTH), (ids, late_keys, late_values))
+    )
+    out_other = swap(late_out)
+    leaves = late_replica != row // ROWS_DEV
+    before = (row[None, :] // ROWS_DEV == row[:, None] // ROWS_DEV) & (row[None, :] < row[:, None])
+    rank = jnp.sum(jnp.where(before & leaves[None, :], 1, 0), 1)
+    before = (late_replica[None, :] == late_replica[:, None]) & (
+        late_slot[None, :] < late_slot[:, None]
+    )
+    place = jnp.sum(jnp.where(before & leaves[None, :], 1, 0), 1)
+    arrival = jnp.where(leaves, late_replica * MOVES + place, -1)
+    chosen = arrival[None, :] == jnp.arange(N_DP * MOVES, dtype=jnp.int32)[:, None]
+    route = jnp.sum(jnp.where(chosen, (row // ROWS_DEV * MOVES + rank)[None, :], 0), 1)[None, :]
+
+    def attend(layer, received, specs="", *more):
         return call(
             lambda *refs: attend_kernel(layer, *refs),
             "attend",
-            "ssvvvvvv" + "v" * len(more),
+            "ssvvvvvv" + specs,
             (shape(N_DP, USED if layer else BLOCK, HEAD), shape(16, HEAD)),
             (ids, table, cosine, sine, received, keys, values, packed, *more),
             [] if layer else [pltpu.VMEM((N_DP * MOVES * PIECES, HEAD), F32)] * 2,
         )
 
-    def output(received, weight):
+    def output(layer, received):
         return call(
-            output_kernel,
+            lambda *refs: output_kernel(layer, *refs),
             "output",
-            "vv",
+            "svvv",
             shape(N_TENSOR, HALF_ROWS, WIDTH),
-            (received, weight),
+            (ids, received, w_out[0], out_other),
             [pltpu.VMEM((N_DP * USED, HEAD), F32), pltpu.VMEM((HALF_ROWS, GROUP * HEAD), BF16)],
         )
 
-    payload, own_0 = attend(0, first, route)
+    payload, own_0 = attend(0, first, "va", route, out_other)
     second = exchange(payload, "dp")
-    out_other = swap(late_out)
-    sums = exchange(output(second, choose(0, late_out, out_other)), "tensor")
-    query = choose(1, late_query, swap(late_query))
+    sums = exchange(output(0, second), "tensor")
     payload, result_0 = call(
         second_kernel,
         "second",
-        "svvvvvvv",
+        "svvvv",
         (shape(N_DP, USED, HEAD), shape(HALF_ROWS, WIDTH)),
-        (ids, sums, residual, late_gain, query, late_key, late_value, packed),
+        (ids, sums, residual, weights, other),
         [pltpu.VMEM((USED * N_DP, HEAD), F32)],
     )
     third = exchange(payload, "dp")
     payload, own_1 = attend(1, third)
     fourth = exchange(payload, "dp")
-    sums = exchange(output(fourth, choose(1, late_out, out_other)), "tensor")
+    sums = exchange(output(1, fourth), "tensor")
     mine, swapped_own = call(
         own_kernel,
         "own",

time: 146 us -> 139 us (0.952)
  blocking collectives: 19.9 us -> 72.9 us
  starting transfers between devices: 66.9 us -> 35.7 us
  waiting for transfers between devices: 31.1 us -> 9.57 us
  local copies, waits for them, and re-layouts: 7.75 us -> 3.49 us
  Pallas kernels: 17.3 us -> 14.7 us
    all_to_all x1 -> x4, blocking collectives: 19.9 us -> 72.9 us  [exchange(): return lax.all_to_all(value, axis, split_axis=0, concat_axis=0, tiled=True)]
    all_to_all x5 -> x2, starting transfers between devices: 30.7 us -> 8.32 us  [exchange(): return lax.all_to_all(value, axis, split_axis=0, concat_axis=0, tiled=True)]
    all_to_all x5 -> x2, waiting for transfers between devices: 25.2 us -> 6.28 us  [exchange(): return lax.all_to_all(value, axis, split_axis=0, concat_axis=0, tiled=True)]
    ppermute x6 -> x5, starting transfers between devices: 36.2 us -> 27.4 us  [swap(): return lax.ppermute(value, 'section', [(0, 1), (1, 0)])]
    unnamed x46 -> x22, local copies, waits for them, and re-layouts: 7.68 us -> 3.42 us
    pallas_call x15 -> x13, Pallas kernels: 17.3 us -> 14.7 us  [call(): pl.pallas_call(kernel, out_shape=out_shapes, in_specs=[spec_of[letter] fo...]
    ppermute x6 -> x5, waiting for transfers between devices: 5.87 us -> 3.29 us  [swap(): return lax.ppermute(value, 'section', [(0, 1), (1, 0)])]
  transfers between devices with their start and end apart: 11 -> 7, of which waited for: 11 -> 6; matrix products, arithmetic and copies ran while one was open for 0% -> 1% of each run, Pallas kernels for 3% -> 3%
where the time goes in v3:
time: 139 us; the launch traced here: 138 us
  blocking collectives  72.9 us (52%)
  starting transfers between devices  35.7 us (26%)
  Pallas kernels  14.7 us (11%)
  waiting for transfers between devices  9.57 us (7%)
  local copies, waits for them, and re-layouts  3.49 us (3%)
    all_to_all x4, blocking collectives, exchange(): return lax.all_to_all(value, axis, split_axis=0, concat_axis=0, tiled=True)  72.9 us
    ppermute x5, starting transfers between devices, swap(): return lax.ppermute(value, 'section', [(0, 1), (1, 0)])  27.4 us
    pallas_call x13, Pallas kernels, call(): pl.pallas_call(kernel, out_shape=out_shapes, in_specs=[spec_of[letter] fo...  14.7 us
    all_to_all x2, starting transfers between devices, exchange(): return lax.all_to_all(value, axis, split_axis=0, concat_axis=0, tiled=True)  8.32 us
    all_to_all x2, waiting for transfers between devices, exchange(): return lax.all_to_all(value, axis, split_axis=0, concat_axis=0, tiled=True)  6.28 us
    unnamed x22, local copies, waits for them, and re-layouts  3.42 us
    ppermute x5, waiting for transfers between devices, swap(): return lax.ppermute(value, 'section', [(0, 1), (1, 0)])  3.29 us
  transfers between devices with their start and end apart: 7, of which 6 were waited for; matrix products, arithmetic and copies ran while one was open for 1% of the time, Pallas kernels for 3%

profile of v3, /device:TPU:1, one launch (start us, length us, event | category | flops | bytes accessed | tf_op | source)
XLA Modules:
  0.0 138.1 jit_solution(8712493273793834292)
XLA Ops:
  0.6 1.0 copy-done.3
  1.7 0.8 copy-done.5
  2.5 0.8 copy-done.6
  3.4 0.7 copy-done.7
  4.2 8.9 %collective-permute-start = (bf16[272,1280]{1,0:T(8,128)(2,1)S(1)}, bf16[272,1280]{1,0:T(8,128)(2,1)S(1)}, u32[]{:S(2)}, u32[]{:S(2)}) collective-permute-start(bf16[272,1280]{1,0:T(8,128)(2,1)S(1)} %load.1.weights), channel_id=1, source_target_pairs={{0,1},{1,0},{2,3},{3,2},{4,5},{5,4},{6,7},{7,6},{8,9},{9,8},{10,11... | collective-permute-start | bytes 2088968 | tf_op jit(solution)/shard_map/ppermute | solution.py:411
  13.6 0.9 prepare.1
  14.9 2.1 %first.1 = bf16[32,48,128]{2,1,0:T(8,128)(2,1)} custom-call(s32[2]{0:T(128)S(1)} %pad_add_fusion.ids.refs_0_, s32[24]{0:T(128)S(1)} %select_reduce_fusion.3.table.refs_1_, bf16[96,256]{1,0:T(8,128)(2,1)S(1)} %get-tuple-element.24.rows.residual, bf16[272,1280]{1,0:T(8,128)(2,1)S(1)} %load.1.weights, bf16[272,1280]{1,0:T(8,128)(2,1)S(1)} %collective-permute-done.other, ...), custom_call_target="tpu_custom_call" | custom-call | tf_op jit(solution)/shard_map/first/pallas_call | solution.py:395
  17.0 4.4 %all-to-all-start = ((bf16[32,48,128]{2,1,0:T(8,128)(2,1)}), bf16[32,48,128]{2,1,0:T(8,128)(2,1)S(1)}, u32[]{:S(2)}, u32[]{:S(2)}) async-start(bf16[32,48,128]{2,1,0:T(8,128)(2,1)} %first.1), calls=%async_computation | async-start | bytes 786432 | tf_op jit(solution)/shard_map/all_to_all | solution.py:407
  21.5 0.6 pack.1
  22.1 2.5 %collective-permute-start.1 = (bf16[192,256]{1,0:T(8,128)(2,1)S(1)}, bf16[192,256]{1,0:T(8,128)(2,1)S(1)}, u32[]{:S(2)}, u32[]{:S(2)}) collective-permute-start(bf16[192,256]{1,0:T(8,128)(2,1)S(1)} %pack.1), channel_id=1, source_target_pairs={{0,1},{1,0},{2,3},{3,2},{4,5},{5,4},{6,7},{7,6},{8,9},{9,8},{10,11... | collective-permute-start | bytes 294920 | tf_op jit(solution)/shard_map/ppermute | solution.py:411
  24.6 1.9 %collective-permute-start.2 = (bf16[1024,256]{1,0:T(8,128)(2,1)S(1)}, bf16[1024,256]{1,0:T(8,128)(2,1)S(1)}, u32[]{:S(2)}, u32[]{:S(2)}) collective-permute-start(bf16[1024,256]{1,0:T(8,128)(2,1)S(1)} %bitcast.20), channel_id=1, source_target_pairs={{0,1},{1,0},{2,3},{3,2},{4,5},{5,4},{6,7},{7,6},{8,9},{9,8},{10,11... | collective-permute-start | bytes 1572872 | tf_op jit(solution)/shard_map/ppermute | solution.py:411
  27.0 1.4 %collective-permute-done.2.refs_9_.refs_3_ = bf16[1024,256]{1,0:T(8,128)(2,1)S(1)} collective-permute-done((bf16[1024,256]{1,0:T(8,128)(2,1)S(1)}, bf16[1024,256]{1,0:T(8,128)(2,1)S(1)}, u32[]{:S(2)}, u32[]{:S(2)}) %collective-permute-start.2) | collective-permute-done | bytes 524320 | tf_op jit(solution)/shard_map/ppermute | solution.py:411
  28.4 4.9 %all-to-all-done.refs_4_ = bf16[32,48,128]{2,1,0:T(8,128)(2,1)S(1)} async-done(((bf16[32,48,128]{2,1,0:T(8,128)(2,1)}), bf16[32,48,128]{2,1,0:T(8,128)(2,1)S(1)}, u32[]{:S(2)}, u32[]{:S(2)}) %all-to-all-start) | async-done | bytes 393248 | tf_op jit(solution)/shard_map/all_to_all | solution.py:407
  33.3 1.6 %attend.2 = (bf16[32,48,128]{2,1,0:T(8,128)(2,1)S(1)}, bf16[16,128]{1,0:T(8,128)(2,1)S(1)}) custom-call(s32[2]{0:T(128)S(1)} %pad_add_fusion.ids.refs_0_, s32[24]{0:T(128)S(1)} %select_reduce_fusion.3.table.refs_1_, f32[8,128]{1,0:T(8,128)S(1)} %get-tuple-element.46.refs_2_, f32[8,128]{1,0:T(8,128)S(1)} %get-tuple-element.45.refs_3_, ...), custom_call_target="tpu_custom_call" | custom-call | tf_op jit(solution)/shard_map/attend/pallas_call | solution.py:395
  34.8 18.2 %all_to_all.30.refs_1_.gathered_0.gathered = bf16[32,48,128]{2,1,0:T(8,128)(2,1)S(1)} all-to-all(bf16[32,48,128]{2,1,0:T(8,128)(2,1)S(1)} %get-tuple-element.30), channel_id=1, replica_groups=mesh['dp'=32,'tensor'=8,'section'=2] {'dp'}, dimensions={0} | all-to-all | bytes 786432 | tf_op jit(solution)/shard_map/all_to_all | solution.py:407
  53.0 1.0 output.2
  54.0 20.8 %all_to_all.31.received = bf16[8,96,256]{2,1,0:T(8,128)(2,1)S(1)} all-to-all(bf16[8,96,256]{2,1,0:T(8,128)(2,1)S(1)} %output.2), channel_id=1, replica_groups=mesh['dp'=32,'tensor'=8,'section'=2] {'tensor'}, dimensions={0} | all-to-all | bytes 786432 | tf_op jit(solution)/shard_map/all_to_all | solution.py:407
  74.8 1.2 second.1
  76.0 19.8 %all_to_all.32.refs_4_ = bf16[32,32,128]{2,1,0:T(8,128)(2,1)S(1)} all-to-all(bf16[32,32,128]{2,1,0:T(8,128)(2,1)S(1)} %get-tuple-element.32), channel_id=1, replica_groups=mesh['dp'=32,'tensor'=8,'section'=2] {'dp'}, dimensions={0} | all-to-all | bytes 524288 | tf_op jit(solution)/shard_map/all_to_all | solution.py:407
  95.8 1.3 attend.3
  97.1 14.1 %all_to_all.33.refs_1_.gathered_1 = bf16[32,32,128]{2,1,0:T(8,128)(2,1)S(1)} all-to-all(bf16[32,32,128]{2,1,0:T(8,128)(2,1)S(1)} %get-tuple-element.33), channel_id=1, replica_groups=mesh['dp'=32,'tensor'=8,'section'=2] {'dp'}, dimensions={0} | all-to-all | bytes 524288 | tf_op jit(solution)/shard_map/all_to_all | solution.py:407
  111.3 1.8 %output.3 = bf16[8,96,256]{2,1,0:T(8,128)(2,1)} custom-call(s32[2]{0:T(128)S(1)} %pad_add_fusion.ids.refs_0_, bf16[32,32,128]{2,1,0:T(8,128)(2,1)S(1)} %all_to_all.33.refs_1_.gathered_1, bf16[1024,256]{1,0:T(8,128)(2,1)S(1)} %bitcast.22, bf16[1024,256]{1,0:T(8,128)(2,1)S(1)} %collective-permute-done.2.refs_9_.refs_3_), custom_call_target="tpu_custom_call" | custom-call | tf_op jit(solution)/shard_map/output/pallas_call | solution.py:395
  113.0 3.9 %all-to-all-start.5 = ((bf16[8,96,256]{2,1,0:T(8,128)(2,1)}), bf16[8,96,256]{2,1,0:T(8,128)(2,1)S(1)}, u32[]{:S(2)}, u32[]{:S(2)}) async-start(bf16[8,96,256]{2,1,0:T(8,128)(2,1)} %output.3), calls=%async_computation.5 | async-start | bytes 786432 | tf_op jit(solution)/shard_map/all_to_all | solution.py:407
  116.9 0.6 own.1
  117.6 6.5 %collective-permute-start.3 = (bf16[16,128]{1,0:T(8,128)(2,1)S(1)}, bf16[16,128]{1,0:T(8,128)(2,1)S(1)}, u32[]{:S(2)}, u32[]{:S(2)}) collective-permute-start(bf16[16,128]{1,0:T(8,128)(2,1)S(1)} %get-tuple-element.37), channel_id=1, source_target_pairs={{0,1},{1,0},{2,3},{3,2},{4,5},{5,4},{6,7},{7,6},{8,9},{9,8},{10,11... | collective-permute-start | bytes 12296 | tf_op jit(solution)/shard_map/ppermute | solution.py:411
  124.1 0.8 collective-permute-done.3.received
  124.9 1.4 %caches.1 = (bf16[6,64,128]{2,1,0:T(8,128)(2,1)}, bf16[6,64,128]{2,1,0:T(8,128)(2,1)}, f32[8,128]{1,0:T(8,128)S(1)}) custom-call(s32[2]{0:T(128)S(1)} %pad_add_fusion.ids.refs_0_, s32[24]{0:T(128)S(1)} %select_reduce_fusion.3.table.refs_1_, bf16[6,64,128]{2,1,0:T(8,128)(2,1)S(1)} %bitcast.14, bf16[6,64,128]{2,1,0:T(8,128)(2,1)S(1)} %bitcast.19, ...), custom_call_target="tpu_custom_call" | custom-call | tf_op jit(solution)/shard_map/caches/pallas_call | solution.py:395
  126.3 1.4 %all-to-all-done.5.received = bf16[8,96,256]{2,1,0:T(8,128)(2,1)S(1)} async-done(((bf16[8,96,256]{2,1,0:T(8,128)(2,1)}), bf16[8,96,256]{2,1,0:T(8,128)(2,1)S(1)}, u32[]{:S(2)}, u32[]{:S(2)}) %all-to-all-start.5) | async-done | bytes 393248 | tf_op jit(solution)/shard_map/all_to_all | solution.py:407
  127.7 0.6 last.1
  128.3 7.5 %collective-permute-start.4 = (bf16[96,256]{1,0:T(8,128)(2,1)S(1)}, bf16[96,256]{1,0:T(8,128)(2,1)S(1)}, u32[]{:S(2)}, u32[]{:S(2)}) collective-permute-start(bf16[96,256]{1,0:T(8,128)(2,1)S(1)} %get-tuple-element.40), channel_id=1, source_target_pairs={{0,1},{1,0},{2,3},{3,2},{4,5},{5,4},{6,7},{7,6},{8,9},{9,8},{10,11... | collective-permute-start | bytes 147464 | tf_op jit(solution)/shard_map/ppermute | solution.py:411
  135.8 0.9 collective-permute-done.4.received
  136.7 1.4 %order.1 = bf16[192,256]{1,0:T(8,128)(2,1)} custom-call(s32[2]{0:T(128)S(1)} %pad_add_fusion.ids.refs_0_, bf16[192,192]{1,0:T(8,128)(2,1)S(1)} %get-tuple-element.23.to_slots, bf16[96,256]{1,0:T(8,128)(2,1)S(1)} %get-tuple-element.31.before.first, bf16[96,256]{1,0:T(8,128)(2,1)S(1)} %get-tuple-element.39.second, ...), custom_call_target="tpu_custom_call" | custom-call | tf_op jit(solution)/shard_map/order/pallas_call | solution.py:395
  (38 shorter events, 1.4 us)
Async XLA Ops:
  0.6 1.0 copy-start.3
  1.7 0.8 copy-start.5
  2.5 0.8 copy-start.6
  3.4 0.7 copy-start.7
  4.0 9.2 %copy-start.8 = (s32[192]{0:T(256)S(1)}, s32[192]{0:T(256)}, u32[]{:S(2)}) copy-start(s32[192]{0:T(256)} %param.20) | copy-start | bytes 2308
  4.0 9.2 %copy-start.9 = (s32[192]{0:T(256)S(1)}, s32[192]{0:T(256)}, u32[]{:S(2)}) copy-start(s32[192]{0:T(256)} %param.21) | copy-start | bytes 2308
  4.0 9.2 %copy-start.10 = (s32[192]{0:T(256)S(1)}, s32[192]{0:T(256)}, u32[]{:S(2)}) copy-start(s32[192]{0:T(256)} %param.19) | copy-start | bytes 2308
  4.0 9.5 %copy-start.4 = (bf16[192,256]{1,0:T(8,128)(2,1)S(1)}, bf16[192,256]{1,0:T(8,128)(2,1)}, u32[]{:S(2)}) copy-start(bf16[192,256]{1,0:T(8,128)(2,1)} %hidden.1) | copy-start | bytes 294916
  4.0 10.8 %copy-start.1 = (bf16[1,6,64,128]{3,2,1,0:T(8,128)(2,1)S(1)}, bf16[1,6,64,128]{3,2,1,0:T(8,128)(2,1)}, u32[]{:S(2)}) copy-start(bf16[1,6,64,128]{3,2,1,0:T(8,128)(2,1)} %param.18) | copy-start | bytes 294916
  4.2 10.7 %copy-start = (bf16[1,6,64,128]{3,2,1,0:T(8,128)(2,1)S(1)}, bf16[1,6,64,128]{3,2,1,0:T(8,128)(2,1)}, u32[]{:S(2)}) copy-start(bf16[1,6,64,128]{3,2,1,0:T(8,128)(2,1)} %param.17) | copy-start | bytes 294916
  4.2 10.7 %collective-permute-start = (bf16[272,1280]{1,0:T(8,128)(2,1)S(1)}, bf16[272,1280]{1,0:T(8,128)(2,1)S(1)}, u32[]{:S(2)}, u32[]{:S(2)}) collective-permute-start(bf16[272,1280]{1,0:T(8,128)(2,1)S(1)} %load.1.weights), channel_id=1, source_target_pairs={{0,1},{1,0},{2,3},{3,2},{4,5},{5,4},{6,7},{7,6},{8,9},{9,8},{10,11... | collective-permute-start | bytes 2088968 | tf_op jit(solution)/shard_map/ppermute | solution.py:411
  17.0 7.6 %copy-start.2 = (bf16[1,1024,256]{2,1,0:T(8,128)(2,1)S(1)}, bf16[1,1024,256]{2,1,0:T(8,128)(2,1)}, u32[]{:S(2)}) copy-start(bf16[1,1024,256]{2,1,0:T(8,128)(2,1)} %param.16) | copy-start | bytes 1572868
  17.0 16.2 %all-to-all-start = ((bf16[32,48,128]{2,1,0:T(8,128)(2,1)}), bf16[32,48,128]{2,1,0:T(8,128)(2,1)S(1)}, u32[]{:S(2)}, u32[]{:S(2)}) async-start(bf16[32,48,128]{2,1,0:T(8,128)(2,1)} %first.1), calls=%async_computation | async-start | bytes 786432 | tf_op jit(solution)/shard_map/all_to_all | solution.py:407
  22.1 4.9 %collective-permute-start.1 = (bf16[192,256]{1,0:T(8,128)(2,1)S(1)}, bf16[192,256]{1,0:T(8,128)(2,1)S(1)}, u32[]{:S(2)}, u32[]{:S(2)}) collective-permute-start(bf16[192,256]{1,0:T(8,128)(2,1)S(1)} %pack.1), channel_id=1, source_target_pairs={{0,1},{1,0},{2,3},{3,2},{4,5},{5,4},{6,7},{7,6},{8,9},{9,8},{10,11... | collective-permute-start | bytes 294920 | tf_op jit(solution)/shard_map/ppermute | solution.py:411
  24.6 3.8 %collective-permute-start.2 = (bf16[1024,256]{1,0:T(8,128)(2,1)S(1)}, bf16[1024,256]{1,0:T(8,128)(2,1)S(1)}, u32[]{:S(2)}, u32[]{:S(2)}) collective-permute-start(bf16[1024,256]{1,0:T(8,128)(2,1)S(1)} %bitcast.20), channel_id=1, source_target_pairs={{0,1},{1,0},{2,3},{3,2},{4,5},{5,4},{6,7},{7,6},{8,9},{9,8},{10,11... | collective-permute-start | bytes 1572872 | tf_op jit(solution)/shard_map/ppermute | solution.py:411
  113.0 14.7 %all-to-all-start.5 = ((bf16[8,96,256]{2,1,0:T(8,128)(2,1)}), bf16[8,96,256]{2,1,0:T(8,128)(2,1)S(1)}, u32[]{:S(2)}, u32[]{:S(2)}) async-start(bf16[8,96,256]{2,1,0:T(8,128)(2,1)} %output.3), calls=%async_computation.5 | async-start | bytes 786432 | tf_op jit(solution)/shard_map/all_to_all | solution.py:407
  117.6 7.3 %collective-permute-start.3 = (bf16[16,128]{1,0:T(8,128)(2,1)S(1)}, bf16[16,128]{1,0:T(8,128)(2,1)S(1)}, u32[]{:S(2)}, u32[]{:S(2)}) collective-permute-start(bf16[16,128]{1,0:T(8,128)(2,1)S(1)} %get-tuple-element.37), channel_id=1, source_target_pairs={{0,1},{1,0},{2,3},{3,2},{4,5},{5,4},{6,7},{7,6},{8,9},{9,8},{10,11... | collective-permute-start | bytes 12296 | tf_op jit(solution)/shard_map/ppermute | solution.py:411
  128.3 8.4 %collective-permute-start.4 = (bf16[96,256]{1,0:T(8,128)(2,1)S(1)}, bf16[96,256]{1,0:T(8,128)(2,1)S(1)}, u32[]{:S(2)}, u32[]{:S(2)}) collective-permute-start(bf16[96,256]{1,0:T(8,128)(2,1)S(1)} %get-tuple-element.40), channel_id=1, source_target_pairs={{0,1},{1,0},{2,3},{3,2},{4,5},{5,4},{6,7},{7,6},{8,9},{9,8},{10,11... | collective-permute-start | bytes 147464 | tf_op jit(solution)/shard_map/ppermute | solution.py:411

commit v4 on v3

--- a/solution.py
+++ b/solution.py
@@ -34,7 +34,6 @@
 
 SMEM_SPEC = pl.BlockSpec(memory_space=pltpu.SMEM)
 VMEM_SPEC = pl.BlockSpec(memory_space=pltpu.VMEM)
-HBM_SPEC = pl.BlockSpec(memory_space=pltpu.HBM)
 
 
 def iota(shape, dim):
@@ -63,7 +62,7 @@
 
 def project(rows, weights, spread):
     by_slot = rows.astype(F32)
-    terms = weights[WIDTH:, :WIDTH].astype(F32)
+    terms = weights[WIDTH:, QUERY:].astype(F32)
     gain = terms[0:1] + terms[1:2] + terms[2:3]
     scaled = (by_slot * gain).astype(BF16)
     for pair in range(PARTS // 2):
@@ -89,30 +88,10 @@
     spread[pl.ds((row + 1) * N_DP, N_DP), :] = squares - high
 
 
-def load_kernel(query_in, key_in, value_in, gain_in, weights, gain, arrived):
-    copies = [
-        pltpu.make_async_copy(source, target, arrived.at[i])
-        for i, (source, target) in enumerate(
-            (
-                (gain_in, gain),
-                (query_in.at[0], weights.at[:WIDTH, :QUERY]),
-                (key_in.at[0], weights.at[:WIDTH, QUERY : QUERY + HEAD]),
-                (value_in.at[0], weights.at[:WIDTH, QUERY + HEAD :]),
-            )
-        )
-    ]
-    for copy in copies:
-        copy.start()
-    copies[0].wait()
-    high = gain[...].astype(BF16).astype(F32)
-    middle = (gain[...] - high).astype(BF16).astype(F32)
-    low = gain[...] - high - middle
-    row = iota((16, WIDTH), 0)
-    terms = jnp.where(row == 0, high, jnp.where(row == 1, middle, jnp.where(row == 2, low, 0.0)))
-    weights[WIDTH:, :WIDTH] = terms.astype(BF16)
-    weights[WIDTH:, WIDTH:] = jnp.zeros((16, ALL_PARTS - WIDTH), BF16)
-    for copy in copies[1:]:
-        copy.wait()
+def load_kernel(query, rest, weights):
+    weights[:WIDTH, :QUERY] = query[0]
+    weights[WIDTH:, :QUERY] = jnp.zeros((16, QUERY), BF16)
+    weights[:, QUERY:] = rest[...]
 
 
 def prepare_kernel(ids, new_index, hidden, residual, to_slots_out):
@@ -299,33 +278,23 @@
         payload[p] = spread[pl.ds(p, USED, stride=N_DP), :].astype(BF16)
 
 
-def last_kernel(ids, received, before, done, result, swapped):
+def last_kernel(
+    ids, table, received, before, gathered_0, gathered_1, own_0, own_1, result, mine, swapped
+):
     rows = summed(received, before)
     result[...] = rows
 
     @pl.when(ids[SECTION] == 0)
     def _():
-        swapped[...] = rows
+        swapped[:HALF_ROWS, :] = rows
 
     @pl.when(ids[SECTION] == 1)
     def _():
-        swapped[...] = before[...]
-
-
-def order_kernel(ids, to_slots, first, second, received, out):
-    def write(low, high):
-        out[...] = (
-            dot(to_slots[:HALF_ROWS, :], low[...], ((0,), (0,)))
-            + dot(to_slots[HALF_ROWS:, :], high[...], ((0,), (0,)))
-        ).astype(BF16)
-
-    pl.when(ids[SECTION] == 0)(lambda: write(first, received))
-    pl.when(ids[SECTION] == 1)(lambda: write(received, second))
-
-
-def own_kernel(ids, table, gathered_0, gathered_1, own_0, own_1, mine, swapped):
+        swapped[:HALF_ROWS, :] = before[...]
+
     me, section = ids[REPLICA], ids[SECTION]
     row = iota((16, HEAD), 0)
+    swapped[HALF_ROWS:, HEAD:] = jnp.zeros((16, WIDTH - HEAD), BF16)
     for layer, (gathered, own) in enumerate(((gathered_0, own_0), (gathered_1, own_1))):
         own_rows = own[...].astype(F32)
         total = jnp.zeros((16, HEAD), F32)
@@ -351,16 +320,26 @@
 
         @pl.when(section != layer)
         def _():
-            swapped[...] = total
-
-
-def cache_kernel(
-    ids, table, keys, values, mine, received, gathered, key_out, value_out, done, pieces
+            swapped[HALF_ROWS:, :HEAD] = total
+
+
+def final_kernel(
+    ids, table, to_slots, first, second, received, keys, values, mine, gathered,
+    out, key_out, value_out, pieces
 ):
+    def write_rows(low, high):
+        out[...] = (
+            dot(to_slots[:HALF_ROWS, :], low, ((0,), (0,)))
+            + dot(to_slots[HALF_ROWS:, :], high, ((0,), (0,)))
+        ).astype(BF16)
+
+    others = received[:HALF_ROWS, :]
+    pl.when(ids[SECTION] == 0)(lambda: write_rows(first[...], others))
+    pl.when(ids[SECTION] == 1)(lambda: write_rows(others, second[...]))
+
     me = ids[REPLICA]
     position = iota((CONTEXT, HEAD), 0)
-    own = mine[...].astype(F32) + received[...].astype(F32)
-    done[...] = own[:8]
+    own = mine[...].astype(F32) + received[HALF_ROWS:, :HEAD].astype(F32)
     for p in range(N_DP):
         pieces[pl.ds(p * MOVES * PIECES, MOVES * PIECES), :] = gathered[p, USED:, :].astype(F32)
     count = jnp.int32(0)
@@ -390,15 +369,15 @@
         count = count + jnp.where(moves, 1, 0)
 
 
-def call(kernel, name, specs, out_shapes, operands, scratch=(), limit=8):
-    spec_of = {"s": SMEM_SPEC, "v": VMEM_SPEC, "h": HBM_SPEC, "a": pl.BlockSpec(memory_space=pl.ANY)}
+def call(kernel, name, specs, out_shapes, operands, scratch=()):
+    spec_of = {"s": SMEM_SPEC, "v": VMEM_SPEC, "a": pl.BlockSpec(memory_space=pl.ANY)}
     return pl.pallas_call(
         kernel,
         out_shape=out_shapes,
         in_specs=[spec_of[letter] for letter in specs],
         out_specs=jax.tree.map(lambda _: VMEM_SPEC, out_shapes),
         scratch_shapes=list(scratch),
-        compiler_params=pltpu.CompilerParams(vmem_limit_bytes=limit * 1024 * 1024),
+        compiler_params=pltpu.CompilerParams(vmem_limit_bytes=8 * 1024 * 1024),
         name=name,
     )(*operands)
 
@@ -450,15 +429,17 @@
     cosine = jnp.cos(angles)
     sine = jnp.sin(angles) * jnp.where(jnp.arange(HEAD) < half, -1.0, 1.0)[None, :]
 
-    weights = call(
-        load_kernel,
-        "load",
-        "hhhh",
-        shape(WIDTH + 16, ALL_PARTS),
-        (w_query, w_key, w_value, norm_gain),
-        [pltpu.VMEM((1, WIDTH), F32), pltpu.SemaphoreType.DMA((4,))],
-        8,
-    )
+    high = norm_gain.astype(BF16).astype(F32)
+    middle = (norm_gain - high).astype(BF16).astype(F32)
+    low = norm_gain - high - middle
+    term = jnp.arange(16, dtype=jnp.int32)[:, None]
+    terms = jnp.where(term == 0, high, jnp.where(term == 1, middle, jnp.where(term == 2, low, 0.0)))
+    rest = (
+        jnp.pad(w_key[0], ((0, 16), (0, HEAD)))
+        + jnp.pad(w_value[0], ((0, 16), (HEAD, 0)))
+        + jnp.pad(terms.astype(BF16), ((WIDTH, 0), (0, 0)))
+    )
+    weights = call(load_kernel, "load", "vv", shape(WIDTH + 16, ALL_PARTS), (w_query, rest))
     other = swap(weights)
     residual, to_slots = call(
         prepare_kernel,
@@ -530,38 +511,20 @@
     payload, own_1 = attend(1, third)
     fourth = exchange(payload, "dp")
     sums = exchange(output(1, fourth), "tensor")
-    mine, swapped_own = call(
-        own_kernel,
-        "own",
-        "ssvvvv",
-        (shape(16, HEAD), shape(16, HEAD)),
-        (ids, table, second, fourth, own_0, own_1),
-    )
-    key_out, value_out, done = call(
-        cache_kernel,
-        "caches",
-        "ssvvvvv",
-        (
-            shape(ROWS_DEV, CONTEXT, HEAD),
-            shape(ROWS_DEV, CONTEXT, HEAD),
-            jax.ShapeDtypeStruct((8, HEAD), F32),
-        ),
-        (ids, table, keys, values, mine, swap(swapped_own), second),
-        [pltpu.VMEM((N_DP * MOVES * PIECES, HEAD), F32)],
-    )
-    result_1, swapped = call(
+    result_1, mine, swapped = call(
         last_kernel,
         "last",
-        "svva",
-        (shape(HALF_ROWS, WIDTH), shape(HALF_ROWS, WIDTH)),
-        (ids, sums, result_0, done),
-    )
-    layer_out = call(
-        order_kernel,
-        "order",
-        "svvvv",
-        shape(ROWS, WIDTH),
-        (ids, to_slots, result_0, result_1, swap(swapped)),
+        "ssvvvvvv",
+        (shape(HALF_ROWS, WIDTH), shape(16, HEAD), shape(HALF_ROWS + 16, WIDTH)),
+        (ids, table, sums, result_0, second, fourth, own_0, own_1),
+    )
+    layer_out, key_out, value_out = call(
+        final_kernel,
+        "final",
+        "ssvvvvvvvv",
+        (shape(ROWS, WIDTH), shape(ROWS_DEV, CONTEXT, HEAD), shape(ROWS_DEV, CONTEXT, HEAD)),
+        (ids, table, to_slots, result_0, result_1, swap(swapped), keys, values, mine, second),
+        [pltpu.VMEM((N_DP * MOVES * PIECES, HEAD), F32)],
     )
     return layer_out[None], key_out[None], value_out[None]
 

time: 139 us -> 137 us (0.986)
  blocking collectives: 72.9 us -> 87.3 us
  starting transfers between devices: 35.7 us -> 24.8 us
  Pallas kernels: 14.7 us -> 12.1 us
  waiting for transfers between devices: 9.57 us -> 7.36 us
  local copies, waits for them, and re-layouts: 3.49 us -> 1.8 us
    all_to_all x4 -> x5, blocking collectives: 72.9 us -> 87.3 us  [exchange(): return lax.all_to_all(value, axis, split_axis=0, concat_axis=0, tiled=True)]
    ppermute x5 -> x4, starting transfers between devices: 27.4 us -> 20.3 us  [swap(): return lax.ppermute(value, 'section', [(0, 1), (1, 0)])]
    all_to_all x2 -> x1, starting transfers between devices: 8.32 us -> 4.43 us  [exchange(): return lax.all_to_all(value, axis, split_axis=0, concat_axis=0, tiled=True)]
    pallas_call x13 -> x11, Pallas kernels: 14.7 us -> 12.1 us  [call(): pl.pallas_call(kernel, out_shape=out_shapes, in_specs=[spec_of[letter] fo...]
    unnamed x22 -> x18, local copies, waits for them, and re-layouts: 3.42 us -> 1.73 us
    all_to_all x2 -> x1, waiting for transfers between devices: 6.28 us -> 4.86 us  [exchange(): return lax.all_to_all(value, axis, split_axis=0, concat_axis=0, tiled=True)]
    ppermute x5 -> x4, waiting for transfers between devices: 3.29 us -> 2.5 us  [swap(): return lax.ppermute(value, 'section', [(0, 1), (1, 0)])]
  transfers between devices with their start and end apart: 7 -> 5, of which waited for: 6 -> 4; matrix products, arithmetic and copies ran while one was open for 1% -> 1% of each run, Pallas kernels for 3% -> 1%
where the time goes in v4:
time: 137 us; the launch traced here: 136 us
  blocking collectives  87.3 us (64%)
  starting transfers between devices  24.8 us (18%)
  Pallas kernels  12.1 us (9%)
  waiting for transfers between devices  7.36 us (5%)
  other arithmetic  1.95 us (1%)
  local copies, waits for them, and re-layouts  1.8 us (1%)
    all_to_all x5, blocking collectives, exchange(): return lax.all_to_all(value, axis, split_axis=0, concat_axis=0, tiled=True)  87.3 us
    ppermute x4, starting transfers between devices, swap(): return lax.ppermute(value, 'section', [(0, 1), (1, 0)])  20.3 us
    pallas_call x11, Pallas kernels, call(): pl.pallas_call(kernel, out_shape=out_shapes, in_specs=[spec_of[letter] fo...  12.1 us
    all_to_all x1, waiting for transfers between devices, exchange(): return lax.all_to_all(value, axis, split_axis=0, concat_axis=0, tiled=True)  4.86 us
    all_to_all x1, starting transfers between devices, exchange(): return lax.all_to_all(value, axis, split_axis=0, concat_axis=0, tiled=True)  4.43 us
  transfers between devices with their start and end apart: 5, of which 4 were waited for; matrix products, arithmetic and copies ran while one was open for 1% of the time, Pallas kernels for 1%

profile of v4, /device:TPU:1, one launch (start us, length us, event | category | flops | bytes accessed | tf_op | source)
XLA Modules:
  0.0 136.2 jit_solution(9259311578566149876)
XLA Ops:
  0.7 0.7 copy-done.7
  1.3 0.1 select_convert_fusion
  1.4 0.9 pad_add_fusion.rest
  2.3 1.0 copy-done.3
  3.4 8.9 %collective-permute-start = (bf16[272,1280]{1,0:T(8,128)(2,1)S(1)}, bf16[272,1280]{1,0:T(8,128)(2,1)S(1)}, u32[]{:S(2)}, u32[]{:S(2)}) collective-permute-start(bf16[272,1280]{1,0:T(8,128)(2,1)S(1)} %load.1.weights), channel_id=1, source_target_pairs={{0,1},{1,0},{2,3},{3,2},{4,5},{5,4},{6,7},{7,6},{8,9},{9,8},{10,11... | collective-permute-start | bytes 2088968 | tf_op jit(solution)/shard_map/ppermute | solution.py:390
  12.5 0.2 select_reduce_fusion.3.table.refs_1_
  12.8 0.9 prepare.1
  13.8 0.1 fusion.2
  13.9 0.2 collective-permute-done.other
  14.1 2.1 %first.1 = bf16[32,48,128]{2,1,0:T(8,128)(2,1)} custom-call(s32[2]{0:T(128)S(1)} %pad_add_fusion.1.ids.refs_0_, s32[24]{0:T(128)S(1)} %select_reduce_fusion.3.table.refs_1_, bf16[96,256]{1,0:T(8,128)(2,1)S(1)} %get-tuple-element.23.rows.residual, bf16[272,1280]{1,0:T(8,128)(2,1)S(1)} %load.1.weights, bf16[272,1280]{1,0:T(8,128)(2,1)S(1)} %collective-permute-done.other, ...), custom_call_target="tpu_custom_call" | custom-call | tf_op jit(solution)/shard_map/first/pallas_call | solution.py:374
  16.3 4.4 %all-to-all-start = ((bf16[32,48,128]{2,1,0:T(8,128)(2,1)}), bf16[32,48,128]{2,1,0:T(8,128)(2,1)S(1)}, u32[]{:S(2)}, u32[]{:S(2)}) async-start(bf16[32,48,128]{2,1,0:T(8,128)(2,1)} %first.1), calls=%async_computation | async-start | bytes 786432 | tf_op jit(solution)/shard_map/all_to_all | solution.py:386
  20.7 0.6 pack.1
  21.3 2.5 %collective-permute-start.1 = (bf16[192,256]{1,0:T(8,128)(2,1)S(1)}, bf16[192,256]{1,0:T(8,128)(2,1)S(1)}, u32[]{:S(2)}, u32[]{:S(2)}) collective-permute-start(bf16[192,256]{1,0:T(8,128)(2,1)S(1)} %pack.1), channel_id=1, source_target_pairs={{0,1},{1,0},{2,3},{3,2},{4,5},{5,4},{6,7},{7,6},{8,9},{9,8},{10,11... | collective-permute-start | bytes 294920 | tf_op jit(solution)/shard_map/ppermute | solution.py:390
  23.8 1.9 %collective-permute-start.2 = (bf16[1024,256]{1,0:T(8,128)(2,1)S(1)}, bf16[1024,256]{1,0:T(8,128)(2,1)S(1)}, u32[]{:S(2)}, u32[]{:S(2)}) collective-permute-start(bf16[1024,256]{1,0:T(8,128)(2,1)S(1)} %bitcast.25), channel_id=1, source_target_pairs={{0,1},{1,0},{2,3},{3,2},{4,5},{5,4},{6,7},{7,6},{8,9},{9,8},{10,11... | collective-permute-start | bytes 1572872 | tf_op jit(solution)/shard_map/ppermute | solution.py:390
  25.8 0.3 select_reduce_fusion.1
  26.1 0.1 select_reduce_fusion.2
  26.2 1.4 %collective-permute-done.2.refs_9_.refs_3_ = bf16[1024,256]{1,0:T(8,128)(2,1)S(1)} collective-permute-done((bf16[1024,256]{1,0:T(8,128)(2,1)S(1)}, bf16[1024,256]{1,0:T(8,128)(2,1)S(1)}, u32[]{:S(2)}, u32[]{:S(2)}) %collective-permute-start.2) | collective-permute-done | bytes 524320 | tf_op jit(solution)/shard_map/ppermute | solution.py:390
  27.6 4.9 %all-to-all-done.refs_4_ = bf16[32,48,128]{2,1,0:T(8,128)(2,1)S(1)} async-done(((bf16[32,48,128]{2,1,0:T(8,128)(2,1)}), bf16[32,48,128]{2,1,0:T(8,128)(2,1)S(1)}, u32[]{:S(2)}, u32[]{:S(2)}) %all-to-all-start) | async-done | bytes 393248 | tf_op jit(solution)/shard_map/all_to_all | solution.py:386
  32.5 1.6 %attend.2 = (bf16[32,48,128]{2,1,0:T(8,128)(2,1)S(1)}, bf16[16,128]{1,0:T(8,128)(2,1)S(1)}) custom-call(s32[2]{0:T(128)S(1)} %pad_add_fusion.1.ids.refs_0_, s32[24]{0:T(128)S(1)} %select_reduce_fusion.3.table.refs_1_, f32[8,128]{1,0:T(8,128)S(1)} %get-tuple-element.47.refs_2_, f32[8,128]{1,0:T(8,128)S(1)} %get-tuple-element.46.refs_3_, ...), custom_call_target="tpu_custom_call" | custom-call | tf_op jit(solution)/shard_map/attend/pallas_call | solution.py:374
  34.1 18.2 %all_to_all.30.refs_1_.gathered_0.gathered = bf16[32,48,128]{2,1,0:T(8,128)(2,1)S(1)} all-to-all(bf16[32,48,128]{2,1,0:T(8,128)(2,1)S(1)} %get-tuple-element.29), channel_id=1, replica_groups=mesh['dp'=32,'tensor'=8,'section'=2] {'dp'}, dimensions={0} | all-to-all | bytes 786432 | tf_op jit(solution)/shard_map/all_to_all | solution.py:386
  52.2 1.0 output.2
  53.3 20.8 %all_to_all.31.received = bf16[8,96,256]{2,1,0:T(8,128)(2,1)S(1)} all-to-all(bf16[8,96,256]{2,1,0:T(8,128)(2,1)S(1)} %output.2), channel_id=1, replica_groups=mesh['dp'=32,'tensor'=8,'section'=2] {'tensor'}, dimensions={0} | all-to-all | bytes 786432 | tf_op jit(solution)/shard_map/all_to_all | solution.py:386
  74.0 1.2 second.1
  75.3 19.8 %all_to_all.32.refs_4_ = bf16[32,32,128]{2,1,0:T(8,128)(2,1)S(1)} all-to-all(bf16[32,32,128]{2,1,0:T(8,128)(2,1)S(1)} %get-tuple-element.31), channel_id=1, replica_groups=mesh['dp'=32,'tensor'=8,'section'=2] {'dp'}, dimensions={0} | all-to-all | bytes 524288 | tf_op jit(solution)/shard_map/all_to_all | solution.py:386
  95.0 1.3 attend.3
  96.4 14.1 %all_to_all.33.refs_1_.gathered_1 = bf16[32,32,128]{2,1,0:T(8,128)(2,1)S(1)} all-to-all(bf16[32,32,128]{2,1,0:T(8,128)(2,1)S(1)} %get-tuple-element.32), channel_id=1, replica_groups=mesh['dp'=32,'tensor'=8,'section'=2] {'dp'}, dimensions={0} | all-to-all | bytes 524288 | tf_op jit(solution)/shard_map/all_to_all | solution.py:386
  110.5 1.0 output.3
  111.5 14.5 %all_to_all.34.received = bf16[8,96,256]{2,1,0:T(8,128)(2,1)S(1)} all-to-all(bf16[8,96,256]{2,1,0:T(8,128)(2,1)S(1)} %output.3), channel_id=1, replica_groups=mesh['dp'=32,'tensor'=8,'section'=2] {'tensor'}, dimensions={0} | all-to-all | bytes 786432 | tf_op jit(solution)/shard_map/all_to_all | solution.py:386
  126.0 0.7 last.1
  126.7 7.0 %collective-permute-start.3 = (bf16[112,256]{1,0:T(8,128)(2,1)S(1)}, bf16[112,256]{1,0:T(8,128)(2,1)S(1)}, u32[]{:S(2)}, u32[]{:S(2)}) collective-permute-start(bf16[112,256]{1,0:T(8,128)(2,1)S(1)} %get-tuple-element.36), channel_id=1, source_target_pairs={{0,1},{1,0},{2,3},{3,2},{4,5},{5,4},{6,7},{7,6},{8,9},{9,8},{10,11... | collective-permute-start | bytes 172040 | tf_op jit(solution)/shard_map/ppermute | solution.py:390
  133.7 0.9 collective-permute-done.3.received
  134.6 1.7 %final.1 = (bf16[192,256]{1,0:T(8,128)(2,1)}, bf16[6,64,128]{2,1,0:T(8,128)(2,1)}, bf16[6,64,128]{2,1,0:T(8,128)(2,1)}) custom-call(s32[2]{0:T(128)S(1)} %pad_add_fusion.1.ids.refs_0_, s32[24]{0:T(128)S(1)} %select_reduce_fusion.3.table.refs_1_, bf16[192,192]{1,0:T(8,128)(2,1)S(1)} %get-tuple-element.22.to_slots, ...), custom_call_target="tpu_custom_call" | custom-call | tf_op jit(solution)/shard_map/final/pallas_call | solution.py:374
  (34 shorter events, 0.4 us)
Async XLA Ops:
  0.6 0.7 copy-start.7
  2.3 1.0 copy-start.3
  3.3 9.1 %copy-start.5 = (s32[192]{0:T(256)S(1)}, s32[192]{0:T(256)}, u32[]{:S(2)}) copy-start(s32[192]{0:T(256)} %param.20) | copy-start | bytes 2308
  3.3 9.1 %copy-start.6 = (s32[192]{0:T(256)S(1)}, s32[192]{0:T(256)}, u32[]{:S(2)}) copy-start(s32[192]{0:T(256)} %param.21) | copy-start | bytes 2308
  3.3 9.1 %copy-start.8 = (s32[192]{0:T(256)S(1)}, s32[192]{0:T(256)}, u32[]{:S(2)}) copy-start(s32[192]{0:T(256)} %param.19) | copy-start | bytes 2308
  3.4 9.4 %copy-start.4 = (bf16[192,256]{1,0:T(8,128)(2,1)S(1)}, bf16[192,256]{1,0:T(8,128)(2,1)}, u32[]{:S(2)}) copy-start(bf16[192,256]{1,0:T(8,128)(2,1)} %hidden.1) | copy-start | bytes 294916
  3.4 10.8 %copy-start.1 = (bf16[1,6,64,128]{3,2,1,0:T(8,128)(2,1)S(1)}, bf16[1,6,64,128]{3,2,1,0:T(8,128)(2,1)}, u32[]{:S(2)}) copy-start(bf16[1,6,64,128]{3,2,1,0:T(8,128)(2,1)} %param.18) | copy-start | bytes 294916
  3.4 10.7 %copy-start = (bf16[1,6,64,128]{3,2,1,0:T(8,128)(2,1)S(1)}, bf16[1,6,64,128]{3,2,1,0:T(8,128)(2,1)}, u32[]{:S(2)}) copy-start(bf16[1,6,64,128]{3,2,1,0:T(8,128)(2,1)} %param.17) | copy-start | bytes 294916
  3.4 10.7 %collective-permute-start = (bf16[272,1280]{1,0:T(8,128)(2,1)S(1)}, bf16[272,1280]{1,0:T(8,128)(2,1)S(1)}, u32[]{:S(2)}, u32[]{:S(2)}) collective-permute-start(bf16[272,1280]{1,0:T(8,128)(2,1)S(1)} %load.1.weights), channel_id=1, source_target_pairs={{0,1},{1,0},{2,3},{3,2},{4,5},{5,4},{6,7},{7,6},{8,9},{9,8},{10,11... | collective-permute-start | bytes 2088968 | tf_op jit(solution)/shard_map/ppermute | solution.py:390
  16.3 7.6 %copy-start.2 = (bf16[1,1024,256]{2,1,0:T(8,128)(2,1)S(1)}, bf16[1,1024,256]{2,1,0:T(8,128)(2,1)}, u32[]{:S(2)}) copy-start(bf16[1,1024,256]{2,1,0:T(8,128)(2,1)} %param.16) | copy-start | bytes 1572868
  16.3 16.2 %all-to-all-start = ((bf16[32,48,128]{2,1,0:T(8,128)(2,1)}), bf16[32,48,128]{2,1,0:T(8,128)(2,1)S(1)}, u32[]{:S(2)}, u32[]{:S(2)}) async-start(bf16[32,48,128]{2,1,0:T(8,128)(2,1)} %first.1), calls=%async_computation | async-start | bytes 786432 | tf_op jit(solution)/shard_map/all_to_all | solution.py:386
  21.3 4.9 %collective-permute-start.1 = (bf16[192,256]{1,0:T(8,128)(2,1)S(1)}, bf16[192,256]{1,0:T(8,128)(2,1)S(1)}, u32[]{:S(2)}, u32[]{:S(2)}) collective-permute-start(bf16[192,256]{1,0:T(8,128)(2,1)S(1)} %pack.1), channel_id=1, source_target_pairs={{0,1},{1,0},{2,3},{3,2},{4,5},{5,4},{6,7},{7,6},{8,9},{9,8},{10,11... | collective-permute-start | bytes 294920 | tf_op jit(solution)/shard_map/ppermute | solution.py:390
  23.8 3.8 %collective-permute-start.2 = (bf16[1024,256]{1,0:T(8,128)(2,1)S(1)}, bf16[1024,256]{1,0:T(8,128)(2,1)S(1)}, u32[]{:S(2)}, u32[]{:S(2)}) collective-permute-start(bf16[1024,256]{1,0:T(8,128)(2,1)S(1)} %bitcast.25), channel_id=1, source_target_pairs={{0,1},{1,0},{2,3},{3,2},{4,5},{5,4},{6,7},{7,6},{8,9},{9,8},{10,11... | collective-permute-start | bytes 1572872 | tf_op jit(solution)/shard_map/ppermute | solution.py:390
  126.7 7.8 %collective-permute-start.3 = (bf16[112,256]{1,0:T(8,128)(2,1)S(1)}, bf16[112,256]{1,0:T(8,128)(2,1)S(1)}, u32[]{:S(2)}, u32[]{:S(2)}) collective-permute-start(bf16[112,256]{1,0:T(8,128)(2,1)S(1)} %get-tuple-element.36), channel_id=1, source_target_pairs={{0,1},{1,0},{2,3},{3,2},{4,5},{5,4},{6,7},{7,6},{8,9},{9,8},{10,11... | collective-permute-start | bytes 172040 | tf_op jit(solution)/shard_map/ppermute | solution.py:390

commit v5 on v4

--- a/solution.py
+++ b/solution.py
@@ -19,6 +19,8 @@
 PARTS = GROUP + 2
 USED = 32
 BLOCK = USED + MOVES * PIECES
+TILE = 8
+TILES = 3 * TILE
 WIDTH = 256
 MODEL = 8192
 CACHE_ROWS = TRIO * CONTEXT
@@ -136,28 +138,38 @@
         packed[s * CONTEXT : (s + 1) * CONTEXT, HEAD:] = values[other + s]
 
 
-def forward(route, received, payload, pieces, sorted_pieces):
+def tile_row(piece):
+    return piece + jnp.where(piece < 14, 2, 4)
+
+
+def forward(route, received, pieces, tiles):
     count = N_DP * MOVES
     for p in range(N_DP):
         pieces[pl.ds(p * MOVES * PIECES, MOVES * PIECES), :] = received[p, USED:, :].astype(F32)
+        tiles[pl.ds(p * TILES, TILE), :] = jnp.zeros((TILE, HEAD), F32)
+        tiles[pl.ds(p * TILES + 2 * TILE, TILE), :] = jnp.zeros((TILE, HEAD), F32)
     to_replica = pick(iota((count, count), 0) == route[...])
     for i in range(PIECES):
         part = pieces[pl.ds(i, count, stride=PIECES), :].astype(BF16)
-        sorted_pieces[pl.ds(i, count, stride=PIECES), :] = dot(to_replica, part, ((0,), (0,)))
-    for p in range(N_DP):
-        payload[p, USED:, :] = sorted_pieces[
-            pl.ds(p * MOVES * PIECES, MOVES * PIECES), :
-        ].astype(BF16)
+        sorted_part = dot(to_replica, part, ((0,), (0,)))
+        for m in range(MOVES):
+            piece = m * PIECES + i
+            row = piece + (2 if piece < 14 else 4)
+            tiles[pl.ds(row, N_DP, stride=TILES), :] = sorted_part[m * N_DP : (m + 1) * N_DP]
 
 
 def attend_kernel(
     layer, ids, table, cosine, sine, received, keys, values, packed, *refs
 ):
     if layer == 0:
-        route, _, payload, own, pieces, sorted_pieces = refs
-        forward(route, received, payload, pieces, sorted_pieces)
+        route, _, payload, own, later, pieces, tiles = refs
+        forward(route, received, pieces, tiles)
+        for p in range(N_DP):
+            later[p] = tiles[pl.ds(p * TILES + TILE, 2 * TILE), :].astype(BF16)
     else:
-        payload, own = refs
+        later, payload, own, tiles = refs
+        for p in range(N_DP):
+            tiles[pl.ds(p * TILE, TILE), :] = later[p].astype(F32)[TILE:]
     section = ids[SECTION]
 
     def attend(all_keys, all_values):
@@ -222,13 +234,17 @@
         )
         own_pair = dot(own_pick, vectors)
         own[...] = own_pair.astype(BF16)
-        block_out = block.astype(BF16)
+        stride = TILES if layer == 0 else TILE
+        for s in range(TRIO):
+            first = table[DEST + section * TRIO + s] * stride
+            tiles[pl.ds(first, 1), :] = own_pair[s : s + 1]
+            tiles[pl.ds(first + 1, 1), :] = own_pair[8 + s : 9 + s]
+        low, high = block[:16].astype(BF16), block[16 : 16 + TILE]
         for p in range(N_DP):
-            payload[p, :USED, :] = block_out
-        for s in range(TRIO):
-            with_own = jnp.where(row == TRIO * 8, own_pair[s : s + 1], block)
-            with_own = jnp.where(row == TRIO * 8 + 1, own_pair[8 + s : 9 + s], with_own)
-            payload[table[DEST + section * TRIO + s], :USED, :] = with_own.astype(BF16)
+            payload[p, :16, :] = low
+            payload[p, 16:, :] = jnp.concatenate(
+                [high, tiles[pl.ds(p * stride, TILE), :]], 0
+            ).astype(BF16)
 
     @pl.when(section == layer)
     def _():
@@ -268,14 +284,15 @@
     return (residual[...].astype(F32) + total).astype(BF16)
 
 
-def second_kernel(ids, received, residual, weights, other, payload, result, spread):
+def second_kernel(ids, received, residual, weights, other, later, payload, result, spread):
     rows = summed(received, residual)
     result[...] = rows
     spread_squares(rows, spread)
     pl.when(ids[SECTION] == 1)(lambda: project(rows, weights, spread))
     pl.when(ids[SECTION] == 0)(lambda: project(rows, other, spread))
     for p in range(N_DP):
-        payload[p] = spread[pl.ds(p, USED, stride=N_DP), :].astype(BF16)
+        payload[p, :USED, :] = spread[pl.ds(p, USED, stride=N_DP), :].astype(BF16)
+        payload[p, USED:, :] = later[p].astype(F32)[:TILE].astype(BF16)
 
 
 def last_kernel(
@@ -304,13 +321,13 @@
             held = source - anchor * ROWS_DEV
             slot = held - section * TRIO
             here = (slot >= 0) & (slot < TRIO)
-            stays = jnp.where(here & (anchor == me), 1.0, 0.0)
-            moves = jnp.where(here & (anchor != me), 1.0, 0.0)
+            stays = here & (anchor == me)
+            moves = here & (anchor != me)
             pair = gathered[anchor, USED - 16 : USED, :].astype(F32)
             kept_key = jnp.sum(jnp.where(row == slot, own_rows, 0.0), axis=0, keepdims=True)
             kept_value = jnp.sum(jnp.where(row == slot + 8, own_rows, 0.0), axis=0, keepdims=True)
-            new_key = kept_key * stays + pair[8:9] * moves
-            new_value = kept_value * stays + pair[9:10] * moves
+            new_key = jnp.where(stays, kept_key, jnp.where(moves, pair[8:9], 0.0))
+            new_value = jnp.where(stays, kept_value, jnp.where(moves, pair[9:10], 0.0))
             total = jnp.where(row == r, new_key, jnp.where(row == r + 8, new_value, total))
         total = total.astype(BF16)
 
@@ -324,7 +341,7 @@
 
 
 def final_kernel(
-    ids, table, to_slots, first, second, received, keys, values, mine, gathered,
+    ids, table, to_slots, first, second, received, keys, values, mine, second_in, third_in, fourth_in,
     out, key_out, value_out, pieces
 ):
     def write_rows(low, high):
@@ -341,7 +358,12 @@
     position = iota((CONTEXT, HEAD), 0)
     own = mine[...].astype(F32) + received[HALF_ROWS:, :HEAD].astype(F32)
     for p in range(N_DP):
-        pieces[pl.ds(p * MOVES * PIECES, MOVES * PIECES), :] = gathered[p, USED:, :].astype(F32)
+        for i, (gathered, first_row) in enumerate(
+            ((second_in, USED - 16), (third_in, USED - TILE), (fourth_in, USED - 16))
+        ):
+            pieces[pl.ds(p * TILES + i * TILE, TILE), :] = gathered[
+                p, first_row : first_row + 16, :
+            ].astype(F32)[TILE:]
     count = jnp.int32(0)
     for r in range(ROWS_DEV):
         source = table[SOURCE + r]
@@ -361,7 +383,7 @@
         @pl.when(moves)
         def _():
             parts = [
-                pieces[pl.ds(count * PIECES + i, N_DP, stride=MOVES * PIECES), :]
+                pieces[pl.ds(tile_row(count * PIECES + i), N_DP, stride=TILES), :]
                 for i in range(PIECES)
             ]
             write(jnp.concatenate(parts[:2], 0), jnp.concatenate(parts[2:], 0))
@@ -429,8 +451,8 @@
     cosine = jnp.cos(angles)
     sine = jnp.sin(angles) * jnp.where(jnp.arange(HEAD) < half, -1.0, 1.0)[None, :]
 
-    high = norm_gain.astype(BF16).astype(F32)
-    middle = (norm_gain - high).astype(BF16).astype(F32)
+    high = lax.reduce_precision(norm_gain, 8, 7)
+    middle = lax.reduce_precision(norm_gain - high, 8, 7)
     low = norm_gain - high - middle
     term = jnp.arange(16, dtype=jnp.int32)[:, None]
     terms = jnp.where(term == 0, high, jnp.where(term == 1, middle, jnp.where(term == 2, low, 0.0)))
@@ -472,7 +494,7 @@
         late_slot[None, :] < late_slot[:, None]
     )
     place = jnp.sum(jnp.where(before & leaves[None, :], 1, 0), 1)
-    arrival = jnp.where(leaves, late_replica * MOVES + place, -1)
+    arrival = jnp.where(leaves, place * N_DP + late_replica, -1)
     chosen = arrival[None, :] == jnp.arange(N_DP * MOVES, dtype=jnp.int32)[:, None]
     route = jnp.sum(jnp.where(chosen, (row // ROWS_DEV * MOVES + rank)[None, :], 0), 1)[None, :]
 
@@ -481,9 +503,15 @@
             lambda *refs: attend_kernel(layer, *refs),
             "attend",
             "ssvvvvvv" + specs,
-            (shape(N_DP, USED if layer else BLOCK, HEAD), shape(16, HEAD)),
+            (shape(N_DP, USED, HEAD), shape(16, HEAD))
+            + (() if layer else (shape(N_DP, 2 * TILE, HEAD),)),
             (ids, table, cosine, sine, received, keys, values, packed, *more),
-            [] if layer else [pltpu.VMEM((N_DP * MOVES * PIECES, HEAD), F32)] * 2,
+            [pltpu.VMEM((N_DP * TILE, HEAD), F32)]
+            if layer
+            else [
+                pltpu.VMEM((N_DP * MOVES * PIECES, HEAD), F32),
+                pltpu.VMEM((N_DP * TILES, HEAD), F32),
+            ],
         )
 
     def output(layer, received):
@@ -496,19 +524,19 @@
             [pltpu.VMEM((N_DP * USED, HEAD), F32), pltpu.VMEM((HALF_ROWS, GROUP * HEAD), BF16)],
         )
 
-    payload, own_0 = attend(0, first, "va", route, out_other)
+    payload, own_0, later = attend(0, first, "va", route, out_other)
     second = exchange(payload, "dp")
     sums = exchange(output(0, second), "tensor")
     payload, result_0 = call(
         second_kernel,
         "second",
-        "svvvv",
-        (shape(N_DP, USED, HEAD), shape(HALF_ROWS, WIDTH)),
-        (ids, sums, residual, weights, other),
+        "svvvvv",
+        (shape(N_DP, USED + TILE, HEAD), shape(HALF_ROWS, WIDTH)),
+        (ids, sums, residual, weights, other, later),
         [pltpu.VMEM((USED * N_DP, HEAD), F32)],
     )
     third = exchange(payload, "dp")
-    payload, own_1 = attend(1, third)
+    payload, own_1 = attend(1, third, "v", later)
     fourth = exchange(payload, "dp")
     sums = exchange(output(1, fourth), "tensor")
     result_1, mine, swapped = call(
@@ -521,10 +549,11 @@
     layer_out, key_out, value_out = call(
         final_kernel,
         "final",
-        "ssvvvvvvvv",
+        "ssvvvvvvvvvv",
         (shape(ROWS, WIDTH), shape(ROWS_DEV, CONTEXT, HEAD), shape(ROWS_DEV, CONTEXT, HEAD)),
-        (ids, table, to_slots, result_0, result_1, swap(swapped), keys, values, mine, second),
-        [pltpu.VMEM((N_DP * MOVES * PIECES, HEAD), F32)],
+        (ids, table, to_slots, result_0, result_1, swap(swapped), keys, values, mine,
+         second, third, fourth),
+        [pltpu.VMEM((N_DP * TILES, HEAD), F32)],
     )
     return layer_out[None], key_out[None], value_out[None]
 

time: 137 us -> 136 us (level)
  blocking collectives: 87.3 us -> 85.4 us
    all_to_all x5, blocking collectives: 87.3 us -> 85.4 us  [exchange(): return lax.all_to_all(value, axis, split_axis=0, concat_axis=0, tiled=True)]
where the time goes in v5:
time: 136 us; the launch traced here: 135 us
  blocking collectives  85.4 us (63%)
  starting transfers between devices  25.4 us (19%)
  Pallas kernels  12.2 us (9%)
  waiting for transfers between devices  7.36 us (5%)
  other arithmetic  1.95 us (1%)
  local copies, waits for them, and re-layouts  1.8 us (1%)
    all_to_all x5, blocking collectives, exchange(): return lax.all_to_all(value, axis, split_axis=0, concat_axis=0, tiled=True)  85.4 us
    ppermute x4, starting transfers between devices, swap(): return lax.ppermute(value, 'section', [(0, 1), (1, 0)])  21 us
    pallas_call x11, Pallas kernels, call(): pl.pallas_call(kernel, out_shape=out_shapes, in_specs=[spec_of[letter] fo...  12.2 us
    all_to_all x1, waiting for transfers between devices, exchange(): return lax.all_to_all(value, axis, split_axis=0, concat_axis=0, tiled=True)  4.86 us
    all_to_all x1, starting transfers between devices, exchange(): return lax.all_to_all(value, axis, split_axis=0, concat_axis=0, tiled=True)  4.43 us
  transfers between devices with their start and end apart: 5, of which 4 were waited for; matrix products, arithmetic and copies ran while one was open for 1% of the time, Pallas kernels for 1%

profile of v5, /device:TPU:1, one launch (start us, length us, event | category | flops | bytes accessed | tf_op | source)
XLA Modules:
  0.0 135.0 jit_solution(1897850232253226188)
XLA Ops:
  0.7 0.7 copy-done.7
  1.3 0.1 select_convert_fusion
  1.4 0.9 pad_add_fusion.rest
  2.3 1.0 copy-done.3
  3.4 8.9 %collective-permute-start = (bf16[272,1280]{1,0:T(8,128)(2,1)S(1)}, bf16[272,1280]{1,0:T(8,128)(2,1)S(1)}, u32[]{:S(2)}, u32[]{:S(2)}) collective-permute-start(bf16[272,1280]{1,0:T(8,128)(2,1)S(1)} %load.1.weights), channel_id=1, source_target_pairs={{0,1},{1,0},{2,3},{3,2},{4,5},{5,4},{6,7},{7,6},{8,9},{9,8},{10,11... | collective-permute-start | bytes 2088968 | tf_op jit(solution)/shard_map/ppermute | solution.py:412
  12.5 0.2 select_reduce_fusion.3.table.refs_1_
  12.8 0.9 prepare.1
  13.8 0.1 fusion.2
  13.9 0.2 collective-permute-done.other
  14.1 2.1 %first.1 = bf16[32,48,128]{2,1,0:T(8,128)(2,1)} custom-call(s32[2]{0:T(128)S(1)} %pad_add_fusion.1.ids.refs_0_, s32[24]{0:T(128)S(1)} %select_reduce_fusion.3.table.refs_1_, bf16[96,256]{1,0:T(8,128)(2,1)S(1)} %get-tuple-element.24.rows.residual, bf16[272,1280]{1,0:T(8,128)(2,1)S(1)} %load.1.weights, bf16[272,1280]{1,0:T(8,128)(2,1)S(1)} %collective-permute-done.other, ...), custom_call_target="tpu_custom_call" | custom-call | tf_op jit(solution)/shard_map/first/pallas_call | solution.py:396
  16.3 4.4 %all-to-all-start = ((bf16[32,48,128]{2,1,0:T(8,128)(2,1)}), bf16[32,48,128]{2,1,0:T(8,128)(2,1)S(1)}, u32[]{:S(2)}, u32[]{:S(2)}) async-start(bf16[32,48,128]{2,1,0:T(8,128)(2,1)} %first.1), calls=%async_computation | async-start | bytes 786432 | tf_op jit(solution)/shard_map/all_to_all | solution.py:408
  20.7 0.6 pack.1
  21.3 2.5 %collective-permute-start.1 = (bf16[192,256]{1,0:T(8,128)(2,1)S(1)}, bf16[192,256]{1,0:T(8,128)(2,1)S(1)}, u32[]{:S(2)}, u32[]{:S(2)}) collective-permute-start(bf16[192,256]{1,0:T(8,128)(2,1)S(1)} %pack.1), channel_id=1, source_target_pairs={{0,1},{1,0},{2,3},{3,2},{4,5},{5,4},{6,7},{7,6},{8,9},{9,8},{10,11... | collective-permute-start | bytes 294920 | tf_op jit(solution)/shard_map/ppermute | solution.py:412
  23.8 1.9 %collective-permute-start.2 = (bf16[1024,256]{1,0:T(8,128)(2,1)S(1)}, bf16[1024,256]{1,0:T(8,128)(2,1)S(1)}, u32[]{:S(2)}, u32[]{:S(2)}) collective-permute-start(bf16[1024,256]{1,0:T(8,128)(2,1)S(1)} %bitcast.25), channel_id=1, source_target_pairs={{0,1},{1,0},{2,3},{3,2},{4,5},{5,4},{6,7},{7,6},{8,9},{9,8},{10,11... | collective-permute-start | bytes 1572872 | tf_op jit(solution)/shard_map/ppermute | solution.py:412
  25.8 0.3 select_reduce_fusion.1
  26.1 0.1 select_reduce_fusion.2
  26.2 1.4 %collective-permute-done.2.refs_9_.refs_3_ = bf16[1024,256]{1,0:T(8,128)(2,1)S(1)} collective-permute-done((bf16[1024,256]{1,0:T(8,128)(2,1)S(1)}, bf16[1024,256]{1,0:T(8,128)(2,1)S(1)}, u32[]{:S(2)}, u32[]{:S(2)}) %collective-permute-start.2) | collective-permute-done | bytes 524320 | tf_op jit(solution)/shard_map/ppermute | solution.py:412
  27.7 4.9 %all-to-all-done.refs_4_ = bf16[32,48,128]{2,1,0:T(8,128)(2,1)S(1)} async-done(((bf16[32,48,128]{2,1,0:T(8,128)(2,1)}), bf16[32,48,128]{2,1,0:T(8,128)(2,1)S(1)}, u32[]{:S(2)}, u32[]{:S(2)}) %all-to-all-start) | async-done | bytes 393248 | tf_op jit(solution)/shard_map/all_to_all | solution.py:408
  32.5 1.6 %attend.2 = (bf16[32,32,128]{2,1,0:T(8,128)(2,1)S(1)}, bf16[16,128]{1,0:T(8,128)(2,1)S(1)}, bf16[32,16,128]{2,1,0:T(8,128)(2,1)S(1)}) custom-call(s32[2]{0:T(128)S(1)} %pad_add_fusion.1.ids.refs_0_, s32[24]{0:T(128)S(1)} %select_reduce_fusion.3.table.refs_1_, f32[8,128]{1,0:T(8,128)S(1)} %get-tuple-element.49.refs_2_, ...), custom_call_target="tpu_custom_call" | custom-call | tf_op jit(solution)/shard_map/attend/pallas_call | solution.py:396
  34.1 17.0 %all_to_all.30.refs_1_.gathered_0.second_in = bf16[32,32,128]{2,1,0:T(8,128)(2,1)S(1)} all-to-all(bf16[32,32,128]{2,1,0:T(8,128)(2,1)S(1)} %get-tuple-element.30), channel_id=1, replica_groups=mesh['dp'=32,'tensor'=8,'section'=2] {'dp'}, dimensions={0} | all-to-all | bytes 524288 | tf_op jit(solution)/shard_map/all_to_all | solution.py:408
  51.1 1.0 output.2
  52.1 20.6 %all_to_all.31.received = bf16[8,96,256]{2,1,0:T(8,128)(2,1)S(1)} all-to-all(bf16[8,96,256]{2,1,0:T(8,128)(2,1)S(1)} %output.2), channel_id=1, replica_groups=mesh['dp'=32,'tensor'=8,'section'=2] {'tensor'}, dimensions={0} | all-to-all | bytes 786432 | tf_op jit(solution)/shard_map/all_to_all | solution.py:408
  72.7 1.2 second.1
  73.9 16.7 %all_to_all.32.refs_4_.third_in = bf16[32,40,128]{2,1,0:T(8,128)(2,1)S(1)} all-to-all(bf16[32,40,128]{2,1,0:T(8,128)(2,1)S(1)} %get-tuple-element.33), channel_id=1, replica_groups=mesh['dp'=32,'tensor'=8,'section'=2] {'dp'}, dimensions={0} | all-to-all | bytes 655360 | tf_op jit(solution)/shard_map/all_to_all | solution.py:408
  90.6 1.3 attend.3
  91.9 14.4 %all_to_all.33.refs_1_.gathered_1.fourth_in = bf16[32,32,128]{2,1,0:T(8,128)(2,1)S(1)} all-to-all(bf16[32,32,128]{2,1,0:T(8,128)(2,1)S(1)} %get-tuple-element.34), channel_id=1, replica_groups=mesh['dp'=32,'tensor'=8,'section'=2] {'dp'}, dimensions={0} | all-to-all | bytes 524288 | tf_op jit(solution)/shard_map/all_to_all | solution.py:408
  106.3 1.0 output.3
  107.3 16.8 %all_to_all.34.received = bf16[8,96,256]{2,1,0:T(8,128)(2,1)S(1)} all-to-all(bf16[8,96,256]{2,1,0:T(8,128)(2,1)S(1)} %output.3), channel_id=1, replica_groups=mesh['dp'=32,'tensor'=8,'section'=2] {'tensor'}, dimensions={0} | all-to-all | bytes 786432 | tf_op jit(solution)/shard_map/all_to_all | solution.py:408
  124.1 0.7 last.1
  124.8 7.6 %collective-permute-start.3 = (bf16[112,256]{1,0:T(8,128)(2,1)S(1)}, bf16[112,256]{1,0:T(8,128)(2,1)S(1)}, u32[]{:S(2)}, u32[]{:S(2)}) collective-permute-start(bf16[112,256]{1,0:T(8,128)(2,1)S(1)} %get-tuple-element.38), channel_id=1, source_target_pairs={{0,1},{1,0},{2,3},{3,2},{4,5},{5,4},{6,7},{7,6},{8,9},{9,8},{10,11... | collective-permute-start | bytes 172040 | tf_op jit(solution)/shard_map/ppermute | solution.py:412
  132.4 0.9 collective-permute-done.3.received
  133.3 1.7 %final.1 = (bf16[192,256]{1,0:T(8,128)(2,1)}, bf16[6,64,128]{2,1,0:T(8,128)(2,1)}, bf16[6,64,128]{2,1,0:T(8,128)(2,1)}) custom-call(s32[2]{0:T(128)S(1)} %pad_add_fusion.1.ids.refs_0_, s32[24]{0:T(128)S(1)} %select_reduce_fusion.3.table.refs_1_, bf16[192,192]{1,0:T(8,128)(2,1)S(1)} %get-tuple-element.23.to_slots, ...), custom_call_target="tpu_custom_call" | custom-call | tf_op jit(solution)/shard_map/final/pallas_call | solution.py:396
  (34 shorter events, 0.4 us)
Async XLA Ops:
  0.6 0.7 copy-start.7
  2.3 1.0 copy-start.3
  3.3 9.1 %copy-start.5 = (s32[192]{0:T(256)S(1)}, s32[192]{0:T(256)}, u32[]{:S(2)}) copy-start(s32[192]{0:T(256)} %param.20) | copy-start | bytes 2308
  3.3 9.1 %copy-start.6 = (s32[192]{0:T(256)S(1)}, s32[192]{0:T(256)}, u32[]{:S(2)}) copy-start(s32[192]{0:T(256)} %param.21) | copy-start | bytes 2308
  3.4 9.1 %copy-start.8 = (s32[192]{0:T(256)S(1)}, s32[192]{0:T(256)}, u32[]{:S(2)}) copy-start(s32[192]{0:T(256)} %param.19) | copy-start | bytes 2308
  3.4 9.4 %copy-start.4 = (bf16[192,256]{1,0:T(8,128)(2,1)S(1)}, bf16[192,256]{1,0:T(8,128)(2,1)}, u32[]{:S(2)}) copy-start(bf16[192,256]{1,0:T(8,128)(2,1)} %hidden.1) | copy-start | bytes 294916
  3.4 10.8 %copy-start.1 = (bf16[1,6,64,128]{3,2,1,0:T(8,128)(2,1)S(1)}, bf16[1,6,64,128]{3,2,1,0:T(8,128)(2,1)}, u32[]{:S(2)}) copy-start(bf16[1,6,64,128]{3,2,1,0:T(8,128)(2,1)} %param.18) | copy-start | bytes 294916
  3.4 10.7 %copy-start = (bf16[1,6,64,128]{3,2,1,0:T(8,128)(2,1)S(1)}, bf16[1,6,64,128]{3,2,1,0:T(8,128)(2,1)}, u32[]{:S(2)}) copy-start(bf16[1,6,64,128]{3,2,1,0:T(8,128)(2,1)} %param.17) | copy-start | bytes 294916
  3.4 10.7 %collective-permute-start = (bf16[272,1280]{1,0:T(8,128)(2,1)S(1)}, bf16[272,1280]{1,0:T(8,128)(2,1)S(1)}, u32[]{:S(2)}, u32[]{:S(2)}) collective-permute-start(bf16[272,1280]{1,0:T(8,128)(2,1)S(1)} %load.1.weights), channel_id=1, source_target_pairs={{0,1},{1,0},{2,3},{3,2},{4,5},{5,4},{6,7},{7,6},{8,9},{9,8},{10,11... | collective-permute-start | bytes 2088968 | tf_op jit(solution)/shard_map/ppermute | solution.py:412
  16.3 7.6 %copy-start.2 = (bf16[1,1024,256]{2,1,0:T(8,128)(2,1)S(1)}, bf16[1,1024,256]{2,1,0:T(8,128)(2,1)}, u32[]{:S(2)}) copy-start(bf16[1,1024,256]{2,1,0:T(8,128)(2,1)} %param.16) | copy-start | bytes 1572868
  16.3 16.2 %all-to-all-start = ((bf16[32,48,128]{2,1,0:T(8,128)(2,1)}), bf16[32,48,128]{2,1,0:T(8,128)(2,1)S(1)}, u32[]{:S(2)}, u32[]{:S(2)}) async-start(bf16[32,48,128]{2,1,0:T(8,128)(2,1)} %first.1), calls=%async_computation | async-start | bytes 786432 | tf_op jit(solution)/shard_map/all_to_all | solution.py:408
  21.3 4.9 %collective-permute-start.1 = (bf16[192,256]{1,0:T(8,128)(2,1)S(1)}, bf16[192,256]{1,0:T(8,128)(2,1)S(1)}, u32[]{:S(2)}, u32[]{:S(2)}) collective-permute-start(bf16[192,256]{1,0:T(8,128)(2,1)S(1)} %pack.1), channel_id=1, source_target_pairs={{0,1},{1,0},{2,3},{3,2},{4,5},{5,4},{6,7},{7,6},{8,9},{9,8},{10,11... | collective-permute-start | bytes 294920 | tf_op jit(solution)/shard_map/ppermute | solution.py:412
  23.8 3.8 %collective-permute-start.2 = (bf16[1024,256]{1,0:T(8,128)(2,1)S(1)}, bf16[1024,256]{1,0:T(8,128)(2,1)S(1)}, u32[]{:S(2)}, u32[]{:S(2)}) collective-permute-start(bf16[1024,256]{1,0:T(8,128)(2,1)S(1)} %bitcast.25), channel_id=1, source_target_pairs={{0,1},{1,0},{2,3},{3,2},{4,5},{5,4},{6,7},{7,6},{8,9},{9,8},{10,11... | collective-permute-start | bytes 1572872 | tf_op jit(solution)/shard_map/ppermute | solution.py:412
  124.8 8.5 %collective-permute-start.3 = (bf16[112,256]{1,0:T(8,128)(2,1)S(1)}, bf16[112,256]{1,0:T(8,128)(2,1)S(1)}, u32[]{:S(2)}, u32[]{:S(2)}) collective-permute-start(bf16[112,256]{1,0:T(8,128)(2,1)S(1)} %get-tuple-element.38), channel_id=1, source_target_pairs={{0,1},{1,0},{2,3},{3,2},{4,5},{5,4},{6,7},{7,6},{8,9},{9,8},{10,11... | collective-permute-start | bytes 172040 | tf_op jit(solution)/shard_map/ppermute | solution.py:412

commit v6 on v5

--- a/solution.py
+++ b/solution.py
@@ -26,6 +26,7 @@
 CACHE_ROWS = TRIO * CONTEXT
 QUERY = GROUP * HEAD
 ALL_PARTS = PARTS * HEAD
+PACKED = ALL_PARTS + 2 * HEAD
 EPSILON = 1e-06
 ROPE_BASE = 1000000.0
 F32 = jnp.float32
@@ -64,7 +65,7 @@
 
 def project(rows, weights, spread):
     by_slot = rows.astype(F32)
-    terms = weights[WIDTH:, QUERY:].astype(F32)
+    terms = weights[WIDTH:, QUERY:ALL_PARTS].astype(F32)
     gain = terms[0:1] + terms[1:2] + terms[2:3]
     scaled = (by_slot * gain).astype(BF16)
     for pair in range(PARTS // 2):
@@ -90,10 +91,17 @@
     spread[pl.ds((row + 1) * N_DP, N_DP), :] = squares - high
 
 
-def load_kernel(query, rest, weights):
+def load_kernel(query, rest, gain, weights):
     weights[:WIDTH, :QUERY] = query[0]
     weights[WIDTH:, :QUERY] = jnp.zeros((16, QUERY), BF16)
-    weights[:, QUERY:] = rest[...]
+    weights[:WIDTH, QUERY:] = rest[...]
+    high = gain[...].astype(BF16).astype(F32)
+    middle = (gain[...] - high).astype(BF16).astype(F32)
+    low = gain[...] - high - middle
+    row = iota((16, WIDTH), 0)
+    terms = jnp.where(row == 0, high, jnp.where(row == 1, middle, jnp.where(row == 2, low, 0.0)))
+    weights[WIDTH:, QUERY:ALL_PARTS] = terms.astype(BF16)
+    weights[WIDTH:, ALL_PARTS:] = jnp.zeros((16, 2 * HEAD), BF16)
 
 
 def prepare_kernel(ids, new_index, hidden, residual, to_slots_out):
@@ -129,13 +137,6 @@
     pl.when(ids[SECTION] == 1)(lambda: project(rows[...], other, spread))
     for p in range(N_DP):
         payload[p] = spread[pl.ds(p, BLOCK, stride=N_DP), :].astype(BF16)
-
-
-def pack_kernel(ids, keys, values, packed):
-    other = (1 - ids[SECTION]) * TRIO
-    for s in range(TRIO):
-        packed[s * CONTEXT : (s + 1) * CONTEXT, :HEAD] = keys[other + s]
-        packed[s * CONTEXT : (s + 1) * CONTEXT, HEAD:] = values[other + s]
 
 
 def tile_row(piece):
@@ -159,7 +160,7 @@
 
 
 def attend_kernel(
-    layer, ids, table, cosine, sine, received, keys, values, packed, *refs
+    layer, ids, table, cosine, sine, received, keys, values, other, *refs
 ):
     if layer == 0:
         route, _, payload, own, later, pieces, tiles = refs
@@ -256,7 +257,7 @@
 
     @pl.when(section != layer)
     def _():
-        attend(packed[:, :HEAD], packed[:, HEAD:])
+        attend(other[:CACHE_ROWS, ALL_PARTS : ALL_PARTS + HEAD], other[:CACHE_ROWS, ALL_PARTS + HEAD :])
 
 
 def output_kernel(layer, ids, received, w_out, w_other, payload, wide, rows):
@@ -451,17 +452,22 @@
     cosine = jnp.cos(angles)
     sine = jnp.sin(angles) * jnp.where(jnp.arange(HEAD) < half, -1.0, 1.0)[None, :]
 
-    high = lax.reduce_precision(norm_gain, 8, 7)
-    middle = lax.reduce_precision(norm_gain - high, 8, 7)
-    low = norm_gain - high - middle
-    term = jnp.arange(16, dtype=jnp.int32)[:, None]
-    terms = jnp.where(term == 0, high, jnp.where(term == 1, middle, jnp.where(term == 2, low, 0.0)))
+    sent_keys, sent_values = (
+        jnp.pad(
+            lax.dynamic_slice_in_dim(cache, (1 - section) * TRIO, TRIO).reshape(CACHE_ROWS, HEAD),
+            ((0, WIDTH - CACHE_ROWS), (left, 3 * HEAD - left)),
+        )
+        for cache, left in ((keys, 2 * HEAD), (values, 3 * HEAD))
+    )
     rest = (
-        jnp.pad(w_key[0], ((0, 16), (0, HEAD)))
-        + jnp.pad(w_value[0], ((0, 16), (HEAD, 0)))
-        + jnp.pad(terms.astype(BF16), ((WIDTH, 0), (0, 0)))
-    )
-    weights = call(load_kernel, "load", "vv", shape(WIDTH + 16, ALL_PARTS), (w_query, rest))
+        jnp.pad(w_key[0], ((0, 0), (0, 3 * HEAD)))
+        + jnp.pad(w_value[0], ((0, 0), (HEAD, 2 * HEAD)))
+        + sent_keys
+        + sent_values
+    )
+    weights = call(
+        load_kernel, "load", "vvv", shape(WIDTH + 16, PACKED), (w_query, rest, norm_gain)
+    )
     other = swap(weights)
     residual, to_slots = call(
         prepare_kernel,
@@ -480,11 +486,8 @@
     )
     first = exchange(payload, "dp")
 
-    late_keys, late_values, late_out, late_replica, late_slot, _ = lax.optimization_barrier(
-        (keys, values, w_out[0], dest_replica, dest_slot, payload)
-    )
-    packed = swap(
-        call(pack_kernel, "pack", "svv", shape(CACHE_ROWS, WIDTH), (ids, late_keys, late_values))
+    late_out, late_replica, late_slot, _ = lax.optimization_barrier(
+        (w_out[0], dest_replica, dest_slot, payload)
     )
     out_other = swap(late_out)
     leaves = late_replica != row // ROWS_DEV
@@ -505,7 +508,7 @@
             "ssvvvvvv" + specs,
             (shape(N_DP, USED, HEAD), shape(16, HEAD))
             + (() if layer else (shape(N_DP, 2 * TILE, HEAD),)),
-            (ids, table, cosine, sine, received, keys, values, packed, *more),
+            (ids, table, cosine, sine, received, keys, values, other, *more),
             [pltpu.VMEM((N_DP * TILE, HEAD), F32)]
             if layer
             else [

time: 136 us -> 135 us (level)
  waiting for transfers between devices: 7.36 us -> 10.1 us
  starting transfers between devices: 25.4 us -> 23.5 us
    all_to_all x1, waiting for transfers between devices: 4.86 us -> 7.71 us  [exchange(): return lax.all_to_all(value, axis, split_axis=0, concat_axis=0, tiled=True)]
    ppermute x4 -> x3, starting transfers between devices: 21 us -> 19.1 us  [swap(): return lax.ppermute(value, 'section', [(0, 1), (1, 0)])]
    unnamed x18, local copies, waits for them, and re-layouts: 1.73 us -> 0.05 us
    pallas_call x11 -> x10, Pallas kernels: 12.2 us -> 11.6 us  [call(): pl.pallas_call(kernel, out_shape=out_shapes, in_specs=[spec_of[letter] fo...]
  transfers between devices with their start and end apart: 5 -> 4, of which waited for: 4 -> 4; matrix products, arithmetic and copies ran while one was open for 1% -> 1% of each run, Pallas kernels for 1% -> 1%
where the time goes in v6:
time: 135 us; the launch traced here: 134 us
  blocking collectives  85.4 us (63%)
  starting transfers between devices  23.5 us (17%)
  Pallas kernels  11.6 us (9%)
  waiting for transfers between devices  10.1 us (7%)
  other arithmetic  1.88 us (1%)
    all_to_all x5, blocking collectives, exchange(): return lax.all_to_all(value, axis, split_axis=0, concat_axis=0, tiled=True)  85.4 us
    ppermute x3, starting transfers between devices, swap(): return lax.ppermute(value, 'section', [(0, 1), (1, 0)])  19.1 us
    pallas_call x10, Pallas kernels, call(): pl.pallas_call(kernel, out_shape=out_shapes, in_specs=[spec_of[letter] fo...  11.6 us
    all_to_all x1, waiting for transfers between devices, exchange(): return lax.all_to_all(value, axis, split_axis=0, concat_axis=0, tiled=True)  7.71 us
    all_to_all x1, starting transfers between devices, exchange(): return lax.all_to_all(value, axis, split_axis=0, concat_axis=0, tiled=True)  4.42 us
  transfers between devices with their start and end apart: 4, of which 4 were waited for; matrix products, arithmetic and copies ran while one was open for 1% of the time, Pallas kernels for 1%

profile of v6, /device:TPU:1, one launch (start us, length us, event | category | flops | bytes accessed | tf_op | source)
XLA Modules:
  0.0 134.3 jit_solution(11776266750909542347)
XLA Ops:
  0.6 0.9 constant_dynamic-slice_fusion
  1.5 0.9 pad_add_fusion.rest
  2.5 0.1 load.1.weights
  2.6 8.9 %collective-permute-start = (bf16[272,1536]{1,0:T(8,128)(2,1)S(1)}, bf16[272,1536]{1,0:T(8,128)(2,1)S(1)}, u32[]{:S(2)}, u32[]{:S(2)}) collective-permute-start(bf16[272,1536]{1,0:T(8,128)(2,1)S(1)} %load.1.weights), channel_id=1, source_target_pairs={{0,1},{1,0},{2,3},{3,2},{4,5},{5,4},{6,7},{7,6},{8,9},{9,8},{10,11... | collective-permute-start | bytes 2506760 | tf_op jit(solution)/shard_map/ppermute | solution.py:413
  11.6 0.2 select_reduce_fusion.3.table.refs_1_
  11.8 0.1 slice.3
  11.9 0.1 pad_add_fusion.1.ids.refs_0_
  12.0 0.9 prepare.1
  12.9 0.1 compare_select_fusion
  13.0 0.1 fusion.2
  13.1 0.4 collective-permute-done.other.refs_7_
  13.5 2.1 %first.1 = bf16[32,48,128]{2,1,0:T(8,128)(2,1)} custom-call(s32[2]{0:T(128)S(1)} %pad_add_fusion.1.ids.refs_0_, s32[24]{0:T(128)S(1)} %select_reduce_fusion.3.table.refs_1_, bf16[96,256]{1,0:T(8,128)(2,1)S(1)} %get-tuple-element.22.rows.residual, bf16[272,1536]{1,0:T(8,128)(2,1)S(1)} %load.1.weights, ...), custom_call_target="tpu_custom_call" | custom-call | tf_op jit(solution)/shard_map/first/pallas_call | solution.py:397
  15.6 4.4 %all-to-all-start = ((bf16[32,48,128]{2,1,0:T(8,128)(2,1)}), bf16[32,48,128]{2,1,0:T(8,128)(2,1)S(1)}, u32[]{:S(2)}, u32[]{:S(2)}) async-start(bf16[32,48,128]{2,1,0:T(8,128)(2,1)} %first.1), calls=%async_computation | async-start | bytes 786432 | tf_op jit(solution)/shard_map/all_to_all | solution.py:409
  20.1 2.5 %collective-permute-start.1 = (bf16[1024,256]{1,0:T(8,128)(2,1)S(1)}, bf16[1024,256]{1,0:T(8,128)(2,1)S(1)}, u32[]{:S(2)}, u32[]{:S(2)}) collective-permute-start(bf16[1024,256]{1,0:T(8,128)(2,1)S(1)} %bitcast.14), channel_id=1, source_target_pairs={{0,1},{1,0},{2,3},{3,2},{4,5},{5,4},{6,7},{7,6},{8,9},{9,8},{10,11... | collective-permute-start | bytes 1572872 | tf_op jit(solution)/shard_map/ppermute | solution.py:413
  22.7 0.3 select_reduce_fusion.1
  23.0 0.1 select_reduce_fusion.2
  23.1 1.1 collective-permute-done.1.refs_9_.refs_3_
  24.2 7.7 %all-to-all-done.refs_4_ = bf16[32,48,128]{2,1,0:T(8,128)(2,1)S(1)} async-done(((bf16[32,48,128]{2,1,0:T(8,128)(2,1)}), bf16[32,48,128]{2,1,0:T(8,128)(2,1)S(1)}, u32[]{:S(2)}, u32[]{:S(2)}) %all-to-all-start) | async-done | bytes 393248 | tf_op jit(solution)/shard_map/all_to_all | solution.py:409
  31.9 1.6 %attend.2 = (bf16[32,32,128]{2,1,0:T(8,128)(2,1)S(1)}, bf16[16,128]{1,0:T(8,128)(2,1)S(1)}, bf16[32,16,128]{2,1,0:T(8,128)(2,1)S(1)}) custom-call(s32[2]{0:T(128)S(1)} %pad_add_fusion.1.ids.refs_0_, s32[24]{0:T(128)S(1)} %select_reduce_fusion.3.table.refs_1_, f32[8,128]{1,0:T(8,128)S(1)} %get-tuple-element.42.refs_2_, ...), custom_call_target="tpu_custom_call" | custom-call | tf_op jit(solution)/shard_map/attend/pallas_call | solution.py:397
  33.5 17.0 %all_to_all.30.refs_1_.gathered_0.second_in = bf16[32,32,128]{2,1,0:T(8,128)(2,1)S(1)} all-to-all(bf16[32,32,128]{2,1,0:T(8,128)(2,1)S(1)} %get-tuple-element.26), channel_id=1, replica_groups=mesh['dp'=32,'tensor'=8,'section'=2] {'dp'}, dimensions={0} | all-to-all | bytes 524288 | tf_op jit(solution)/shard_map/all_to_all | solution.py:409
  50.5 1.0 output.2
  51.5 20.6 %all_to_all.31.received = bf16[8,96,256]{2,1,0:T(8,128)(2,1)S(1)} all-to-all(bf16[8,96,256]{2,1,0:T(8,128)(2,1)S(1)} %output.2), channel_id=1, replica_groups=mesh['dp'=32,'tensor'=8,'section'=2] {'tensor'}, dimensions={0} | all-to-all | bytes 786432 | tf_op jit(solution)/shard_map/all_to_all | solution.py:409
  72.1 1.2 second.1
  73.3 16.7 %all_to_all.32.refs_4_.third_in = bf16[32,40,128]{2,1,0:T(8,128)(2,1)S(1)} all-to-all(bf16[32,40,128]{2,1,0:T(8,128)(2,1)S(1)} %get-tuple-element.29), channel_id=1, replica_groups=mesh['dp'=32,'tensor'=8,'section'=2] {'dp'}, dimensions={0} | all-to-all | bytes 655360 | tf_op jit(solution)/shard_map/all_to_all | solution.py:409
  89.9 1.3 attend.3
  91.3 14.4 %all_to_all.33.refs_1_.gathered_1.fourth_in = bf16[32,32,128]{2,1,0:T(8,128)(2,1)S(1)} all-to-all(bf16[32,32,128]{2,1,0:T(8,128)(2,1)S(1)} %get-tuple-element.30), channel_id=1, replica_groups=mesh['dp'=32,'tensor'=8,'section'=2] {'dp'}, dimensions={0} | all-to-all | bytes 524288 | tf_op jit(solution)/shard_map/all_to_all | solution.py:409
  105.6 1.0 output.3
  106.7 16.8 %all_to_all.34.received = bf16[8,96,256]{2,1,0:T(8,128)(2,1)S(1)} all-to-all(bf16[8,96,256]{2,1,0:T(8,128)(2,1)S(1)} %output.3), channel_id=1, replica_groups=mesh['dp'=32,'tensor'=8,'section'=2] {'tensor'}, dimensions={0} | all-to-all | bytes 786432 | tf_op jit(solution)/shard_map/all_to_all | solution.py:409
  123.5 0.7 last.1
  124.2 7.6 %collective-permute-start.2 = (bf16[112,256]{1,0:T(8,128)(2,1)S(1)}, bf16[112,256]{1,0:T(8,128)(2,1)S(1)}, u32[]{:S(2)}, u32[]{:S(2)}) collective-permute-start(bf16[112,256]{1,0:T(8,128)(2,1)S(1)} %get-tuple-element.34), channel_id=1, source_target_pairs={{0,1},{1,0},{2,3},{3,2},{4,5},{5,4},{6,7},{7,6},{8,9},{9,8},{10,11... | collective-permute-start | bytes 172040 | tf_op jit(solution)/shard_map/ppermute | solution.py:413
  131.8 0.9 collective-permute-done.2.received
  132.7 1.7 %final.1 = (bf16[192,256]{1,0:T(8,128)(2,1)}, bf16[6,64,128]{2,1,0:T(8,128)(2,1)}, bf16[6,64,128]{2,1,0:T(8,128)(2,1)}) custom-call(s32[2]{0:T(128)S(1)} %pad_add_fusion.1.ids.refs_0_, s32[24]{0:T(128)S(1)} %select_reduce_fusion.3.table.refs_1_, bf16[192,192]{1,0:T(8,128)(2,1)S(1)} %get-tuple-element.21.to_slots, ...), custom_call_target="tpu_custom_call" | custom-call | tf_op jit(solution)/shard_map/final/pallas_call | solution.py:397
  (28 shorter events, 0.2 us)
Async XLA Ops:
  0.6 1.8 %copy-start.3 = (bf16[1,256,1024]{2,1,0:T(8,128)(2,1)S(1)}, bf16[1,256,1024]{2,1,0:T(8,128)(2,1)}, u32[]{:S(2)}) copy-start(bf16[1,256,1024]{2,1,0:T(8,128)(2,1)} %query.1) | copy-start | bytes 1572868
  1.5 0.9 copy-start.5
  2.5 9.1 %copy-start.6 = (s32[192]{0:T(256)S(1)}, s32[192]{0:T(256)}, u32[]{:S(2)}) copy-start(s32[192]{0:T(256)} %param.20) | copy-start | bytes 2308
  2.5 9.1 %copy-start.7 = (s32[192]{0:T(256)S(1)}, s32[192]{0:T(256)}, u32[]{:S(2)}) copy-start(s32[192]{0:T(256)} %param.21) | copy-start | bytes 2308
  2.5 9.1 %copy-start.8 = (s32[192]{0:T(256)S(1)}, s32[192]{0:T(256)}, u32[]{:S(2)}) copy-start(s32[192]{0:T(256)} %param.19) | copy-start | bytes 2308
  2.5 9.5 %copy-start.4 = (bf16[192,256]{1,0:T(8,128)(2,1)S(1)}, bf16[192,256]{1,0:T(8,128)(2,1)}, u32[]{:S(2)}) copy-start(bf16[192,256]{1,0:T(8,128)(2,1)} %hidden.1) | copy-start | bytes 294916
  2.5 11.0 %copy-start.2 = (bf16[1,6,64,128]{3,2,1,0:T(8,128)(2,1)S(1)}, bf16[1,6,64,128]{3,2,1,0:T(8,128)(2,1)}, u32[]{:S(2)}) copy-start(bf16[1,6,64,128]{3,2,1,0:T(8,128)(2,1)} %param.17) | copy-start | bytes 294916
  2.6 10.9 %copy-start.1 = (bf16[1,6,64,128]{3,2,1,0:T(8,128)(2,1)S(1)}, bf16[1,6,64,128]{3,2,1,0:T(8,128)(2,1)}, u32[]{:S(2)}) copy-start(bf16[1,6,64,128]{3,2,1,0:T(8,128)(2,1)} %param.18) | copy-start | bytes 294916
  2.6 10.9 %collective-permute-start = (bf16[272,1536]{1,0:T(8,128)(2,1)S(1)}, bf16[272,1536]{1,0:T(8,128)(2,1)S(1)}, u32[]{:S(2)}, u32[]{:S(2)}) collective-permute-start(bf16[272,1536]{1,0:T(8,128)(2,1)S(1)} %load.1.weights), channel_id=1, source_target_pairs={{0,1},{1,0},{2,3},{3,2},{4,5},{5,4},{6,7},{7,6},{8,9},{9,8},{10,11... | collective-permute-start | bytes 2506760 | tf_op jit(solution)/shard_map/ppermute | solution.py:413
  15.6 4.5 %copy-start = (bf16[1,1024,256]{2,1,0:T(8,128)(2,1)S(1)}, bf16[1,1024,256]{2,1,0:T(8,128)(2,1)}, u32[]{:S(2)}) copy-start(bf16[1,1024,256]{2,1,0:T(8,128)(2,1)} %param.16) | copy-start | bytes 1572868
  15.6 16.2 %all-to-all-start = ((bf16[32,48,128]{2,1,0:T(8,128)(2,1)}), bf16[32,48,128]{2,1,0:T(8,128)(2,1)S(1)}, u32[]{:S(2)}, u32[]{:S(2)}) async-start(bf16[32,48,128]{2,1,0:T(8,128)(2,1)} %first.1), calls=%async_computation | async-start | bytes 786432 | tf_op jit(solution)/shard_map/all_to_all | solution.py:409
  20.1 4.1 %collective-permute-start.1 = (bf16[1024,256]{1,0:T(8,128)(2,1)S(1)}, bf16[1024,256]{1,0:T(8,128)(2,1)S(1)}, u32[]{:S(2)}, u32[]{:S(2)}) collective-permute-start(bf16[1024,256]{1,0:T(8,128)(2,1)S(1)} %bitcast.14), channel_id=1, source_target_pairs={{0,1},{1,0},{2,3},{3,2},{4,5},{5,4},{6,7},{7,6},{8,9},{9,8},{10,11... | collective-permute-start | bytes 1572872 | tf_op jit(solution)/shard_map/ppermute | solution.py:413
  124.2 8.5 %collective-permute-start.2 = (bf16[112,256]{1,0:T(8,128)(2,1)S(1)}, bf16[112,256]{1,0:T(8,128)(2,1)S(1)}, u32[]{:S(2)}, u32[]{:S(2)}) collective-permute-start(bf16[112,256]{1,0:T(8,128)(2,1)S(1)} %get-tuple-element.34), channel_id=1, source_target_pairs={{0,1},{1,0},{2,3},{3,2},{4,5},{5,4},{6,7},{7,6},{8,9},{9,8},{10,11... | collective-permute-start | bytes 172040 | tf_op jit(solution)/shard_map/ppermute | solution.py:413

commit v7 on v6

--- a/solution.py
+++ b/solution.py
@@ -341,23 +341,15 @@
             swapped[HALF_ROWS:, :HEAD] = total
 
 
-def final_kernel(
-    ids, table, to_slots, first, second, received, keys, values, mine, second_in, third_in, fourth_in,
-    out, key_out, value_out, pieces
+def arrive_kernel(
+    ids, table, to_slots, first, second, keys, values, second_in, third_in, fourth_in,
+    part, key_rows, value_rows, pieces
 ):
-    def write_rows(low, high):
-        out[...] = (
-            dot(to_slots[:HALF_ROWS, :], low, ((0,), (0,)))
-            + dot(to_slots[HALF_ROWS:, :], high, ((0,), (0,)))
-        ).astype(BF16)
-
-    others = received[:HALF_ROWS, :]
-    pl.when(ids[SECTION] == 0)(lambda: write_rows(first[...], others))
-    pl.when(ids[SECTION] == 1)(lambda: write_rows(others, second[...]))
-
-    me = ids[REPLICA]
-    position = iota((CONTEXT, HEAD), 0)
-    own = mine[...].astype(F32) + received[HALF_ROWS:, :HEAD].astype(F32)
+    def write_rows(order, rows):
+        part[...] = dot(order, rows[...], ((0,), (0,)))
+
+    pl.when(ids[SECTION] == 0)(lambda: write_rows(to_slots[:HALF_ROWS, :], first))
+    pl.when(ids[SECTION] == 1)(lambda: write_rows(to_slots[HALF_ROWS:, :], second))
     for p in range(N_DP):
         for i, (gathered, first_row) in enumerate(
             ((second_in, USED - 16), (third_in, USED - TILE), (fourth_in, USED - 16))
@@ -369,27 +361,40 @@
     for r in range(ROWS_DEV):
         source = table[SOURCE + r]
         anchor = over_six(source)
-        written = position == table[NEW_LEN + r]
-        moves = anchor != me
-
-        def write(key_rows, value_rows):
-            key_out[r] = jnp.where(written, own[r : r + 1], key_rows).astype(BF16)
-            value_out[r] = jnp.where(written, own[r + 8 : r + 9], value_rows).astype(BF16)
-
-        @pl.when(anchor == me)
+        moves = anchor != ids[REPLICA]
+
+        @pl.when(anchor == ids[REPLICA])
         def _():
             held = source - anchor * ROWS_DEV
-            write(keys[held].astype(F32), values[held].astype(F32))
+            key_rows[r] = keys[held]
+            value_rows[r] = values[held]
 
         @pl.when(moves)
         def _():
             parts = [
-                pieces[pl.ds(tile_row(count * PIECES + i), N_DP, stride=TILES), :]
+                pieces[pl.ds(tile_row(count * PIECES + i), N_DP, stride=TILES), :].astype(BF16)
                 for i in range(PIECES)
             ]
-            write(jnp.concatenate(parts[:2], 0), jnp.concatenate(parts[2:], 0))
+            key_rows[r] = jnp.concatenate(parts[:2], 0)
+            value_rows[r] = jnp.concatenate(parts[2:], 0)
 
         count = count + jnp.where(moves, 1, 0)
+
+
+def final_kernel(
+    ids, table, to_slots, part, key_rows, value_rows, received, mine, out, key_out, value_out
+):
+    def write_rows(order):
+        out[...] = (part[...] + dot(order, received[:HALF_ROWS, :], ((0,), (0,)))).astype(BF16)
+
+    pl.when(ids[SECTION] == 0)(lambda: write_rows(to_slots[HALF_ROWS:, :]))
+    pl.when(ids[SECTION] == 1)(lambda: write_rows(to_slots[:HALF_ROWS, :]))
+    position = iota((CONTEXT, HEAD), 0)
+    own = mine[...].astype(F32) + received[HALF_ROWS:, :HEAD].astype(F32)
+    for r in range(ROWS_DEV):
+        written = position == table[NEW_LEN + r]
+        for rows, target, row in ((key_rows, key_out, r), (value_rows, value_out, r + 8)):
+            target[r] = jnp.where(written, own[row : row + 1], rows[r].astype(F32)).astype(BF16)
 
 
 def call(kernel, name, specs, out_shapes, operands, scratch=()):
@@ -549,14 +554,22 @@
         (shape(HALF_ROWS, WIDTH), shape(16, HEAD), shape(HALF_ROWS + 16, WIDTH)),
         (ids, table, sums, result_0, second, fourth, own_0, own_1),
     )
+    cache_shape = shape(ROWS_DEV, CONTEXT, HEAD)
+    received = swap(swapped)
+    part, key_rows, value_rows = call(
+        arrive_kernel,
+        "arrive",
+        "ssvvvvvvvv",
+        (jax.ShapeDtypeStruct((ROWS, WIDTH), F32), cache_shape, cache_shape),
+        (ids, table, to_slots, result_0, result_1, keys, values, second, third, fourth),
+        [pltpu.VMEM(((N_DP + 1) * TILES, HEAD), F32)],
+    )
     layer_out, key_out, value_out = call(
         final_kernel,
         "final",
-        "ssvvvvvvvvvv",
-        (shape(ROWS, WIDTH), shape(ROWS_DEV, CONTEXT, HEAD), shape(ROWS_DEV, CONTEXT, HEAD)),
-        (ids, table, to_slots, result_0, result_1, swap(swapped), keys, values, mine,
-         second, third, fourth),
-        [pltpu.VMEM((N_DP * TILES, HEAD), F32)],
+        "ssvvvvvv",
+        (shape(ROWS, WIDTH), cache_shape, cache_shape),
+        (ids, table, to_slots, part, key_rows, value_rows, received, mine),
     )
     return layer_out[None], key_out[None], value_out[None]
 

time: 135 us -> 135 us (level)
    pallas_call x10 -> x11, Pallas kernels: 11.6 us -> 12.4 us  [call(): pl.pallas_call(kernel, out_shape=out_shapes, in_specs=[spec_of[letter] fo...]
  transfers between devices with their start and end apart: 4 -> 4, of which waited for: 4 -> 3; matrix products, arithmetic and copies ran while one was open for 1% -> 1% of each run, Pallas kernels for 1% -> 1%
where the time goes in v7:
time: 135 us; the launch traced here: 134 us
  blocking collectives  85.4 us (63%)
  starting transfers between devices  23.5 us (17%)
  Pallas kernels  12.4 us (9%)
  waiting for transfers between devices  9.19 us (7%)
  other arithmetic  1.88 us (1%)
    all_to_all x5, blocking collectives, exchange(): return lax.all_to_all(value, axis, split_axis=0, concat_axis=0, tiled=True)  85.4 us
    ppermute x3, starting transfers between devices, swap(): return lax.ppermute(value, 'section', [(0, 1), (1, 0)])  19.1 us
    pallas_call x11, Pallas kernels, call(): pl.pallas_call(kernel, out_shape=out_shapes, in_specs=[spec_of[letter] fo...  12.4 us
    all_to_all x1, waiting for transfers between devices, exchange(): return lax.all_to_all(value, axis, split_axis=0, concat_axis=0, tiled=True)  7.72 us
    all_to_all x1, starting transfers between devices, exchange(): return lax.all_to_all(value, axis, split_axis=0, concat_axis=0, tiled=True)  4.42 us
  transfers between devices with their start and end apart: 4, of which 3 were waited for; matrix products, arithmetic and copies ran while one was open for 1% of the time, Pallas kernels for 1%

profile of v7, /device:TPU:1, one launch (start us, length us, event | category | flops | bytes accessed | tf_op | source)
XLA Modules:
  0.0 134.2 jit_solution(4840449200406389028)
XLA Ops:
  0.6 0.9 constant_dynamic-slice_fusion
  1.5 0.9 pad_add_fusion.rest
  2.5 0.1 load.1.weights
  2.6 8.9 %collective-permute-start = (bf16[272,1536]{1,0:T(8,128)(2,1)S(1)}, bf16[272,1536]{1,0:T(8,128)(2,1)S(1)}, u32[]{:S(2)}, u32[]{:S(2)}) collective-permute-start(bf16[272,1536]{1,0:T(8,128)(2,1)S(1)} %load.1.weights), channel_id=1, source_target_pairs={{0,1},{1,0},{2,3},{3,2},{4,5},{5,4},{6,7},{7,6},{8,9},{9,8},{10,11... | collective-permute-start | bytes 2506760 | tf_op jit(solution)/shard_map/ppermute | solution.py:418
  11.6 0.2 select_reduce_fusion.3.table.refs_1_
  11.8 0.1 slice.3
  11.9 0.1 pad_add_fusion.1.ids.refs_0_
  12.0 0.9 prepare.1
  12.9 0.1 compare_select_fusion
  13.0 0.1 fusion.2
  13.1 0.4 collective-permute-done.other.refs_7_
  13.5 2.1 %first.1 = bf16[32,48,128]{2,1,0:T(8,128)(2,1)} custom-call(s32[2]{0:T(128)S(1)} %pad_add_fusion.1.ids.refs_0_, s32[24]{0:T(128)S(1)} %select_reduce_fusion.3.table.refs_1_, bf16[96,256]{1,0:T(8,128)(2,1)S(1)} %get-tuple-element.25.rows.residual, bf16[272,1536]{1,0:T(8,128)(2,1)S(1)} %load.1.weights, ...), custom_call_target="tpu_custom_call" | custom-call | tf_op jit(solution)/shard_map/first/pallas_call | solution.py:402
  15.6 4.4 %all-to-all-start = ((bf16[32,48,128]{2,1,0:T(8,128)(2,1)}), bf16[32,48,128]{2,1,0:T(8,128)(2,1)S(1)}, u32[]{:S(2)}, u32[]{:S(2)}) async-start(bf16[32,48,128]{2,1,0:T(8,128)(2,1)} %first.1), calls=%async_computation | async-start | bytes 786432 | tf_op jit(solution)/shard_map/all_to_all | solution.py:414
  20.1 2.5 %collective-permute-start.1 = (bf16[1024,256]{1,0:T(8,128)(2,1)S(1)}, bf16[1024,256]{1,0:T(8,128)(2,1)S(1)}, u32[]{:S(2)}, u32[]{:S(2)}) collective-permute-start(bf16[1024,256]{1,0:T(8,128)(2,1)S(1)} %bitcast.14), channel_id=1, source_target_pairs={{0,1},{1,0},{2,3},{3,2},{4,5},{5,4},{6,7},{7,6},{8,9},{9,8},{10,11... | collective-permute-start | bytes 1572872 | tf_op jit(solution)/shard_map/ppermute | solution.py:418
  22.6 0.3 select_reduce_fusion.1
  23.0 0.1 select_reduce_fusion.2
  23.1 1.1 collective-permute-done.1.refs_9_.refs_3_
  24.2 7.7 %all-to-all-done.refs_4_ = bf16[32,48,128]{2,1,0:T(8,128)(2,1)S(1)} async-done(((bf16[32,48,128]{2,1,0:T(8,128)(2,1)}), bf16[32,48,128]{2,1,0:T(8,128)(2,1)S(1)}, u32[]{:S(2)}, u32[]{:S(2)}) %all-to-all-start) | async-done | bytes 393248 | tf_op jit(solution)/shard_map/all_to_all | solution.py:414
  31.9 1.6 %attend.2 = (bf16[32,32,128]{2,1,0:T(8,128)(2,1)S(1)}, bf16[16,128]{1,0:T(8,128)(2,1)S(1)}, bf16[32,16,128]{2,1,0:T(8,128)(2,1)S(1)}) custom-call(s32[2]{0:T(128)S(1)} %pad_add_fusion.1.ids.refs_0_, s32[24]{0:T(128)S(1)} %select_reduce_fusion.3.table.refs_1_, f32[8,128]{1,0:T(8,128)S(1)} %get-tuple-element.48.refs_2_, ...), custom_call_target="tpu_custom_call" | custom-call | tf_op jit(solution)/shard_map/attend/pallas_call | solution.py:402
  33.5 17.0 %all_to_all.30.refs_1_.gathered_0.second_in = bf16[32,32,128]{2,1,0:T(8,128)(2,1)S(1)} all-to-all(bf16[32,32,128]{2,1,0:T(8,128)(2,1)S(1)} %get-tuple-element.29), channel_id=1, replica_groups=mesh['dp'=32,'tensor'=8,'section'=2] {'dp'}, dimensions={0} | all-to-all | bytes 524288 | tf_op jit(solution)/shard_map/all_to_all | solution.py:414
  50.5 1.0 output.2
  51.5 20.6 %all_to_all.31.received = bf16[8,96,256]{2,1,0:T(8,128)(2,1)S(1)} all-to-all(bf16[8,96,256]{2,1,0:T(8,128)(2,1)S(1)} %output.2), channel_id=1, replica_groups=mesh['dp'=32,'tensor'=8,'section'=2] {'tensor'}, dimensions={0} | all-to-all | bytes 786432 | tf_op jit(solution)/shard_map/all_to_all | solution.py:414
  72.1 1.2 second.1
  73.3 16.7 %all_to_all.32.refs_4_.third_in = bf16[32,40,128]{2,1,0:T(8,128)(2,1)S(1)} all-to-all(bf16[32,40,128]{2,1,0:T(8,128)(2,1)S(1)} %get-tuple-element.32), channel_id=1, replica_groups=mesh['dp'=32,'tensor'=8,'section'=2] {'dp'}, dimensions={0} | all-to-all | bytes 655360 | tf_op jit(solution)/shard_map/all_to_all | solution.py:414
  89.9 1.3 attend.3
  91.3 14.4 %all_to_all.33.refs_1_.gathered_1.fourth_in = bf16[32,32,128]{2,1,0:T(8,128)(2,1)S(1)} all-to-all(bf16[32,32,128]{2,1,0:T(8,128)(2,1)S(1)} %get-tuple-element.33), channel_id=1, replica_groups=mesh['dp'=32,'tensor'=8,'section'=2] {'dp'}, dimensions={0} | all-to-all | bytes 524288 | tf_op jit(solution)/shard_map/all_to_all | solution.py:414
  105.6 1.0 output.3
  106.7 16.8 %all_to_all.34.received = bf16[8,96,256]{2,1,0:T(8,128)(2,1)S(1)} all-to-all(bf16[8,96,256]{2,1,0:T(8,128)(2,1)S(1)} %output.3), channel_id=1, replica_groups=mesh['dp'=32,'tensor'=8,'section'=2] {'tensor'}, dimensions={0} | all-to-all | bytes 786432 | tf_op jit(solution)/shard_map/all_to_all | solution.py:414
  123.5 0.7 last.1
  124.2 7.6 %collective-permute-start.2 = (bf16[112,256]{1,0:T(8,128)(2,1)S(1)}, bf16[112,256]{1,0:T(8,128)(2,1)S(1)}, u32[]{:S(2)}, u32[]{:S(2)}) collective-permute-start(bf16[112,256]{1,0:T(8,128)(2,1)S(1)} %get-tuple-element.40), channel_id=1, source_target_pairs={{0,1},{1,0},{2,3},{3,2},{4,5},{5,4},{6,7},{7,6},{8,9},{9,8},{10,11... | collective-permute-start | bytes 172040 | tf_op jit(solution)/shard_map/ppermute | solution.py:418
  131.8 0.9 arrive.1
  132.7 1.5 %final.1 = (bf16[192,256]{1,0:T(8,128)(2,1)}, bf16[6,64,128]{2,1,0:T(8,128)(2,1)}, bf16[6,64,128]{2,1,0:T(8,128)(2,1)}) custom-call(s32[2]{0:T(128)S(1)} %pad_add_fusion.1.ids.refs_0_, s32[24]{0:T(128)S(1)} %select_reduce_fusion.3.table.refs_1_, bf16[192,192]{1,0:T(8,128)(2,1)S(1)} %get-tuple-element.24.to_slots, f32[192,256]{1,0:T(8,128)S(1)} %get-tuple-element.37.part, ...), custom_call_target="tpu_custom_call" | custom-call | tf_op jit(solution)/shard_map/final/pallas_call | solution.py:402
  (29 shorter events, 0.2 us)
Async XLA Ops:
  0.6 1.8 %copy-start.3 = (bf16[1,256,1024]{2,1,0:T(8,128)(2,1)S(1)}, bf16[1,256,1024]{2,1,0:T(8,128)(2,1)}, u32[]{:S(2)}) copy-start(bf16[1,256,1024]{2,1,0:T(8,128)(2,1)} %query.1) | copy-start | bytes 1572868
  1.5 0.9 copy-start.5
  2.5 9.1 %copy-start.6 = (s32[192]{0:T(256)S(1)}, s32[192]{0:T(256)}, u32[]{:S(2)}) copy-start(s32[192]{0:T(256)} %param.20) | copy-start | bytes 2308
  2.5 9.1 %copy-start.7 = (s32[192]{0:T(256)S(1)}, s32[192]{0:T(256)}, u32[]{:S(2)}) copy-start(s32[192]{0:T(256)} %param.21) | copy-start | bytes 2308
  2.5 9.1 %copy-start.8 = (s32[192]{0:T(256)S(1)}, s32[192]{0:T(256)}, u32[]{:S(2)}) copy-start(s32[192]{0:T(256)} %param.19) | copy-start | bytes 2308
  2.5 9.5 %copy-start.4 = (bf16[192,256]{1,0:T(8,128)(2,1)S(1)}, bf16[192,256]{1,0:T(8,128)(2,1)}, u32[]{:S(2)}) copy-start(bf16[192,256]{1,0:T(8,128)(2,1)} %hidden.1) | copy-start | bytes 294916
  2.5 11.0 %copy-start.2 = (bf16[1,6,64,128]{3,2,1,0:T(8,128)(2,1)S(1)}, bf16[1,6,64,128]{3,2,1,0:T(8,128)(2,1)}, u32[]{:S(2)}) copy-start(bf16[1,6,64,128]{3,2,1,0:T(8,128)(2,1)} %param.17) | copy-start | bytes 294916
  2.6 10.9 %copy-start.1 = (bf16[1,6,64,128]{3,2,1,0:T(8,128)(2,1)S(1)}, bf16[1,6,64,128]{3,2,1,0:T(8,128)(2,1)}, u32[]{:S(2)}) copy-start(bf16[1,6,64,128]{3,2,1,0:T(8,128)(2,1)} %param.18) | copy-start | bytes 294916
  2.6 10.9 %collective-permute-start = (bf16[272,1536]{1,0:T(8,128)(2,1)S(1)}, bf16[272,1536]{1,0:T(8,128)(2,1)S(1)}, u32[]{:S(2)}, u32[]{:S(2)}) collective-permute-start(bf16[272,1536]{1,0:T(8,128)(2,1)S(1)} %load.1.weights), channel_id=1, source_target_pairs={{0,1},{1,0},{2,3},{3,2},{4,5},{5,4},{6,7},{7,6},{8,9},{9,8},{10,11... | collective-permute-start | bytes 2506760 | tf_op jit(solution)/shard_map/ppermute | solution.py:418
  15.6 4.5 %copy-start = (bf16[1,1024,256]{2,1,0:T(8,128)(2,1)S(1)}, bf16[1,1024,256]{2,1,0:T(8,128)(2,1)}, u32[]{:S(2)}) copy-start(bf16[1,1024,256]{2,1,0:T(8,128)(2,1)} %param.16) | copy-start | bytes 1572868
  15.6 16.2 %all-to-all-start = ((bf16[32,48,128]{2,1,0:T(8,128)(2,1)}), bf16[32,48,128]{2,1,0:T(8,128)(2,1)S(1)}, u32[]{:S(2)}, u32[]{:S(2)}) async-start(bf16[32,48,128]{2,1,0:T(8,128)(2,1)} %first.1), calls=%async_computation | async-start | bytes 786432 | tf_op jit(solution)/shard_map/all_to_all | solution.py:414
  20.1 4.1 %collective-permute-start.1 = (bf16[1024,256]{1,0:T(8,128)(2,1)S(1)}, bf16[1024,256]{1,0:T(8,128)(2,1)S(1)}, u32[]{:S(2)}, u32[]{:S(2)}) collective-permute-start(bf16[1024,256]{1,0:T(8,128)(2,1)S(1)} %bitcast.14), channel_id=1, source_target_pairs={{0,1},{1,0},{2,3},{3,2},{4,5},{5,4},{6,7},{7,6},{8,9},{9,8},{10,11... | collective-permute-start | bytes 1572872 | tf_op jit(solution)/shard_map/ppermute | solution.py:418
  124.2 8.6 %collective-permute-start.2 = (bf16[112,256]{1,0:T(8,128)(2,1)S(1)}, bf16[112,256]{1,0:T(8,128)(2,1)S(1)}, u32[]{:S(2)}, u32[]{:S(2)}) collective-permute-start(bf16[112,256]{1,0:T(8,128)(2,1)S(1)} %get-tuple-element.40), channel_id=1, source_target_pairs={{0,1},{1,0},{2,3},{3,2},{4,5},{5,4},{6,7},{7,6},{8,9},{9,8},{10,11... | collective-permute-start | bytes 172040 | tf_op jit(solution)/shard_map/ppermute | solution.py:418

commit v8 on v7

--- a/solution.py
+++ b/solution.py
@@ -78,7 +78,7 @@
                 ]
 
 
-def spread_squares(rows, spread):
+def spread_squares(rows, spread, row=TRIO * PARTS):
     by_slot = rows.astype(F32)
     square = jnp.sum(by_slot * by_slot, axis=1, keepdims=True)
     lane = iota((N_DP, HEAD), 1)
@@ -86,7 +86,6 @@
     for s in range(TRIO):
         squares = jnp.where(lane == s, square[s * N_DP : (s + 1) * N_DP], squares)
     high = squares.astype(BF16).astype(F32)
-    row = TRIO * PARTS
     spread[pl.ds(row * N_DP, N_DP), :] = high
     spread[pl.ds((row + 1) * N_DP, N_DP), :] = squares - high
 
@@ -104,7 +103,9 @@
     weights[WIDTH:, ALL_PARTS:] = jnp.zeros((16, 2 * HEAD), BF16)
 
 
-def prepare_kernel(ids, new_index, hidden, residual, to_slots_out):
+def prepare_kernel(
+    ids, table, new_index, hidden, keys, values, residual, to_slots_out, squares, cut, spread
+):
     row, column = iota((ROWS, ROWS), 0), iota((ROWS, ROWS), 1)
     by_slot_order = pick(column == (row & (N_DP - 1)) * ROWS_DEV + (row >> 5))
     to_slots = dot(by_slot_order, to_new_order(new_index[...]), ((1,), (1,))).astype(BF16)
@@ -114,29 +115,35 @@
     @pl.when(ids[SECTION] == 0)
     def _():
         residual[...] = by_slot[:HALF_ROWS]
+        spread_squares(by_slot[:HALF_ROWS], squares, 0)
 
     @pl.when(ids[SECTION] == 1)
     def _():
         residual[...] = by_slot[HALF_ROWS:]
-
-
-def first_kernel(ids, table, rows, weights, other, keys, values, payload, spread):
+        spread_squares(by_slot[HALF_ROWS:], squares, 0)
+
     count = jnp.int32(0)
     for s in range(ROWS_DEV):
         leaves = table[DEST + s] != ids[REPLICA]
 
         @pl.when(leaves)
         def _():
-            base = pl.multiple_of(USED * N_DP + count * (PIECES * N_DP), N_DP)
+            base = pl.multiple_of(count * (PIECES * N_DP), N_DP)
             spread[pl.ds(base, CONTEXT), :] = keys[s].astype(F32)
             spread[pl.ds(base + CONTEXT, CONTEXT), :] = values[s].astype(F32)
 
         count = count + jnp.where(leaves, 1, 0)
-    spread_squares(rows[...], spread)
+    for p in range(N_DP):
+        cut[p] = spread[pl.ds(p, MOVES * PIECES, stride=N_DP), :].astype(BF16)
+
+
+def first_kernel(ids, rows, squares, cut, weights, other, payload, spread):
+    spread[pl.ds(TRIO * PARTS * N_DP, 2 * N_DP), :] = squares[...]
     pl.when(ids[SECTION] == 0)(lambda: project(rows[...], weights, spread))
     pl.when(ids[SECTION] == 1)(lambda: project(rows[...], other, spread))
     for p in range(N_DP):
-        payload[p] = spread[pl.ds(p, BLOCK, stride=N_DP), :].astype(BF16)
+        payload[p, :USED, :] = spread[pl.ds(p, USED, stride=N_DP), :].astype(BF16)
+        payload[p, USED:, :] = cut[p]
 
 
 def tile_row(piece):
@@ -474,20 +481,26 @@
         load_kernel, "load", "vvv", shape(WIDTH + 16, PACKED), (w_query, rest, norm_gain)
     )
     other = swap(weights)
-    residual, to_slots = call(
+    residual, to_slots, squares, cut = call(
         prepare_kernel,
         "prepare",
-        "svv",
-        (shape(HALF_ROWS, WIDTH), shape(ROWS, ROWS)),
-        (ids, new_index, hidden_in),
+        "ssvvvv",
+        (
+            shape(HALF_ROWS, WIDTH),
+            shape(ROWS, ROWS),
+            jax.ShapeDtypeStruct((2 * N_DP, HEAD), F32),
+            shape(N_DP, MOVES * PIECES, HEAD),
+        ),
+        (ids, table, new_index, hidden_in, keys, values),
+        [pltpu.VMEM((MOVES * PIECES * N_DP, HEAD), F32)],
     )
     payload = call(
         first_kernel,
         "first",
-        "ssvvvvv",
+        "svvvvv",
         shape(N_DP, BLOCK, HEAD),
-        (ids, table, residual, weights, other, keys, values),
-        [pltpu.VMEM((BLOCK * N_DP, HEAD), F32)],
+        (ids, residual, squares, cut, weights, other),
+        [pltpu.VMEM((USED * N_DP, HEAD), F32)],
     )
     first = exchange(payload, "dp")
 

time: 135 us -> 136 us (level)
  transfers between devices with their start and end apart: 4 -> 4, of which waited for: 3 -> 2; matrix products, arithmetic and copies ran while one was open for 1% -> 1% of each run, Pallas kernels for 1% -> 2%
where the time goes in v8:
time: 136 us; the launch traced here: 135 us
  blocking collectives  85.2 us (63%)
  starting transfers between devices  23.2 us (17%)
  Pallas kernels  12.4 us (9%)
  waiting for transfers between devices  9.51 us (7%)
  local copies, waits for them, and re-layouts  2.33 us (2%)
  other arithmetic  1.87 us (1%)
    all_to_all x5, blocking collectives, exchange(): return lax.all_to_all(value, axis, split_axis=0, concat_axis=0, tiled=True)  85.2 us
    ppermute x3, starting transfers between devices, swap(): return lax.ppermute(value, 'section', [(0, 1), (1, 0)])  18.7 us
    pallas_call x11, Pallas kernels, call(): pl.pallas_call(kernel, out_shape=out_shapes, in_specs=[spec_of[letter] fo...  12.4 us
    all_to_all x1, waiting for transfers between devices, exchange(): return lax.all_to_all(value, axis, split_axis=0, concat_axis=0, tiled=True)  8.36 us
    all_to_all x1, starting transfers between devices, exchange(): return lax.all_to_all(value, axis, split_axis=0, concat_axis=0, tiled=True)  4.42 us
  transfers between devices with their start and end apart: 4, of which 2 were waited for; matrix products, arithmetic and copies ran while one was open for 1% of the time, Pallas kernels for 2%

profile of v8, /device:TPU:1, one launch (start us, length us, event | category | flops | bytes accessed | tf_op | source)
XLA Modules:
  0.0 135.3 jit_solution(14154085370484090549)
XLA Ops:
  0.6 0.9 constant_dynamic-slice_fusion
  1.5 0.9 pad_add_fusion.rest
  2.6 8.9 %collective-permute-start = (bf16[272,1536]{1,0:T(8,128)(2,1)S(1)}, bf16[272,1536]{1,0:T(8,128)(2,1)S(1)}, u32[]{:S(2)}, u32[]{:S(2)}) collective-permute-start(bf16[272,1536]{1,0:T(8,128)(2,1)S(1)} %load.1.weights), channel_id=1, source_target_pairs={{0,1},{1,0},{2,3},{3,2},{4,5},{5,4},{6,7},{7,6},{8,9},{9,8},{10,11... | collective-permute-start | bytes 2506760 | tf_op jit(solution)/shard_map/ppermute | solution.py:425
  11.6 0.6 copy-done.6
  12.2 0.7 copy-done.8
  12.9 0.2 select_reduce_fusion.3.table.refs_1_
  13.1 0.1 slice.3
  13.2 0.1 pad_add_fusion.1.ids.refs_0_
  13.3 1.2 prepare.1
  14.5 0.1 compare_select_fusion
  14.6 0.1 fusion.2
  14.7 1.8 %first.1 = bf16[32,48,128]{2,1,0:T(8,128)(2,1)} custom-call(s32[2]{0:T(128)S(1)} %pad_add_fusion.1.ids.refs_0_, bf16[96,256]{1,0:T(8,128)(2,1)S(1)} %get-tuple-element.27.rows.residual, f32[64,128]{1,0:T(8,128)S(1)} %get-tuple-element.28.squares, bf16[32,16,128]{2,1,0:T(8,128)(2,1)S(1)} %get-tuple-element.29.cut, bf16[272,1536]{1,0:T(8,128)(2,1)S(1)} %load.1.weights, ...), custom_call_target="tpu_custom_call" | custom-call | tf_op jit(solution)/shard_map/first/pallas_call | solution.py:409
  16.6 4.4 %all-to-all-start = ((bf16[32,48,128]{2,1,0:T(8,128)(2,1)}), bf16[32,48,128]{2,1,0:T(8,128)(2,1)S(1)}, u32[]{:S(2)}, u32[]{:S(2)}) async-start(bf16[32,48,128]{2,1,0:T(8,128)(2,1)} %first.1), calls=%async_computation | async-start | bytes 786432 | tf_op jit(solution)/shard_map/all_to_all | solution.py:421
  21.0 2.2 %collective-permute-start.1 = (bf16[1024,256]{1,0:T(8,128)(2,1)S(1)}, bf16[1024,256]{1,0:T(8,128)(2,1)S(1)}, u32[]{:S(2)}, u32[]{:S(2)}) collective-permute-start(bf16[1024,256]{1,0:T(8,128)(2,1)S(1)} %bitcast.14), channel_id=1, source_target_pairs={{0,1},{1,0},{2,3},{3,2},{4,5},{5,4},{6,7},{7,6},{8,9},{9,8},{10,11... | collective-permute-start | bytes 1572872 | tf_op jit(solution)/shard_map/ppermute | solution.py:425
  23.2 0.3 select_reduce_fusion.1
  23.5 0.1 select_reduce_fusion.2
  23.7 1.1 collective-permute-done.1.refs_9_.refs_3_
  24.8 8.4 %all-to-all-done.refs_4_ = bf16[32,48,128]{2,1,0:T(8,128)(2,1)S(1)} async-done(((bf16[32,48,128]{2,1,0:T(8,128)(2,1)}), bf16[32,48,128]{2,1,0:T(8,128)(2,1)S(1)}, u32[]{:S(2)}, u32[]{:S(2)}) %all-to-all-start) | async-done | bytes 393248 | tf_op jit(solution)/shard_map/all_to_all | solution.py:421
  33.2 1.6 %attend.2 = (bf16[32,32,128]{2,1,0:T(8,128)(2,1)S(1)}, bf16[16,128]{1,0:T(8,128)(2,1)S(1)}, bf16[32,16,128]{2,1,0:T(8,128)(2,1)S(1)}) custom-call(s32[2]{0:T(128)S(1)} %pad_add_fusion.1.ids.refs_0_, s32[24]{0:T(128)S(1)} %select_reduce_fusion.3.table.refs_1_, f32[8,128]{1,0:T(8,128)S(1)} %get-tuple-element.52.refs_2_, ...), custom_call_target="tpu_custom_call" | custom-call | tf_op jit(solution)/shard_map/attend/pallas_call | solution.py:409
  34.8 16.8 %all_to_all.30.refs_1_.gathered_0.second_in = bf16[32,32,128]{2,1,0:T(8,128)(2,1)S(1)} all-to-all(bf16[32,32,128]{2,1,0:T(8,128)(2,1)S(1)} %get-tuple-element.33), channel_id=1, replica_groups=mesh['dp'=32,'tensor'=8,'section'=2] {'dp'}, dimensions={0} | all-to-all | bytes 524288 | tf_op jit(solution)/shard_map/all_to_all | solution.py:421
  51.6 1.0 output.2
  52.6 20.6 %all_to_all.31.received = bf16[8,96,256]{2,1,0:T(8,128)(2,1)S(1)} all-to-all(bf16[8,96,256]{2,1,0:T(8,128)(2,1)S(1)} %output.2), channel_id=1, replica_groups=mesh['dp'=32,'tensor'=8,'section'=2] {'tensor'}, dimensions={0} | all-to-all | bytes 786432 | tf_op jit(solution)/shard_map/all_to_all | solution.py:421
  73.2 1.2 second.1
  74.5 17.3 %all_to_all.32.refs_4_.third_in = bf16[32,40,128]{2,1,0:T(8,128)(2,1)S(1)} all-to-all(bf16[32,40,128]{2,1,0:T(8,128)(2,1)S(1)} %get-tuple-element.36), channel_id=1, replica_groups=mesh['dp'=32,'tensor'=8,'section'=2] {'dp'}, dimensions={0} | all-to-all | bytes 655360 | tf_op jit(solution)/shard_map/all_to_all | solution.py:421
  91.7 1.3 attend.3
  93.1 14.4 %all_to_all.33.refs_1_.gathered_1.fourth_in = bf16[32,32,128]{2,1,0:T(8,128)(2,1)S(1)} all-to-all(bf16[32,32,128]{2,1,0:T(8,128)(2,1)S(1)} %get-tuple-element.37), channel_id=1, replica_groups=mesh['dp'=32,'tensor'=8,'section'=2] {'dp'}, dimensions={0} | all-to-all | bytes 524288 | tf_op jit(solution)/shard_map/all_to_all | solution.py:421
  107.5 1.0 output.3
  108.5 16.1 %all_to_all.34.received = bf16[8,96,256]{2,1,0:T(8,128)(2,1)S(1)} all-to-all(bf16[8,96,256]{2,1,0:T(8,128)(2,1)S(1)} %output.3), channel_id=1, replica_groups=mesh['dp'=32,'tensor'=8,'section'=2] {'tensor'}, dimensions={0} | all-to-all | bytes 786432 | tf_op jit(solution)/shard_map/all_to_all | solution.py:421
  124.6 0.7 last.1
  125.3 7.6 %collective-permute-start.2 = (bf16[112,256]{1,0:T(8,128)(2,1)S(1)}, bf16[112,256]{1,0:T(8,128)(2,1)S(1)}, u32[]{:S(2)}, u32[]{:S(2)}) collective-permute-start(bf16[112,256]{1,0:T(8,128)(2,1)S(1)} %get-tuple-element.44), channel_id=1, source_target_pairs={{0,1},{1,0},{2,3},{3,2},{4,5},{5,4},{6,7},{7,6},{8,9},{9,8},{10,11... | collective-permute-start | bytes 172040 | tf_op jit(solution)/shard_map/ppermute | solution.py:425
  132.9 0.9 arrive.1
  133.9 1.5 %final.1 = (bf16[192,256]{1,0:T(8,128)(2,1)}, bf16[6,64,128]{2,1,0:T(8,128)(2,1)}, bf16[6,64,128]{2,1,0:T(8,128)(2,1)}) custom-call(s32[2]{0:T(128)S(1)} %pad_add_fusion.1.ids.refs_0_, s32[24]{0:T(128)S(1)} %select_reduce_fusion.3.table.refs_1_, bf16[192,192]{1,0:T(8,128)(2,1)S(1)} %get-tuple-element.26.to_slots, f32[192,256]{1,0:T(8,128)S(1)} %get-tuple-element.41.part, ...), custom_call_target="tpu_custom_call" | custom-call | tf_op jit(solution)/shard_map/final/pallas_call | solution.py:409
  (29 shorter events, 0.2 us)
Async XLA Ops:
  0.6 1.8 %copy-start.3 = (bf16[1,256,1024]{2,1,0:T(8,128)(2,1)S(1)}, bf16[1,256,1024]{2,1,0:T(8,128)(2,1)}, u32[]{:S(2)}) copy-start(bf16[1,256,1024]{2,1,0:T(8,128)(2,1)} %query.1) | copy-start | bytes 1572868
  1.5 0.9 copy-start.5
  2.5 9.1 %copy-start.7 = (s32[192]{0:T(256)S(1)}, s32[192]{0:T(256)}, u32[]{:S(2)}) copy-start(s32[192]{0:T(256)} %param.21) | copy-start | bytes 2308
  2.5 10.8 %copy-start.1 = (bf16[1,6,64,128]{3,2,1,0:T(8,128)(2,1)S(1)}, bf16[1,6,64,128]{3,2,1,0:T(8,128)(2,1)}, u32[]{:S(2)}) copy-start(bf16[1,6,64,128]{3,2,1,0:T(8,128)(2,1)} %param.17) | copy-start | bytes 294916
  2.5 10.8 %copy-start.2 = (bf16[1,6,64,128]{3,2,1,0:T(8,128)(2,1)S(1)}, bf16[1,6,64,128]{3,2,1,0:T(8,128)(2,1)}, u32[]{:S(2)}) copy-start(bf16[1,6,64,128]{3,2,1,0:T(8,128)(2,1)} %param.18) | copy-start | bytes 294916
  2.5 10.8 %copy-start.4 = (bf16[192,256]{1,0:T(8,128)(2,1)S(1)}, bf16[192,256]{1,0:T(8,128)(2,1)}, u32[]{:S(2)}) copy-start(bf16[192,256]{1,0:T(8,128)(2,1)} %hidden.1) | copy-start | bytes 294916
  2.6 12.1 %collective-permute-start = (bf16[272,1536]{1,0:T(8,128)(2,1)S(1)}, bf16[272,1536]{1,0:T(8,128)(2,1)S(1)}, u32[]{:S(2)}, u32[]{:S(2)}) collective-permute-start(bf16[272,1536]{1,0:T(8,128)(2,1)S(1)} %load.1.weights), channel_id=1, source_target_pairs={{0,1},{1,0},{2,3},{3,2},{4,5},{5,4},{6,7},{7,6},{8,9},{9,8},{10,11... | collective-permute-start | bytes 2506760 | tf_op jit(solution)/shard_map/ppermute | solution.py:425
  11.6 0.7 copy-start.6
  12.2 0.7 copy-start.8
  16.5 4.4 %copy-start = (bf16[1,1024,256]{2,1,0:T(8,128)(2,1)S(1)}, bf16[1,1024,256]{2,1,0:T(8,128)(2,1)}, u32[]{:S(2)}) copy-start(bf16[1,1024,256]{2,1,0:T(8,128)(2,1)} %param.16) | copy-start | bytes 1572868
  16.6 16.6 %all-to-all-start = ((bf16[32,48,128]{2,1,0:T(8,128)(2,1)}), bf16[32,48,128]{2,1,0:T(8,128)(2,1)S(1)}, u32[]{:S(2)}, u32[]{:S(2)}) async-start(bf16[32,48,128]{2,1,0:T(8,128)(2,1)} %first.1), calls=%async_computation | async-start | bytes 786432 | tf_op jit(solution)/shard_map/all_to_all | solution.py:421
  21.0 3.8 %collective-permute-start.1 = (bf16[1024,256]{1,0:T(8,128)(2,1)S(1)}, bf16[1024,256]{1,0:T(8,128)(2,1)S(1)}, u32[]{:S(2)}, u32[]{:S(2)}) collective-permute-start(bf16[1024,256]{1,0:T(8,128)(2,1)S(1)} %bitcast.14), channel_id=1, source_target_pairs={{0,1},{1,0},{2,3},{3,2},{4,5},{5,4},{6,7},{7,6},{8,9},{9,8},{10,11... | collective-permute-start | bytes 1572872 | tf_op jit(solution)/shard_map/ppermute | solution.py:425
  125.3 8.6 %collective-permute-start.2 = (bf16[112,256]{1,0:T(8,128)(2,1)S(1)}, bf16[112,256]{1,0:T(8,128)(2,1)S(1)}, u32[]{:S(2)}, u32[]{:S(2)}) collective-permute-start(bf16[112,256]{1,0:T(8,128)(2,1)S(1)} %get-tuple-element.44), channel_id=1, source_target_pairs={{0,1},{1,0},{2,3},{3,2},{4,5},{5,4},{6,7},{7,6},{8,9},{9,8},{10,11... | collective-permute-start | bytes 172040 | tf_op jit(solution)/shard_map/ppermute | solution.py:425

commit v9 on v8

--- a/solution.py
+++ b/solution.py
@@ -104,7 +104,7 @@
 
 
 def prepare_kernel(
-    ids, table, new_index, hidden, keys, values, residual, to_slots_out, squares, cut, spread
+    ids, new_index, hidden, residual, to_slots_out, squares
 ):
     row, column = iota((ROWS, ROWS), 0), iota((ROWS, ROWS), 1)
     by_slot_order = pick(column == (row & (N_DP - 1)) * ROWS_DEV + (row >> 5))
@@ -122,6 +122,8 @@
         residual[...] = by_slot[HALF_ROWS:]
         spread_squares(by_slot[HALF_ROWS:], squares, 0)
 
+
+def cut_kernel(ids, table, keys, values, after, cut, spread):
     count = jnp.int32(0)
     for s in range(ROWS_DEV):
         leaves = table[DEST + s] != ids[REPLICA]
@@ -481,17 +483,19 @@
         load_kernel, "load", "vvv", shape(WIDTH + 16, PACKED), (w_query, rest, norm_gain)
     )
     other = swap(weights)
-    residual, to_slots, squares, cut = call(
+    residual, to_slots, squares = call(
         prepare_kernel,
         "prepare",
-        "ssvvvv",
-        (
-            shape(HALF_ROWS, WIDTH),
-            shape(ROWS, ROWS),
-            jax.ShapeDtypeStruct((2 * N_DP, HEAD), F32),
-            shape(N_DP, MOVES * PIECES, HEAD),
-        ),
-        (ids, table, new_index, hidden_in, keys, values),
+        "svv",
+        (shape(HALF_ROWS, WIDTH), shape(ROWS, ROWS), jax.ShapeDtypeStruct((2 * N_DP, HEAD), F32)),
+        (ids, new_index, hidden_in),
+    )
+    cut = call(
+        cut_kernel,
+        "cut",
+        "ssvva",
+        shape(N_DP, MOVES * PIECES, HEAD),
+        (ids, table, keys, values, squares),
         [pltpu.VMEM((MOVES * PIECES * N_DP, HEAD), F32)],
     )
     payload = call(

time: 136 us -> 135 us (level)
    pallas_call x11 -> x12, Pallas kernels: 12.4 us -> 12.9 us  [call(): pl.pallas_call(kernel, out_shape=out_shapes, in_specs=[spec_of[letter] fo...]
where the time goes in v9:
time: 135 us
  blocking collectives  85.2 us (63%)
  starting transfers between devices  23.2 us (17%)
  Pallas kernels  12.9 us (10%)
  waiting for transfers between devices  9.52 us (7%)
  other arithmetic  1.87 us (1%)
    all_to_all x5, blocking collectives, exchange(): return lax.all_to_all(value, axis, split_axis=0, concat_axis=0, tiled=True)  85.2 us
    ppermute x3, starting transfers between devices, swap(): return lax.ppermute(value, 'section', [(0, 1), (1, 0)])  18.7 us
    pallas_call x12, Pallas kernels, call(): pl.pallas_call(kernel, out_shape=out_shapes, in_specs=[spec_of[letter] fo...  12.9 us
    all_to_all x1, waiting for transfers between devices, exchange(): return lax.all_to_all(value, axis, split_axis=0, concat_axis=0, tiled=True)  8.37 us
    all_to_all x1, starting transfers between devices, exchange(): return lax.all_to_all(value, axis, split_axis=0, concat_axis=0, tiled=True)  4.43 us
  transfers between devices with their start and end apart: 4, of which 2 were waited for; matrix products, arithmetic and copies ran while one was open for 1% of the time, Pallas kernels for 2%

profile of v9, /device:TPU:1, one launch (start us, length us, event | category | flops | bytes accessed | tf_op | source)
XLA Modules:
  0.0 134.6 jit_solution(16255392931546359988)
XLA Ops:
  0.6 0.9 constant_dynamic-slice_fusion
  1.5 0.9 pad_add_fusion.rest
  2.5 0.1 load.1.weights
  2.6 8.9 %collective-permute-start = (bf16[272,1536]{1,0:T(8,128)(2,1)S(1)}, bf16[272,1536]{1,0:T(8,128)(2,1)S(1)}, u32[]{:S(2)}, u32[]{:S(2)}) collective-permute-start(bf16[272,1536]{1,0:T(8,128)(2,1)S(1)} %load.1.weights), channel_id=1, source_target_pairs={{0,1},{1,0},{2,3},{3,2},{4,5},{5,4},{6,7},{7,6},{8,9},{9,8},{10,11... | collective-permute-start | bytes 2506760 | tf_op jit(solution)/shard_map/ppermute | solution.py:427
  11.6 0.2 select_reduce_fusion.3.table.refs_1_
  11.8 0.1 slice.3
  11.9 0.1 pad_add_fusion.1.ids.refs_0_
  12.0 1.0 prepare.1
  13.0 0.8 cut.1
  13.8 0.1 compare_select_fusion
  13.9 0.1 fusion.2
  14.0 1.8 %first.1 = bf16[32,48,128]{2,1,0:T(8,128)(2,1)} custom-call(s32[2]{0:T(128)S(1)} %pad_add_fusion.1.ids.refs_0_, bf16[96,256]{1,0:T(8,128)(2,1)S(1)} %get-tuple-element.26.rows.residual, f32[64,128]{1,0:T(8,128)S(1)} %get-tuple-element.27.after.squares, bf16[32,16,128]{2,1,0:T(8,128)(2,1)S(1)} %cut.1, bf16[272,1536]{1,0:T(8,128)(2,1)S(1)} %load.1.weights, ...), custom_call_target="tpu_custom_call" | custom-call | tf_op jit(solution)/shard_map/first/pallas_call | solution.py:411
  15.8 4.4 %all-to-all-start = ((bf16[32,48,128]{2,1,0:T(8,128)(2,1)}), bf16[32,48,128]{2,1,0:T(8,128)(2,1)S(1)}, u32[]{:S(2)}, u32[]{:S(2)}) async-start(bf16[32,48,128]{2,1,0:T(8,128)(2,1)} %first.1), calls=%async_computation | async-start | bytes 786432 | tf_op jit(solution)/shard_map/all_to_all | solution.py:423
  20.3 2.2 %collective-permute-start.1 = (bf16[1024,256]{1,0:T(8,128)(2,1)S(1)}, bf16[1024,256]{1,0:T(8,128)(2,1)S(1)}, u32[]{:S(2)}, u32[]{:S(2)}) collective-permute-start(bf16[1024,256]{1,0:T(8,128)(2,1)S(1)} %bitcast.14), channel_id=1, source_target_pairs={{0,1},{1,0},{2,3},{3,2},{4,5},{5,4},{6,7},{7,6},{8,9},{9,8},{10,11... | collective-permute-start | bytes 1572872 | tf_op jit(solution)/shard_map/ppermute | solution.py:427
  22.5 0.3 select_reduce_fusion.1
  22.8 0.1 select_reduce_fusion.2
  22.9 1.1 collective-permute-done.1.refs_9_.refs_3_
  24.1 8.4 %all-to-all-done.refs_4_ = bf16[32,48,128]{2,1,0:T(8,128)(2,1)S(1)} async-done(((bf16[32,48,128]{2,1,0:T(8,128)(2,1)}), bf16[32,48,128]{2,1,0:T(8,128)(2,1)S(1)}, u32[]{:S(2)}, u32[]{:S(2)}) %all-to-all-start) | async-done | bytes 393248 | tf_op jit(solution)/shard_map/all_to_all | solution.py:423
  32.5 1.6 %attend.2 = (bf16[32,32,128]{2,1,0:T(8,128)(2,1)S(1)}, bf16[16,128]{1,0:T(8,128)(2,1)S(1)}, bf16[32,16,128]{2,1,0:T(8,128)(2,1)S(1)}) custom-call(s32[2]{0:T(128)S(1)} %pad_add_fusion.1.ids.refs_0_, s32[24]{0:T(128)S(1)} %select_reduce_fusion.3.table.refs_1_, f32[8,128]{1,0:T(8,128)S(1)} %get-tuple-element.50.refs_2_, ...), custom_call_target="tpu_custom_call" | custom-call | tf_op jit(solution)/shard_map/attend/pallas_call | solution.py:411
  34.0 16.8 %all_to_all.30.refs_1_.gathered_0.second_in = bf16[32,32,128]{2,1,0:T(8,128)(2,1)S(1)} all-to-all(bf16[32,32,128]{2,1,0:T(8,128)(2,1)S(1)} %get-tuple-element.31), channel_id=1, replica_groups=mesh['dp'=32,'tensor'=8,'section'=2] {'dp'}, dimensions={0} | all-to-all | bytes 524288 | tf_op jit(solution)/shard_map/all_to_all | solution.py:423
  50.9 1.0 output.2
  51.9 20.6 %all_to_all.31.received = bf16[8,96,256]{2,1,0:T(8,128)(2,1)S(1)} all-to-all(bf16[8,96,256]{2,1,0:T(8,128)(2,1)S(1)} %output.2), channel_id=1, replica_groups=mesh['dp'=32,'tensor'=8,'section'=2] {'tensor'}, dimensions={0} | all-to-all | bytes 786432 | tf_op jit(solution)/shard_map/all_to_all | solution.py:423
  72.5 1.2 second.1
  73.7 17.3 %all_to_all.32.refs_4_.third_in = bf16[32,40,128]{2,1,0:T(8,128)(2,1)S(1)} all-to-all(bf16[32,40,128]{2,1,0:T(8,128)(2,1)S(1)} %get-tuple-element.34), channel_id=1, replica_groups=mesh['dp'=32,'tensor'=8,'section'=2] {'dp'}, dimensions={0} | all-to-all | bytes 655360 | tf_op jit(solution)/shard_map/all_to_all | solution.py:423
  91.0 1.3 attend.3
  92.4 14.5 %all_to_all.33.refs_1_.gathered_1.fourth_in = bf16[32,32,128]{2,1,0:T(8,128)(2,1)S(1)} all-to-all(bf16[32,32,128]{2,1,0:T(8,128)(2,1)S(1)} %get-tuple-element.35), channel_id=1, replica_groups=mesh['dp'=32,'tensor'=8,'section'=2] {'dp'}, dimensions={0} | all-to-all | bytes 524288 | tf_op jit(solution)/shard_map/all_to_all | solution.py:423
  106.8 1.0 output.3
  107.9 16.0 %all_to_all.34.received = bf16[8,96,256]{2,1,0:T(8,128)(2,1)S(1)} all-to-all(bf16[8,96,256]{2,1,0:T(8,128)(2,1)S(1)} %output.3), channel_id=1, replica_groups=mesh['dp'=32,'tensor'=8,'section'=2] {'tensor'}, dimensions={0} | all-to-all | bytes 786432 | tf_op jit(solution)/shard_map/all_to_all | solution.py:423
  123.9 0.7 last.1
  124.6 7.6 %collective-permute-start.2 = (bf16[112,256]{1,0:T(8,128)(2,1)S(1)}, bf16[112,256]{1,0:T(8,128)(2,1)S(1)}, u32[]{:S(2)}, u32[]{:S(2)}) collective-permute-start(bf16[112,256]{1,0:T(8,128)(2,1)S(1)} %get-tuple-element.42), channel_id=1, source_target_pairs={{0,1},{1,0},{2,3},{3,2},{4,5},{5,4},{6,7},{7,6},{8,9},{9,8},{10,11... | collective-permute-start | bytes 172040 | tf_op jit(solution)/shard_map/ppermute | solution.py:427
  132.2 0.9 arrive.1
  133.1 1.5 %final.1 = (bf16[192,256]{1,0:T(8,128)(2,1)}, bf16[6,64,128]{2,1,0:T(8,128)(2,1)}, bf16[6,64,128]{2,1,0:T(8,128)(2,1)}) custom-call(s32[2]{0:T(128)S(1)} %pad_add_fusion.1.ids.refs_0_, s32[24]{0:T(128)S(1)} %select_reduce_fusion.3.table.refs_1_, bf16[192,192]{1,0:T(8,128)(2,1)S(1)} %get-tuple-element.25.to_slots, f32[192,256]{1,0:T(8,128)S(1)} %get-tuple-element.39.part, ...), custom_call_target="tpu_custom_call" | custom-call | tf_op jit(solution)/shard_map/final/pallas_call | solution.py:411
  (30 shorter events, 0.2 us)
Async XLA Ops:
  0.6 1.8 %copy-start.3 = (bf16[1,256,1024]{2,1,0:T(8,128)(2,1)S(1)}, bf16[1,256,1024]{2,1,0:T(8,128)(2,1)}, u32[]{:S(2)}) copy-start(bf16[1,256,1024]{2,1,0:T(8,128)(2,1)} %query.1) | copy-start | bytes 1572868
  1.5 0.9 copy-start.5
  2.5 9.1 %copy-start.6 = (s32[192]{0:T(256)S(1)}, s32[192]{0:T(256)}, u32[]{:S(2)}) copy-start(s32[192]{0:T(256)} %param.20) | copy-start | bytes 2308
  2.5 9.1 %copy-start.7 = (s32[192]{0:T(256)S(1)}, s32[192]{0:T(256)}, u32[]{:S(2)}) copy-start(s32[192]{0:T(256)} %param.21) | copy-start | bytes 2308
  2.5 9.1 %copy-start.8 = (s32[192]{0:T(256)S(1)}, s32[192]{0:T(256)}, u32[]{:S(2)}) copy-start(s32[192]{0:T(256)} %param.19) | copy-start | bytes 2308
  2.5 9.5 %copy-start.4 = (bf16[192,256]{1,0:T(8,128)(2,1)S(1)}, bf16[192,256]{1,0:T(8,128)(2,1)}, u32[]{:S(2)}) copy-start(bf16[192,256]{1,0:T(8,128)(2,1)} %hidden.1) | copy-start | bytes 294916
  2.5 10.4 %copy-start.2 = (bf16[1,6,64,128]{3,2,1,0:T(8,128)(2,1)S(1)}, bf16[1,6,64,128]{3,2,1,0:T(8,128)(2,1)}, u32[]{:S(2)}) copy-start(bf16[1,6,64,128]{3,2,1,0:T(8,128)(2,1)} %param.18) | copy-start | bytes 294916
  2.6 10.4 %copy-start.1 = (bf16[1,6,64,128]{3,2,1,0:T(8,128)(2,1)S(1)}, bf16[1,6,64,128]{3,2,1,0:T(8,128)(2,1)}, u32[]{:S(2)}) copy-start(bf16[1,6,64,128]{3,2,1,0:T(8,128)(2,1)} %param.17) | copy-start | bytes 294916
  2.6 11.4 %collective-permute-start = (bf16[272,1536]{1,0:T(8,128)(2,1)S(1)}, bf16[272,1536]{1,0:T(8,128)(2,1)S(1)}, u32[]{:S(2)}, u32[]{:S(2)}) collective-permute-start(bf16[272,1536]{1,0:T(8,128)(2,1)S(1)} %load.1.weights), channel_id=1, source_target_pairs={{0,1},{1,0},{2,3},{3,2},{4,5},{5,4},{6,7},{7,6},{8,9},{9,8},{10,11... | collective-permute-start | bytes 2506760 | tf_op jit(solution)/shard_map/ppermute | solution.py:427
  15.8 4.5 %copy-start = (bf16[1,1024,256]{2,1,0:T(8,128)(2,1)S(1)}, bf16[1,1024,256]{2,1,0:T(8,128)(2,1)}, u32[]{:S(2)}) copy-start(bf16[1,1024,256]{2,1,0:T(8,128)(2,1)} %param.16) | copy-start | bytes 1572868
  15.8 16.6 %all-to-all-start = ((bf16[32,48,128]{2,1,0:T(8,128)(2,1)}), bf16[32,48,128]{2,1,0:T(8,128)(2,1)S(1)}, u32[]{:S(2)}, u32[]{:S(2)}) async-start(bf16[32,48,128]{2,1,0:T(8,128)(2,1)} %first.1), calls=%async_computation | async-start | bytes 786432 | tf_op jit(solution)/shard_map/all_to_all | solution.py:423
  20.3 3.8 %collective-permute-start.1 = (bf16[1024,256]{1,0:T(8,128)(2,1)S(1)}, bf16[1024,256]{1,0:T(8,128)(2,1)S(1)}, u32[]{:S(2)}, u32[]{:S(2)}) collective-permute-start(bf16[1024,256]{1,0:T(8,128)(2,1)S(1)} %bitcast.14), channel_id=1, source_target_pairs={{0,1},{1,0},{2,3},{3,2},{4,5},{5,4},{6,7},{7,6},{8,9},{9,8},{10,11... | collective-permute-start | bytes 1572872 | tf_op jit(solution)/shard_map/ppermute | solution.py:427
  124.6 8.6 %collective-permute-start.2 = (bf16[112,256]{1,0:T(8,128)(2,1)S(1)}, bf16[112,256]{1,0:T(8,128)(2,1)S(1)}, u32[]{:S(2)}, u32[]{:S(2)}) collective-permute-start(bf16[112,256]{1,0:T(8,128)(2,1)S(1)} %get-tuple-element.42), channel_id=1, source_target_pairs={{0,1},{1,0},{2,3},{3,2},{4,5},{5,4},{6,7},{7,6},{8,9},{9,8},{10,11... | collective-permute-start | bytes 172040 | tf_op jit(solution)/shard_map/ppermute | solution.py:427
